TPU v7x, 256 devices: a whole 4x4x8 slice. The times are simulated.
256 devices in a mesh: tx: 8 (over z_hi, y), rx: 32 (over x, z_lo, core).
Axes of the slice: x: 4, y: 4, z: 8 (z_hi: 2, z_lo: 4; z = z_hi * 4 + z_lo), core: 2. Of those that a mesh axis runs over, the one named last changes fastest.
Arguments:
- slowness: bfloat16 [32], replicated, may hold values from -4 to 4
- tx_paths: bfloat16 [64, 32, 4096], P('tx', None, 'rx'), may hold values from 0 to 0.25
- rx_paths: bfloat16 [1024, 32, 4096], P('rx'), may hold values from 0 to 0.25
- traces: bfloat16 [64, 1024, 512], P('tx', 'rx'), may hold values from -6 to 6
- tap_start: int32 [64, 1024, 32], P('tx', 'rx'), may hold values from 0 to 504
- pixel_order: int32 [4096], replicated, may hold values from 0 to 4095, each once
- patch_cotangent: float32 [16], replicated, may hold values from 30 to 300
Outputs:
- slowness_grad: float32 [32], replicated
Inputs may be any that keep to these rules, and one draw needn't show every extreme that they name: `pixel_order`: each pixel rank occurs once, so every patch holds 256 pixels.
All inputs are finite; a program needn't handle non-finite values.
Results may differ from a plain program's by a relative error of at most 0.00085.
Values may be sent and summed in bfloat16 or wider, within the bound.
No kernel may reach another device: no remote copies, remote signals or barrier semaphores. Data moves between devices by JAX's collectives and lax.ppermute only.
A program may use at most 64 MiB of HBM per device.

v0:
```python
import jax
import jax.numpy as jnp
from jax import lax
from jax.sharding import PartitionSpec as P

W = 8
PB = 128
PP = 256


EPS = 1e-06


def patch_table(order, patch_count):
    patch_ids = order // PP
    return (patch_ids[None, :] == jnp.arange(patch_count, dtype=jnp.int32)[:, None]).astype(
        jnp.float32
    )


def loss_grad(beam, coherent, table, numer, denom, patch_cotangent, total_tx):
    hi = lax.Precision.HIGHEST
    scale_num = jnp.dot(patch_cotangent / (numer + EPS), table, precision=hi)
    scale_den = jnp.dot(patch_cotangent * total_tx / (denom + EPS), table, precision=hi)
    return -2.0 * (coherent * scale_num)[None, :] + 2.0 * beam * scale_den[None, :]


def select_windows(traces, tap_start):
    samples = jnp.arange(traces.shape[2], dtype=jnp.int32)
    offsets = jnp.arange(W, dtype=jnp.int32)

    def one_event(pair):
        trace_rows, start_rows = pair
        target = start_rows[:, :, None] + offsets
        select = (target[..., None] == samples).astype(jnp.bfloat16)
        return jnp.einsum("rbjk,rk->rbj", select, trace_rows, preferred_element_type=jnp.float32)

    return lax.map(one_event, (traces, tap_start))


def on_device(slowness, tx_paths, rx_paths, traces, tap_start, pixel_order, patch_cotangent):
    hi = lax.Precision.HIGHEST
    tx_count = tx_paths.shape[0]
    rx_count = rx_paths.shape[0]
    pixels = rx_paths.shape[2]
    blocks = pixels // PB
    patch_count = pixels // PP
    total_tx = tx_count * lax.axis_size("tx")
    slow_cells = slowness.astype(jnp.float32)
    tx_delay = lax.all_gather(
        jnp.einsum("tgp,g->tp", tx_paths.astype(jnp.float32), slow_cells, precision=hi),
        "rx",
        axis=1,
        tiled=True,
    )
    rx_delay = jnp.einsum("rgp,g->rp", rx_paths.astype(jnp.float32), slow_cells, precision=hi)
    window = select_windows(traces, tap_start)
    tau = (W - 1) / 2.0 + tx_delay[:, None, :] + rx_delay[None, :, :]
    tau = tau.reshape(tx_count, rx_count, blocks, PB)
    focused = jnp.zeros(tau.shape, jnp.float32)
    slope = jnp.zeros(tau.shape, jnp.float32)
    for position in range(W):
        offset = tau - position
        kernel = jnp.exp(-0.5 * offset * offset)
        sample = window[:, :, :, position][..., None]
        focused = focused + kernel * sample
        slope = slope - offset * kernel * sample
    beam_part = focused.sum(1).reshape(tx_count, pixels)
    beam = lax.psum(beam_part, "rx")
    coherent, power = lax.psum((beam.sum(0), (beam * beam).sum(0)), "tx")
    table = patch_table(pixel_order, patch_count)
    numer = jnp.dot(table, coherent * coherent, precision=hi)
    denom = total_tx * jnp.dot(table, power, precision=hi)
    beam_grad = loss_grad(beam, coherent, table, numer, denom, patch_cotangent, total_tx)
    delay_grad = beam_grad.reshape(tx_count, 1, blocks, PB) * slope
    tx_sum = delay_grad.sum(1).reshape(tx_count, pixels)
    rx_sum = delay_grad.sum(0).reshape(rx_count, pixels)
    grad_rx = jnp.einsum("rgp,rp->g", rx_paths.astype(jnp.float32), rx_sum, precision=hi)
    tx_share = lax.psum_scatter(tx_sum, "rx", scatter_dimension=1, tiled=True)
    grad_tx = jnp.einsum("tgp,tp->g", tx_paths.astype(jnp.float32), tx_share, precision=hi)
    return lax.psum(grad_tx + grad_rx, ("tx", "rx"))


def solution(mesh):
    in_specs = (
        P(),
        P("tx", None, "rx"),
        P("rx", None, None),
        P("tx", "rx", None),
        P("tx", "rx", None),
        P(),
        P(),
    )
    out_specs = P()
    return jax.shard_map(
        on_device, mesh=mesh, in_specs=in_specs, out_specs=out_specs, check_vma=False
    )
```

profile of v0, /device:TPU:1, one launch (start us, length us, event | category | flops | bytes accessed | tf_op | source)
XLA Modules:
  0.0 787.1 jit_solution(5893813319226655166)
XLA Ops:
  6.5 169.4 %while.11 = (s32[]{:T(128)}, f32[8,32,32,8]{2,3,1,0:T(8,128)S(1)}, s32[8,32,32]{2,1,0:T(8,128)}, bf16[8,32,512]{2,1,0:T(8,128)(2,1)}, s32[]{:T(128)}) while((s32[]{:T(128)}, f32[8,32,32,8]{2,3,1,0:T(8,128)S(1)}, s32[8,32,32]{2,1,0:T(8,128)}, bf16[8,32,512]{2,1,0:T(8,128)(2,1)}, s32[]{:T(128)}) %tuple.31), condition=%wide.region_1.2_spmd.clone, body=%wide.region_0.1_spmd.clone.sunk | while | flops 12591106 | bytes 536649 | solution.py:38
  7.5 0.8 dynamic-slice_bitcast_fusion.5
  8.3 19.1 %fusion.106 = f32[32,1,32,8]{3,1,2,0:T(1,128)S(1)} fusion(s32[32,32,8]{2,1,0:T(8,128)S(1)} %iota_add_fusion.2, bf16[32,512,1,1]{1,0,2,3:T(8,128)(2,1)S(1)} %dynamic-slice_bitcast_fusion.5), kind=kOutput, calls=%fused_computation.3.clone.1 | convolution fusion | flops 12582912 | bytes 98304 | tf_op jit(solution)/shard_map/while/body/eval_jaxpr/rbjk,rk->rbj/dot_general | solution.py:36
  29.5 19.1 %fusion.106 = f32[32,1,32,8]{3,1,2,0:T(1,128)S(1)} fusion(s32[32,32,8]{2,1,0:T(8,128)S(1)} %iota_add_fusion.2, bf16[32,512,1,1]{1,0,2,3:T(8,128)(2,1)S(1)} %dynamic-slice_bitcast_fusion.5), kind=kOutput, calls=%fused_computation.3.clone.1 | convolution fusion | flops 12582912 | bytes 98304 | tf_op jit(solution)/shard_map/while/body/eval_jaxpr/rbjk,rk->rbj/dot_general | solution.py:36
  50.6 19.1 %fusion.106 = f32[32,1,32,8]{3,1,2,0:T(1,128)S(1)} fusion(s32[32,32,8]{2,1,0:T(8,128)S(1)} %iota_add_fusion.2, bf16[32,512,1,1]{1,0,2,3:T(8,128)(2,1)S(1)} %dynamic-slice_bitcast_fusion.5), kind=kOutput, calls=%fused_computation.3.clone.1 | convolution fusion | flops 12582912 | bytes 98304 | tf_op jit(solution)/shard_map/while/body/eval_jaxpr/rbjk,rk->rbj/dot_general | solution.py:36
  71.8 19.1 %fusion.106 = f32[32,1,32,8]{3,1,2,0:T(1,128)S(1)} fusion(s32[32,32,8]{2,1,0:T(8,128)S(1)} %iota_add_fusion.2, bf16[32,512,1,1]{1,0,2,3:T(8,128)(2,1)S(1)} %dynamic-slice_bitcast_fusion.5), kind=kOutput, calls=%fused_computation.3.clone.1 | convolution fusion | flops 12582912 | bytes 98304 | tf_op jit(solution)/shard_map/while/body/eval_jaxpr/rbjk,rk->rbj/dot_general | solution.py:36
  92.2 0.8 dynamic-slice_bitcast_fusion.5
  93.0 19.1 %fusion.106 = f32[32,1,32,8]{3,1,2,0:T(1,128)S(1)} fusion(s32[32,32,8]{2,1,0:T(8,128)S(1)} %iota_add_fusion.2, bf16[32,512,1,1]{1,0,2,3:T(8,128)(2,1)S(1)} %dynamic-slice_bitcast_fusion.5), kind=kOutput, calls=%fused_computation.3.clone.1 | convolution fusion | flops 12582912 | bytes 98304 | tf_op jit(solution)/shard_map/while/body/eval_jaxpr/rbjk,rk->rbj/dot_general | solution.py:36
  114.2 19.1 %fusion.106 = f32[32,1,32,8]{3,1,2,0:T(1,128)S(1)} fusion(s32[32,32,8]{2,1,0:T(8,128)S(1)} %iota_add_fusion.2, bf16[32,512,1,1]{1,0,2,3:T(8,128)(2,1)S(1)} %dynamic-slice_bitcast_fusion.5), kind=kOutput, calls=%fused_computation.3.clone.1 | convolution fusion | flops 12582912 | bytes 98304 | tf_op jit(solution)/shard_map/while/body/eval_jaxpr/rbjk,rk->rbj/dot_general | solution.py:36
  135.3 19.1 %fusion.106 = f32[32,1,32,8]{3,1,2,0:T(1,128)S(1)} fusion(s32[32,32,8]{2,1,0:T(8,128)S(1)} %iota_add_fusion.2, bf16[32,512,1,1]{1,0,2,3:T(8,128)(2,1)S(1)} %dynamic-slice_bitcast_fusion.5), kind=kOutput, calls=%fused_computation.3.clone.1 | convolution fusion | flops 12582912 | bytes 98304 | tf_op jit(solution)/shard_map/while/body/eval_jaxpr/rbjk,rk->rbj/dot_general | solution.py:36
  156.5 19.1 %fusion.106 = f32[32,1,32,8]{3,1,2,0:T(1,128)S(1)} fusion(s32[32,32,8]{2,1,0:T(8,128)S(1)} %iota_add_fusion.2, bf16[32,512,1,1]{1,0,2,3:T(8,128)(2,1)S(1)} %dynamic-slice_bitcast_fusion.5), kind=kOutput, calls=%fused_computation.3.clone.1 | convolution fusion | flops 12582912 | bytes 98304 | tf_op jit(solution)/shard_map/while/body/eval_jaxpr/rbjk,rk->rbj/dot_general | solution.py:36
  176.0 1.0 fusion.92
  177.0 5.1 fusion.87
  182.7 46.2 %all_gather.3 = f32[8,4096]{1,0:T(8,128)S(1)} all-gather(f32[8,128]{1,0:T(8,128)S(1)} %bitcast.125), channel_id=1, replica_groups=mesh['tx'=8,'rx'=32] {'rx'}, dimensions={1}, use_global_device_ids=true | all-gather | bytes 135168 | tf_op jit(solution)/shard_map/all_gather | solution.py:50
  228.9 9.3 %fusion.66 = f32[8,32,128]{2,1,0:T(8,128)S(1)} fusion(f32[8,32,32]{2,1,0:T(8,128)S(1)} %bitcast.116, f32[8,32,32]{2,1,0:T(8,128)S(1)} %bitcast.104, f32[8,32,32]{2,1,0:T(8,128)S(1)} %bitcast.106, f32[8,32,32]{2,1,0:T(8,128)S(1)} %bitcast.108, f32[8,32,32]{2,1,0:T(8,128)S(1)} %bitcast.110, f32[8,32,32]{2,1,0:T(8,128)S(1)} %bitcast.112, ...), kind=kLoop, calls=%fused_computation.79 | loop fusion | flops 41910272 | bytes 1048576 | tf_op jit(solution)/shard_map/reduce_sum | solution.py:68
  239.1 249.4 %all-reduce.3.cloned.1.call-done = f32[8,4096]{1,0:T(8,128)} async-done(((f32[8,4096]{1,0:T(8,128)}), f32[8,4096]{1,0:T(8,128)}) %all-reduce.3.cloned.1.call-update) | async-done | bytes 131088 | tf_op jit(solution)/shard_map/psum | solution.py:69
  488.5 1.0 fusion.91
  489.5 45.0 %all-reduce = (f32[4096]{0:T(1024)S(1)}, f32[4096]{0:T(1024)S(1)}) all-reduce(f32[4096]{0:T(1024)S(1)} %get-tuple-element.52, f32[4096]{0:T(1024)S(1)} %get-tuple-element.51), channel_id=1, replica_groups=mesh['tx'=8,'rx'=32] {'tx'}, use_global_device_ids=true, to_apply=%region_7.8 | all-reduce | flops 8192 | bytes 65536 | tf_op jit(solution)/shard_map/psum | solution.py:70
  535.5 0.9 add_bitcast_fusion
  536.5 12.3 %fusion.69 = (f32[32,32,128]{2,1,0:T(8,128)S(1)}, f32[8,32,128]{2,1,0:T(8,128)S(1)}) fusion(f32[8,32,32]{2,1,0:T(8,128)S(1)} %bitcast.117, f32[8,32,32]{2,1,0:T(8,128)S(1)} %bitcast.105, f32[8,32,32]{2,1,0:T(8,128)S(1)} %bitcast.107, f32[8,32,32]{2,1,0:T(8,128)S(1)} %bitcast.109, f32[8,32,32]{2,1,0:T(8,128)S(1)} %bitcast.111, f32[8,32,32]{2,1,0:T(8,128)S(1)} %bitcast.113, ...), kind=kLoop, calls=%fused_computation.82 | loop fusion | flops 53313536 | bytes 1703936 | tf_op jit(solution)/shard_map/reduce_sum | solution.py:77
  549.6 139.7 %reduce-scatter.2.cloned.1.call-done = f32[8,128]{1,0:T(8,128)} async-done(((f32[8,4096]{1,0:T(8,128)}), f32[8,128]{1,0:T(8,128)}) %reduce-scatter.2.cloned.1.call-update) | async-done | bytes 4112 | tf_op jit(solution)/shard_map/reduce_scatter | solution.py:79
  689.3 0.8 convolution_bitcast_fusion.1
  690.1 9.2 %fusion.71 = f32[32]{0:T(128)S(1)} fusion(f32[32]{0:T(128)S(1)} %convolution_bitcast_fusion.1, f32[32,4096,1]{1,2,0:T(1,128)S(1)} %bitcast.128, bf16[32,32,4096]{2,1,0:T(8,128)(2,1)} %param.11), kind=kOutput, calls=%fused_computation.85 | convolution fusion | flops 50331680 | bytes 8913152 | tf_op jit(solution)/shard_map/rgp,rp->g/dot_general | solution.py:78
  699.2 81.0 %psum.31 = f32[32]{0:T(128)} all-reduce(f32[32]{0:T(128)S(1)} %fusion.71), channel_id=1, replica_groups=mesh['tx'=8,'rx'=32] {'tx','rx'}, use_global_device_ids=true, to_apply=%region_11.12 | all-reduce | flops 32 | bytes 256 | tf_op jit(solution)/shard_map/psum | solution.py:81
  (66 shorter events, 17.8 us)
Async XLA Ops:
  6.5 176.0 %copy-start = (bf16[8,32,128]{2,1,0:T(8,128)(2,1)S(1)}, bf16[8,32,128]{2,1,0:T(8,128)(2,1)}, u32[]{:S(2)}) copy-start(bf16[8,32,128]{2,1,0:T(8,128)(2,1)} %param.10) | copy-start | bytes 196612
  6.5 482.0 %all-reduce.3.cloned.1.call-start = ((), (), s32[]{:S(2)}) async-start(), calls=%async_computation.1 | async-start | bytes 262144 | tf_op jit(solution)/shard_map/psum | solution.py:69
  6.5 170.5 %copy-start.2 = (bf16[32]{0:T(256)(128)(2,1)S(1)}, bf16[32]{0:T(256)(128)(2,1)}, u32[]{:S(2)}) copy-start(bf16[32]{0:T(256)(128)(2,1)} %param.9) | copy-start | bytes 196
  228.9 10.2 %copy-start.1 = (s32[4096]{0:T(1024)S(1)}, s32[4096]{0:T(1024)}, u32[]{:S(2)}) copy-start(s32[4096]{0:T(1024)} %param.14) | copy-start | bytes 49156
  228.9 305.6 %copy-start.3 = (f32[16]{0:T(128)S(1)}, f32[16]{0:T(128)}, u32[]{:S(2)}) copy-start(f32[16]{0:T(128)} %param.15) | copy-start | bytes 196
  239.0 450.2 %reduce-scatter.2.cloned.1.call-start = ((), (), s32[]{:S(2)}) async-start(), calls=%async_computation.2 | async-start | bytes 135168 | tf_op jit(solution)/shard_map/reduce_scatter | solution.py:79
Sparse Core Ops, SparseCore 0:
  239.2 249.3 all-reduce.2
  549.7 139.5 reduce-scatter.1
where the time goes:
time: 788 us; the launch traced here: 787 us
  waiting for transfers between devices  389 us (49%)
  blocking collectives  172 us (22%)
  matrix products  169 us (21%)
  other arithmetic  25.2 us (3%)
  local copies, waits for them, and re-layouts  17.5 us (2%)
  between operations  13.6 us (2%)
    psum x1, waiting for transfers between devices, on_device(): beam = lax.psum(beam_part, 'rx')  249 us
    dot_general x8, matrix products, one_event(): jnp.einsum('rbjk,rk->rbj', select, trace_rows, preferred_element_type=jnp...  153 us
    reduce_scatter x1, waiting for transfers between devices, on_device(): tx_share = lax.psum_scatter(tx_sum, 'rx', scatter_dimension=1, tiled=True)  140 us
    psum x1, blocking collectives, on_device(): return lax.psum(grad_tx + grad_rx, ('tx', 'rx'))  81 us
    all_gather x1, blocking collectives, on_device(): lax.all_gather(jnp.einsum('tgp,g->tp', tx_paths.astype(jnp.float32), slow...  46.2 us
    psum x1, blocking collectives, on_device(): coherent, power = lax.psum((beam.sum(0), (beam * beam).sum(0)), 'tx')  45 us
  transfers between devices with their start and end apart: 2, of which 2 were waited for; matrix products, arithmetic and copies ran while one was open for 0% of the time, Pallas kernels for 0%

commit v1 on v0

v1 whole, which is shorter than its diff:
```python
import math

import jax
import jax.numpy as jnp
from jax import lax
from jax.experimental import pallas as pl
from jax.experimental.pallas import tpu as pltpu
from jax.sharding import PartitionSpec as P

W = 8
PB = 128
PP = 256
EPS = 1e-06
LN2 = math.log(2.0)
HALF_LOG2E = 0.5 / LN2
F32 = jnp.float32
VMEM_LIMIT = 48 * 1024 * 1024


def block_diagonal(s_row, rows, cells):
    wide = jnp.concatenate([s_row] * rows, axis=1)
    shape = (rows, rows * cells)
    owner = lax.broadcasted_iota(jnp.int32, shape, 1) // cells
    mine = owner == lax.broadcasted_iota(jnp.int32, shape, 0)
    return jnp.where(mine, jnp.broadcast_to(wide, shape), 0.0).astype(jnp.bfloat16)


def tx_delay_kernel(s_ref, path_ref, out_ref):
    rows, cells, width = path_ref.shape
    left = block_diagonal(s_ref[...].astype(F32), rows, cells)
    delay = jnp.dot(
        left, path_ref[...].reshape(rows * cells, width), preferred_element_type=F32
    )
    out_ref[...] = jnp.broadcast_to((delay * HALF_LOG2E)[None], out_ref.shape)


def prepare_kernel(s_ref, path_ref, trace_ref, start_ref, delay_ref, win_ref):
    rows, cells, width = path_ref.shape
    left = block_diagonal(s_ref[...].astype(F32), 8, cells)
    for first in range(0, rows, 8):
        paths = path_ref[pl.ds(first, 8)].reshape(8 * cells, width)
        delay = jnp.dot(left, paths, preferred_element_type=F32)
        delay_ref[pl.ds(first, 8), :] = delay * HALF_LOG2E
    samples = trace_ref[0].astype(F32)
    starts = start_ref[0]
    blocks = starts.shape[1]
    per = 128 // blocks
    starts = jnp.concatenate([starts] * per, axis=1)
    lane = lax.broadcasted_iota(jnp.int32, starts.shape, 1)
    for half in range(W // per):
        tap = lane // blocks + half * per
        index = starts + tap
        low = index & 127
        high = index >> 7
        picked = None
        for part in range(samples.shape[1] // 128):
            source = samples[:, part * 128 : (part + 1) * 128]
            got = jnp.take_along_axis(source, low, axis=1, mode="promise_in_bounds")
            picked = got if picked is None else jnp.where(high == part, got, picked)
        off = tap.astype(F32) - (W - 1) / 2.0
        win_ref[0, :, half * 128 : (half + 1) * 128] = picked * jnp.exp(-0.5 * off * off)


def focus_kernel(tx_ref, rx_ref, win_ref, slope_ref, sum_ref):
    t = pl.program_id(0)
    blocks = tx_ref.shape[0]
    rows = rx_ref.shape[0]
    per = 128 // blocks
    limit = 9.25 / LN2

    def point(k, first):
        def tap(j):
            lane = (j // per) * 128 + (j % per) * blocks + k
            return jnp.broadcast_to(win_ref[0, first : first + 8, lane : lane + 1], (8, PB))

        h = tx_ref[k, pl.ds(t, 1), :] + rx_ref[first : first + 8, k * PB : (k + 1) * PB]
        h = jnp.minimum(jnp.maximum(h, -limit), limit)
        m = h * (-LN2)
        s = jnp.exp2(h)
        si = jnp.exp2(-h)
        gauss = jnp.exp2(m * h)
        u = s * s
        v = si * si

        def horner(z, c3, c2, c1, c0):
            p1 = c3 * z + c2
            p2 = p1 * z + c1
            d2 = c3 * z + p1
            return p2 * z + c0, d2 * z + p2

        up, dup = horner(u, tap(7), tap(6), tap(5), tap(4))
        down, ddown = horner(v, tap(0), tap(1), tap(2), tap(3))
        x = s * up
        y = si * down
        both = x + y
        change = (x - y) * 0.5 + ((s * u) * dup - (si * v) * ddown)
        focused = gauss * (gauss * both)
        slope = gauss * (gauss * (change + (m + m) * both))
        return focused, slope

    for k in range(blocks):
        total_f = None
        total_s = None
        for first in range(0, rows, 8):
            focused, slope = point(k, first)
            slope_ref[0, first : first + 8, k * PB : (k + 1) * PB] = slope
            total_f = focused if total_f is None else total_f + focused
            total_s = slope if total_s is None else total_s + slope
        count = pl.num_programs(0)
        sum_ref[k, pl.ds(t, 1), :] = jnp.sum(total_f, axis=0, keepdims=True)
        sum_ref[k, pl.ds(count + t, 1), :] = jnp.sum(total_s, axis=0, keepdims=True)


def gather_sum_kernel(part_ref, red_ref, rep_ref):
    total = part_ref[0]
    for i in range(1, part_ref.shape[0]):
        total = total + part_ref[i]
    red_ref[...] = total
    beam = total[0 : total.shape[0] // 2]
    coherent = jnp.sum(beam, axis=0, keepdims=True)
    power = jnp.sum(beam * beam, axis=0, keepdims=True)
    pair = jnp.concatenate([coherent, power], axis=0)
    rep_ref[...] = jnp.broadcast_to(pair[None], rep_ref.shape)


def spread_kernel(pair_ref, red_ref, out_ref):
    pair = pair_ref[0]
    for i in range(1, pair_ref.shape[0]):
        pair = pair + pair_ref[i]
    count = red_ref.shape[0] // 2
    out_ref[:, 0:count, :] = jnp.broadcast_to(
        red_ref[0:count, :][None], (out_ref.shape[0], count, PB)
    )
    out_ref[:, count : count + 2, :] = jnp.broadcast_to(
        pair[None], (out_ref.shape[0], 2, PB)
    )


def gradient_kernel(
    total_tx,
    me_ref,
    cot_ref,
    all_ref,
    ids_ref,
    red_ref,
    tx_path_ref,
    slope_ref,
    path_ref,
    out_ref,
    bg_ref,
    acc_ref,
):
    step = pl.program_id(0)
    count, rows, width = slope_ref.shape
    blocks = all_ref.shape[0]
    cells = path_ref.shape[1]
    patches = cot_ref.shape[0]

    @pl.when(step == 0)
    def _():
        ids = ids_ref[...] // PP
        coherent = all_ref[:, count, :]
        power = all_ref[:, count + 1, :]
        square = coherent * coherent
        scale_n = jnp.zeros_like(square)
        scale_d = jnp.zeros_like(square)
        for q in range(patches):
            inside = ids == q
            numer = jnp.sum(jnp.where(inside, square, 0.0), keepdims=True)
            denom = total_tx * jnp.sum(jnp.where(inside, power, 0.0), keepdims=True)
            cot = jnp.full((1, 1), cot_ref[q], F32)
            value_n = -2.0 * (cot / (numer + EPS))
            value_d = 2.0 * (cot * total_tx / (denom + EPS))
            scale_n = jnp.where(inside, value_n, scale_n)
            scale_d = jnp.where(inside, value_d, scale_d)
        common = coherent * scale_n
        for k in range(blocks):
            bg_ref[k] = common[k : k + 1, :] + all_ref[k, 0:count, :] * scale_d[k : k + 1, :]
        own = bg_ref[me_ref[0]] * red_ref[count : 2 * count, :]
        acc = jnp.zeros((cells, PB), F32)
        for t in range(count):
            acc = acc + tx_path_ref[t].astype(F32) * own[t : t + 1, :]
        acc_ref[...] = acc

    acc = [acc_ref[...], jnp.zeros((cells, PB), F32)]
    for kk in range(width // PB):
        lanes = slice(kk * PB, (kk + 1) * PB)
        bg = bg_ref[step * (width // PB) + kk]
        for first in range(0, rows, 8):
            grad = None
            for t in range(count):
                term = bg[t : t + 1, :] * slope_ref[t, first : first + 8, lanes]
                grad = term if grad is None else grad + term
            for r in range(8):
                paths = path_ref[first + r, :, lanes].astype(F32)
                acc[r % 2] = acc[r % 2] + paths * grad[r : r + 1, :]
    acc = acc[0] + acc[1]
    acc_ref[...] = acc

    @pl.when(step == pl.num_programs(0) - 1)
    def _():
        ones = jnp.ones((8, PB), F32)
        row = lax.dot_general(
            ones,
            acc,
            (((1,), (1,)), ((), ())),
            precision=lax.Precision.HIGHEST,
            preferred_element_type=F32,
        )
        row = jnp.concatenate([row] * (PB // cells), axis=1)
        out_ref[...] = jnp.broadcast_to(row[0:1, :], out_ref.shape)


def params(**more):
    return pltpu.CompilerParams(vmem_limit_bytes=VMEM_LIMIT, **more)


def whole(shape):
    return pl.BlockSpec(shape, lambda *_: (0,) * len(shape))


def on_device(slowness, tx_paths, rx_paths, traces, tap_start, pixel_order, patch_cotangent):
    tx_count, cells, own_pixels = tx_paths.shape
    rx_count, _, pixels = rx_paths.shape
    blocks = pixels // PB
    samples = traces.shape[2]
    tx_size = lax.axis_size("tx")
    rx_size = lax.axis_size("rx")
    total_tx = tx_count * tx_size
    s_row = slowness.reshape(1, cells)
    chunk = pixels // tx_count

    delay = pl.pallas_call(
        tx_delay_kernel,
        out_shape=jax.ShapeDtypeStruct((rx_size, tx_count, own_pixels), F32),
        compiler_params=params(),
        name="tx_delay",
    )(s_row, tx_paths)
    rx_delay, window = pl.pallas_call(
        prepare_kernel,
        grid=(tx_count,),
        in_specs=[
            whole((1, cells)),
            pl.BlockSpec((rx_count, cells, chunk), lambda i: (0, 0, i)),
            pl.BlockSpec((1, rx_count, samples), lambda i: (i, 0, 0)),
            pl.BlockSpec((1, rx_count, blocks), lambda i: (i, 0, 0)),
        ],
        out_specs=[
            pl.BlockSpec((rx_count, chunk), lambda i: (0, i)),
            pl.BlockSpec((1, rx_count, W * blocks), lambda i: (i, 0, 0)),
        ],
        out_shape=[
            jax.ShapeDtypeStruct((rx_count, pixels), F32),
            jax.ShapeDtypeStruct((tx_count, rx_count, W * blocks), F32),
        ],
        compiler_params=params(),
        name="prepare",
    )(s_row, rx_paths, traces, tap_start)
    tx_delay = lax.all_to_all(delay, "rx", 0, 0)
    slope, part = pl.pallas_call(
        focus_kernel,
        grid=(tx_count,),
        in_specs=[
            whole((blocks, tx_count, PB)),
            whole((rx_count, pixels)),
            pl.BlockSpec((1, rx_count, W * blocks), lambda i: (i, 0, 0)),
        ],
        out_specs=[
            pl.BlockSpec((1, rx_count, pixels), lambda i: (i, 0, 0)),
            whole((blocks, 2 * tx_count, PB)),
        ],
        out_shape=[
            jax.ShapeDtypeStruct((tx_count, rx_count, pixels), F32),
            jax.ShapeDtypeStruct((blocks, 2 * tx_count, PB), F32),
        ],
        compiler_params=params(),
        name="focus",
    )(tx_delay, rx_delay, window)
    part = lax.all_to_all(part, "rx", 0, 0)
    red, pair = pl.pallas_call(
        gather_sum_kernel,
        out_shape=[
            jax.ShapeDtypeStruct((2 * tx_count, PB), F32),
            jax.ShapeDtypeStruct((tx_size, 2, PB), F32),
        ],
        compiler_params=params(),
        name="sum_receivers",
    )(part)
    pair = lax.all_to_all(pair, "tx", 0, 0)
    spread = pl.pallas_call(
        spread_kernel,
        out_shape=jax.ShapeDtypeStruct((rx_size, tx_count + 2, PB), F32),
        compiler_params=params(),
        name="sum_transmits",
    )(pair, red)
    every = lax.all_to_all(spread, "rx", 0, 0)
    me = lax.axis_index("rx").astype(jnp.int32).reshape(1)
    smem = pl.BlockSpec(memory_space=pltpu.SMEM)
    share = pl.pallas_call(
        lambda *refs: gradient_kernel(total_tx, *refs),
        grid=(tx_count,),
        in_specs=[
            smem,
            smem,
            whole((blocks, tx_count + 2, PB)),
            whole((blocks, PB)),
            whole((2 * tx_count, PB)),
            whole((tx_count, cells, own_pixels)),
            pl.BlockSpec((tx_count, rx_count, chunk), lambda i: (0, 0, i)),
            pl.BlockSpec((rx_count, cells, chunk), lambda i: (0, 0, i)),
        ],
        out_specs=whole((tx_size * rx_size, PB)),
        out_shape=jax.ShapeDtypeStruct((tx_size * rx_size, PB), F32),
        scratch_shapes=[
            pltpu.VMEM((blocks, tx_count, PB), F32),
            pltpu.VMEM((cells, PB), F32),
        ],
        compiler_params=params(),
        name="gradient",
    )(
        me,
        patch_cotangent,
        every,
        pixel_order.reshape(blocks, PB),
        red,
        tx_paths,
        slope,
        rx_paths,
    )
    share = lax.all_to_all(share, ("tx", "rx"), 0, 0, tiled=True)
    return share.sum(0)[:cells]


def solution(mesh):
    in_specs = (
        P(),
        P("tx", None, "rx"),
        P("rx", None, None),
        P("tx", "rx", None),
        P("tx", "rx", None),
        P(),
        P(),
    )
    out_specs = P()
    return jax.shard_map(
        on_device, mesh=mesh, in_specs=in_specs, out_specs=out_specs, check_vma=False
    )
```

time: 788 us -> 119 us (0.15)
  waiting for transfers between devices: 389 us -> 11.4 us
  matrix products: 169 us -> 0 us
  blocking collectives: 172 us -> 53.3 us
  Pallas kernels: 0 us -> 29.4 us
  other arithmetic: 25.2 us -> 0.79 us
  starting transfers between devices: 0.04 us -> 15 us
  between operations: 13.6 us -> 0.08 us
  local copies, waits for them, and re-layouts: 17.5 us -> 8.14 us
    psum x1 -> x0, waiting for transfers between devices: 249 us -> none  [on_device(): beam = lax.psum(beam_part, 'rx')]
    dot_general x16 -> x0, matrix products: 169 us -> none  [the longest x8 153 us: one_event(): jnp.einsum('rbjk,rk->rbj', select, trace_rows, preferred_element_type=jnp...]
    reduce_scatter x1 -> x0, waiting for transfers between devices: 140 us -> none  [on_device(): tx_share = lax.psum_scatter(tx_sum, 'rx', scatter_dimension=1, tiled=True)]
    psum x2 -> x0, blocking collectives: 126 us -> none  [the longest x1 81 us: on_device(): return lax.psum(grad_tx + grad_rx, ('tx', 'rx'))]
    all_to_all x0 -> x3, blocking collectives: none -> 53.3 us  [the longest x1 18.8 us: on_device(): part = lax.all_to_all(part, 'rx', 0, 0)]
    all_gather x1 -> x0, blocking collectives: 46.2 us -> none  [on_device(): lax.all_gather(jnp.einsum('tgp,g->tp', tx_paths.astype(jnp.float32), slow...]
    pallas_call x0 -> x6, Pallas kernels: none -> 29.4 us  [the longest x1 13.7 us: on_device(): pl.pallas_call(focus_kernel, grid=(tx_count,), in_specs=[whole((blocks, t...]
    reduce_sum x3 -> x1, other arithmetic: 22.6 us -> 0.79 us  [on_device(): return share.sum(0)[:cells]]
  transfers between devices with their start and end apart: 2 -> 2, of which waited for: 2 -> 1; matrix products, arithmetic and copies ran while one was open for 0% -> 0% of each run, Pallas kernels for 0% -> 6%
where the time goes in v1:
time: 119 us; the launch traced here: 118 us
  blocking collectives  53.3 us (45%)
  Pallas kernels  29.4 us (25%)
  starting transfers between devices  15 us (13%)
  waiting for transfers between devices  11.4 us (10%)
  local copies, waits for them, and re-layouts  8.14 us (7%)
    all_to_all x1, blocking collectives, on_device(): part = lax.all_to_all(part, 'rx', 0, 0)  18.8 us
    all_to_all x1, blocking collectives, on_device(): share = lax.all_to_all(share, ('tx', 'rx'), 0, 0, tiled=True)  17.7 us
    all_to_all x1, blocking collectives, on_device(): pair = lax.all_to_all(pair, 'tx', 0, 0)  16.9 us
    pallas_call x1, Pallas kernels, on_device(): pl.pallas_call(focus_kernel, grid=(tx_count,), in_specs=[whole((blocks, t...  13.7 us
    all_to_all x1, waiting for transfers between devices, on_device(): every = lax.all_to_all(spread, 'rx', 0, 0)  11.4 us
    all_to_all x1, starting transfers between devices, on_device(): tx_delay = lax.all_to_all(delay, 'rx', 0, 0)  10 us
    unnamed x20, local copies, waits for them, and re-layouts  8.14 us
    pallas_call x1, Pallas kernels, on_device(): pl.pallas_call(lambda *refs: gradient_kernel(total_tx, *refs), grid=(tx_c...  7.43 us
  transfers between devices with their start and end apart: 2, of which 1 were waited for; matrix products, arithmetic and copies ran while one was open for 0% of the time, Pallas kernels for 6%

profile of v1, /device:TPU:1, one launch (start us, length us, event | category | flops | bytes accessed | tf_op | source)
XLA Modules:
  0.0 118.1 jit_solution(18041671322724086861)
XLA Ops:
  0.0 0.9 copy-done.2
  0.9 0.7 copy-done.7
  1.5 0.8 tx_delay.1
  2.4 10.0 %all-to-all-start = ((f32[32,8,128]{2,1,0:T(8,128)}), f32[32,8,128]{2,1,0:T(8,128)S(1)}, u32[]{:S(2)}, u32[]{:S(2)}) async-start(f32[32,8,128]{2,1,0:T(8,128)} %tx_delay.1), calls=%async_computation | async-start | bytes 262144 | tf_op jit(solution)/shard_map/all_to_all | solution.py:259
  12.4 0.0 copy-start.4
  12.4 0.9 copy-done.4
  13.3 0.9 copy-done.5
  14.3 0.7 copy-done.8
  14.9 6.7 %prepare.1 = (f32[32,4096]{1,0:T(8,128)S(1)}, f32[8,32,256]{2,1,0:T(8,128)S(1)}) custom-call(bf16[1,32]{1,0:T(2,128)(2,1)S(1)} %bitcast.10, bf16[32,32,4096]{2,1,0:T(8,128)(2,1)} %refs_7_.1, bf16[8,32,512]{2,1,0:T(8,128)(2,1)S(1)} %copy-done.4, s32[8,32,32]{2,1,0:T(8,128)S(1)} %copy-done.5), custom_call_target="tpu_custom_call" | custom-call | tf_op jit(solution)/shard_map/prepare/pallas_call | solution.py:239
  21.6 0.0 all-to-all-done.tx_ref
  21.6 13.7 %focus.1 = (f32[8,32,4096]{2,1,0:T(8,128)S(1)}, f32[32,16,128]{2,1,0:T(8,128)S(1)}) custom-call(f32[32,8,128]{2,1,0:T(8,128)S(1)} %all-to-all-done.tx_ref, f32[32,4096]{1,0:T(8,128)S(1)} %get-tuple-element.11.rx_ref, f32[8,32,256]{2,1,0:T(8,128)S(1)} %get-tuple-element.12.win_ref), custom_call_target="tpu_custom_call" | custom-call | tf_op jit(solution)/shard_map/focus/pallas_call | solution.py:260
  35.3 0.0 copy-start
  35.3 1.9 %copy-done = f32[8,32,4096]{2,1,0:T(8,128)} copy-done((f32[8,32,4096]{2,1,0:T(8,128)}, f32[8,32,4096]{2,1,0:T(8,128)S(1)}, u32[]{:S(2)}) %copy-start) | copy-done | bytes 4194328
  37.2 18.8 %all_to_all.29.part_ref = f32[32,16,128]{2,1,0:T(8,128)S(1)} all-to-all(f32[32,16,128]{2,1,0:T(8,128)S(1)} %get-tuple-element.13), channel_id=1, replica_groups=mesh['tx'=8,'rx'=32] {'rx'}, dimensions={0} | all-to-all | bytes 524288 | tf_op jit(solution)/shard_map/all_to_all | solution.py:279
  56.0 16.9 %all_to_all.30.pair_ref = f32[8,2,128]{2,1,0:T(2,128)S(1)} all-to-all(f32[8,2,128]{2,1,0:T(2,128)S(1)} %get-tuple-element.14), channel_id=1, replica_groups=mesh['tx'=8,'rx'=32] {'tx'}, dimensions={0} | all-to-all | bytes 16384 | tf_op jit(solution)/shard_map/all_to_all | solution.py:289
  72.9 0.7 sum_transmits.1
  73.6 5.0 %all-to-all-start.3 = ((f32[32,10,128]{2,1,0:T(8,128)}), f32[32,10,128]{2,1,0:T(8,128)S(1)}, u32[]{:S(2)}, u32[]{:S(2)}) async-start(f32[32,10,128]{2,1,0:T(8,128)} %sum_transmits.1), calls=%async_computation.3 | async-start | bytes 524288 | tf_op jit(solution)/shard_map/all_to_all | solution.py:296
  78.6 11.4 %all-to-all-done.3.refs_2_ = f32[32,10,128]{2,1,0:T(8,128)S(1)} async-done(((f32[32,10,128]{2,1,0:T(8,128)}), f32[32,10,128]{2,1,0:T(8,128)S(1)}, u32[]{:S(2)}, u32[]{:S(2)}) %all-to-all-start.3) | async-done | bytes 163872 | tf_op jit(solution)/shard_map/all_to_all | solution.py:296
  90.0 0.0 copy-done.9
  90.0 0.0 copy-done.3
  90.0 2.2 %copy-done.1 = f32[8,32,4096]{2,1,0:T(8,128)S(1)} copy-done((f32[8,32,4096]{2,1,0:T(8,128)S(1)}, f32[8,32,4096]{2,1,0:T(8,128)}, u32[]{:S(2)}) %copy-start.1) | copy-done | bytes 4194328
  92.2 7.4 %gradient.1 = f32[256,128]{1,0:T(8,128)S(1)} custom-call(s32[1]{0:T(128)} %bitcast.refs_0_, f32[16]{0:T(128)S(1)} %copy-done.9, f32[32,10,128]{2,1,0:T(8,128)S(1)} %all-to-all-done.3.refs_2_, s32[32,128]{1,0:T(8,128)S(1)} %bitcast.8, f32[16,128]{1,0:T(8,128)S(1)} %get-tuple-element.15.red_ref.refs_4_, bf16[8,32,128]{2,1,0:T(8,128)(2,1)S(1)} %copy-done.3, ...), custom_call_target="tpu_custom_call" | custom-call | tf_op jit(solution)/shard_map/gradient/pallas_call | solution.py:299
  99.6 17.7 %all_to_all.31 = f32[256,1,128]{2,1,0:T(1,128)S(1)} all-to-all(f32[256,1,128]{2,1,0:T(1,128)S(1)} %bitcast.7), channel_id=1, replica_groups=mesh['tx'=8,'rx'=32] {'tx','rx'}, dimensions={0} | all-to-all | bytes 262144 | tf_op jit(solution)/shard_map/all_to_all | solution.py:330
  117.3 0.8 reduce_sum.9
  (10 shorter events, 0.1 us)
Async XLA Ops:
  0.0 90.0 %copy-start.9 = (f32[16]{0:T(128)S(1)}, f32[16]{0:T(128)}, u32[]{:S(2)}) copy-start(f32[16]{0:T(128)} %refs_1_.1) | copy-start | bytes 196
  0.0 0.9 copy-start.2
  0.9 0.7 copy-start.7
  1.5 88.5 %copy-start.3 = (bf16[8,32,128]{2,1,0:T(8,128)(2,1)S(1)}, bf16[8,32,128]{2,1,0:T(8,128)(2,1)}, u32[]{:S(2)}) copy-start(bf16[8,32,128]{2,1,0:T(8,128)(2,1)} %refs_5_.1) | copy-start | bytes 196612
  1.5 88.5 %copy-start.6 = (s32[4096]{0:T(1024)S(1)}, s32[4096]{0:T(1024)}, u32[]{:S(2)}) copy-start(s32[4096]{0:T(1024)} %param.12) | copy-start | bytes 49156
  2.4 19.2 %all-to-all-start = ((f32[32,8,128]{2,1,0:T(8,128)}), f32[32,8,128]{2,1,0:T(8,128)S(1)}, u32[]{:S(2)}, u32[]{:S(2)}) async-start(f32[32,8,128]{2,1,0:T(8,128)} %tx_delay.1), calls=%async_computation | async-start | bytes 262144 | tf_op jit(solution)/shard_map/all_to_all | solution.py:259
  12.4 1.0 copy-start.4
  13.3 0.9 copy-start.5
  14.3 0.7 copy-start.8
  35.3 1.9 %copy-start = (f32[8,32,4096]{2,1,0:T(8,128)}, f32[8,32,4096]{2,1,0:T(8,128)S(1)}, u32[]{:S(2)}) copy-start(f32[8,32,4096]{2,1,0:T(8,128)S(1)} %get-tuple-element.16.refs_6_) | copy-start | bytes 12582916
  73.6 16.4 %all-to-all-start.3 = ((f32[32,10,128]{2,1,0:T(8,128)}), f32[32,10,128]{2,1,0:T(8,128)S(1)}, u32[]{:S(2)}, u32[]{:S(2)}) async-start(f32[32,10,128]{2,1,0:T(8,128)} %sum_transmits.1), calls=%async_computation.3 | async-start | bytes 524288 | tf_op jit(solution)/shard_map/all_to_all | solution.py:296
  90.0 2.2 %copy-start.1 = (f32[8,32,4096]{2,1,0:T(8,128)S(1)}, f32[8,32,4096]{2,1,0:T(8,128)}, u32[]{:S(2)}) copy-start(f32[8,32,4096]{2,1,0:T(8,128)} %copy-done) | copy-start | bytes 12582916

commit v2 on v1

v2 whole, which is shorter than its diff:
```python
import math

import jax
import jax.numpy as jnp
from jax import lax
from jax.experimental import pallas as pl
from jax.experimental.pallas import tpu as pltpu
from jax.sharding import PartitionSpec as P

W = 8
PB = 128
PP = 256
EPS = 1e-06
LN2 = math.log(2.0)
HALF_LOG2E = 0.5 / LN2
F32 = jnp.float32


def block_diagonal(s_row, rows, cells):
    wide = jnp.concatenate([s_row] * rows, axis=1)
    shape = (rows, rows * cells)
    owner = lax.broadcasted_iota(jnp.int32, shape, 1) // cells
    mine = owner == lax.broadcasted_iota(jnp.int32, shape, 0)
    return jnp.where(mine, jnp.broadcast_to(wide, shape), 0.0).astype(jnp.bfloat16)


def tx_delay_kernel(s_ref, path_ref, out_ref):
    rows, cells, width = path_ref.shape
    left = block_diagonal(s_ref[...].astype(F32), rows, cells)
    delay = jnp.dot(
        left, path_ref[...].reshape(rows * cells, width), preferred_element_type=F32
    )
    out_ref[...] = jnp.broadcast_to((delay * HALF_LOG2E)[None], out_ref.shape)


def prepare_kernel(s_ref, path_ref, trace_ref, start_ref, delay_ref, win_ref, sample_ref, plain_ref):
    step = pl.program_id(0)
    rows, cells, pixels = path_ref.shape
    count = trace_ref.shape[0]
    blocks = start_ref.shape[2]
    per = 128 // blocks

    @pl.when(step == 0)
    def _():
        sample_ref[...] = trace_ref[...].astype(F32)

    left = block_diagonal(s_ref[...].astype(F32), rows, cells)
    delay = jnp.dot(
        left, path_ref[...].reshape(rows * cells, pixels), preferred_element_type=F32
    )
    delay = delay * HALF_LOG2E
    for k in range(blocks):
        plain_ref[:, k, :] = delay[:, k * PB : (k + 1) * PB]
    for r in range(rows):
        delay_ref[r] = jnp.concatenate([plain_ref[r]] * per, axis=0).T

    mine = pl.ds(pl.multiple_of(step * rows, rows), rows)
    shape = (rows, 128)
    group = lax.broadcasted_iota(jnp.int32, shape, 1) // blocks
    for early in range(0, count, per):
        picks = []
        for t in range(early, early + per):
            starts = jnp.concatenate([start_ref[t, mine, :]] * per, axis=1)
            for first in range(0, W, per):
                index = starts + (group + first)
                low = index & 127
                high = index >> 7
                picked = None
                for part in range(sample_ref.shape[2] // 128):
                    source = sample_ref[t, mine, part * 128 : (part + 1) * 128]
                    got = jnp.take_along_axis(source, low, axis=1, mode="promise_in_bounds")
                    picked = got if picked is None else jnp.where(high == part, got, picked)
                picks.append(picked)
        for j in range(W):
            total = None
            for i in range(per):
                rolled = picks[i * (W // per) + j // per]
                shift = ((i - j % per) * blocks) % 128
                if shift:
                    rolled = pltpu.roll(rolled, shift, 1)
                total = rolled if total is None else jnp.where(group == i, rolled, total)
            off = j - (W - 1) / 2.0
            lanes = slice(early * blocks, early * blocks + 128)
            win_ref[:, j, lanes] = total * math.exp(-0.5 * off * off)


def focus_kernel(tx_ref, rx_ref, win_ref, slope_ref, sum_ref, tx_lane_ref, total_f_ref, total_s_ref):
    blocks, count, _ = tx_ref.shape
    rows = rx_ref.shape[0]
    per = 128 // blocks
    limit = 9.25 / LN2
    halves = count // per

    for half in range(halves):
        stack = [tx_ref[:, half * per + i, :] for i in range(per)]
        tx_lane_ref[:, half * 128 : (half + 1) * 128] = jnp.concatenate(stack, axis=0).T
    total_f_ref[...] = jnp.zeros_like(total_f_ref)
    total_s_ref[...] = jnp.zeros_like(total_s_ref)

    def horner(z, c3, c2, c1, c0):
        p1 = c3 * z + c2
        p2 = p1 * z + c1
        d2 = c3 * z + p1
        return p2 * z + c0, d2 * z + p2

    def point(tap, h):
        h = jnp.minimum(jnp.maximum(h, -limit), limit)
        m = h * (-LN2)
        s = jnp.exp2(h)
        si = jnp.exp2(-h)
        gauss = jnp.exp2(m * h)
        u = s * s
        v = si * si
        up, dup = horner(u, tap[7], tap[6], tap[5], tap[4])
        down, ddown = horner(v, tap[0], tap[1], tap[2], tap[3])
        x = s * up
        y = si * down
        both = x + y
        change = (x - y) * 0.5 + ((s * u) * dup - (si * v) * ddown)
        focused = gauss * (gauss * both)
        slope = gauss * (gauss * (change + (m + m) * both))
        return focused, slope

    def receiver(r, carry):
        for half in range(halves):
            lanes = slice(half * 128, (half + 1) * 128)
            tap = [
                jnp.broadcast_to(win_ref[r, j : j + 1, lanes], (8, 128)) for j in range(W)
            ]
            for first in range(0, PB, 8):
                here = slice(first, first + 8)
                h = tx_lane_ref[here, lanes] + rx_ref[r, here, :]
                focused, slope = point(tap, h)
                slope_ref[r, here, lanes] = slope
                total_f_ref[here, lanes] += focused
                total_s_ref[here, lanes] += slope
        return carry

    lax.fori_loop(0, rows, receiver, 0)
    for source, base in ((total_f_ref, 0), (total_s_ref, count)):
        for half in range(halves):
            turned = source[:, half * 128 : (half + 1) * 128].T
            for i in range(per):
                sum_ref[:, base + half * per + i, :] = turned[i * blocks : (i + 1) * blocks]


def gather_sum_kernel(part_ref, red_ref, rep_ref):
    total = part_ref[0]
    for i in range(1, part_ref.shape[0]):
        total = total + part_ref[i]
    red_ref[...] = total
    beam = total[0 : total.shape[0] // 2]
    coherent = jnp.sum(beam, axis=0, keepdims=True)
    power = jnp.sum(beam * beam, axis=0, keepdims=True)
    pair = jnp.concatenate([coherent, power], axis=0)
    rep_ref[...] = jnp.broadcast_to(pair[None], rep_ref.shape)


def spread_kernel(pair_ref, red_ref, out_ref):
    pair = pair_ref[0]
    for i in range(1, pair_ref.shape[0]):
        pair = pair + pair_ref[i]
    count = red_ref.shape[0] // 2
    out_ref[:, 0:count, :] = jnp.broadcast_to(
        red_ref[0:count, :][None], (out_ref.shape[0], count, PB)
    )
    out_ref[:, count : count + 2, :] = jnp.broadcast_to(
        pair[None], (out_ref.shape[0], 2, PB)
    )


def patch_scales(total_tx, cot_ref, ids, coherent, power):
    patches = cot_ref.shape[0]
    square = coherent * coherent
    sums = []
    for field in (square, power):
        rows = [
            jnp.sum(jnp.where(ids == q, field, 0.0), axis=0, keepdims=True)
            for q in range(patches)
        ]
        sums.append(jnp.sum(jnp.concatenate(rows, axis=0), axis=1, keepdims=True))
    numer, power_sum = sums
    denom = total_tx * power_sum
    cot = cot_ref[...]
    value_n = -2.0 * (cot / (numer + EPS))
    value_d = 2.0 * (cot * total_tx / (denom + EPS))
    scale_n = jnp.zeros_like(square)
    scale_d = jnp.zeros_like(square)
    for q in range(patches):
        inside = ids == q
        scale_n = jnp.where(inside, value_n[q : q + 1, :], scale_n)
        scale_d = jnp.where(inside, value_d[q : q + 1, :], scale_d)
    return scale_n, scale_d


def gradient_kernel(
    total_tx,
    me_ref,
    cot_ref,
    all_ref,
    ids_ref,
    red_ref,
    tx_path_ref,
    slope_ref,
    path_ref,
    out_ref,
    bg_ref,
    bg_lane_ref,
    grad_ref,
    acc_ref,
):
    step = pl.program_id(0)
    rows, cells, _ = path_ref.shape
    blocks = all_ref.shape[0]
    count = red_ref.shape[0] // 2
    per = 128 // blocks

    @pl.when(step == 0)
    def _():
        coherent = all_ref[:, count, :]
        power = all_ref[:, count + 1, :]
        scale_n, scale_d = patch_scales(total_tx, cot_ref, ids_ref[...] // PP, coherent, power)
        common = coherent * scale_n
        for t in range(count):
            bg_ref[t] = common + all_ref[:, t, :] * scale_d
        for half in range(count // per):
            stack = [bg_ref[half * per + i] for i in range(per)]
            bg_lane_ref[:, half * 128 : (half + 1) * 128] = jnp.concatenate(stack, axis=0).T
        acc = jnp.zeros((cells, PB), F32)
        for t in range(count):
            own = bg_ref[t, pl.ds(me_ref[0], 1), :] * red_ref[count + t : count + t + 1, :]
            acc = acc + tx_path_ref[t].astype(F32) * own
        acc_ref[...] = acc

    acc = [acc_ref[...], jnp.zeros((cells, PB), F32)]
    for r in range(rows):
        grad = None
        for half in range(count // per):
            lanes = slice(half * 128, (half + 1) * 128)
            term = slope_ref[r, :, lanes] * bg_lane_ref[:, lanes]
            grad = term if grad is None else grad + term
        grad = grad.T
        total = grad[0:blocks]
        for i in range(1, per):
            total = total + grad[i * blocks : (i + 1) * blocks]
        grad_ref[r] = total
        for k in range(blocks):
            paths = path_ref[r, :, k * PB : (k + 1) * PB].astype(F32)
            acc[k % 2] = acc[k % 2] + paths * grad_ref[r, k : k + 1, :]
    acc = acc[0] + acc[1]
    acc_ref[...] = acc

    @pl.when(step == pl.num_programs(0) - 1)
    def _():
        ones = jnp.ones((8, PB), F32)
        row = lax.dot_general(
            ones,
            acc,
            (((1,), (1,)), ((), ())),
            precision=lax.Precision.HIGHEST,
            preferred_element_type=F32,
        )
        row = jnp.concatenate([row] * (PB // cells), axis=1)
        out_ref[...] = jnp.broadcast_to(row[0:1, :], out_ref.shape)


def params(megabytes):
    return pltpu.CompilerParams(vmem_limit_bytes=megabytes * 1024 * 1024)


def whole(shape):
    return pl.BlockSpec(shape, lambda *_: (0,) * len(shape))


def shaped(*shape):
    return jax.ShapeDtypeStruct(shape, F32)


def tx_delays(s_row, tx_paths, rx_size):
    tx_count, _, own_pixels = tx_paths.shape
    return pl.pallas_call(
        tx_delay_kernel,
        out_shape=shaped(rx_size, tx_count, own_pixels),
        compiler_params=params(4),
        name="tx_delay",
    )(s_row, tx_paths)


def prepare(s_row, rx_paths, traces, tap_start):
    rx_count, cells, pixels = rx_paths.shape
    tx_count, _, samples = traces.shape
    blocks = pixels // PB
    rows = 8
    return pl.pallas_call(
        prepare_kernel,
        grid=(rx_count // rows,),
        in_specs=[
            whole((1, cells)),
            pl.BlockSpec((rows, cells, pixels), lambda i: (i, 0, 0)),
            whole((tx_count, rx_count, samples)),
            whole((tx_count, rx_count, blocks)),
        ],
        out_specs=[
            pl.BlockSpec((rows, PB, 128), lambda i: (i, 0, 0)),
            pl.BlockSpec((rows, W, tx_count * blocks), lambda i: (i, 0, 0)),
        ],
        out_shape=[shaped(rx_count, PB, 128), shaped(rx_count, W, tx_count * blocks)],
        scratch_shapes=[
            pltpu.VMEM((tx_count, rx_count, samples), F32),
            pltpu.VMEM((rows, blocks, PB), F32),
        ],
        compiler_params=params(12),
        name="prepare",
    )(s_row, rx_paths, traces, tap_start)


def focus(tx_delay, rx_delay, window):
    blocks, tx_count, _ = tx_delay.shape
    rx_count = rx_delay.shape[0]
    lanes = tx_count * blocks
    return pl.pallas_call(
        focus_kernel,
        out_shape=[shaped(rx_count, PB, lanes), shaped(blocks, 2 * tx_count, PB)],
        scratch_shapes=[pltpu.VMEM((PB, lanes), F32)] * 3,
        compiler_params=params(12),
        name="focus",
    )(tx_delay, rx_delay, window)


def gradient(total_tx, parts, me, patch_cotangent, every, pixel_order, red, tx_paths, slope, rx_paths):
    rx_count, cells, pixels = rx_paths.shape
    blocks = pixels // PB
    tx_count = tx_paths.shape[0]
    lanes = tx_count * blocks
    rows = 4
    return pl.pallas_call(
        lambda *refs: gradient_kernel(total_tx, *refs),
        grid=(rx_count // rows,),
        in_specs=[
            pl.BlockSpec(memory_space=pltpu.SMEM),
            whole((patch_cotangent.shape[0], 1)),
            whole(every.shape),
            whole((blocks, PB)),
            whole(red.shape),
            whole(tx_paths.shape),
            pl.BlockSpec((rows, PB, lanes), lambda i: (i, 0, 0)),
            pl.BlockSpec((rows, cells, pixels), lambda i: (i, 0, 0)),
        ],
        out_specs=whole((parts, PB)),
        out_shape=shaped(parts, PB),
        scratch_shapes=[
            pltpu.VMEM((tx_count, blocks, PB), F32),
            pltpu.VMEM((PB, lanes), F32),
            pltpu.VMEM((rows, blocks, PB), F32),
            pltpu.VMEM((cells, PB), F32),
        ],
        compiler_params=params(12),
        name="gradient",
    )(
        me,
        patch_cotangent.reshape(-1, 1),
        every,
        pixel_order.reshape(blocks, PB),
        red,
        tx_paths,
        slope,
        rx_paths,
    )


def on_device(slowness, tx_paths, rx_paths, traces, tap_start, pixel_order, patch_cotangent):
    tx_count, cells, _ = tx_paths.shape
    tx_size = lax.axis_size("tx")
    rx_size = lax.axis_size("rx")
    s_row = slowness.reshape(1, cells)

    delay = tx_delays(s_row, tx_paths, rx_size)
    rx_delay, window = prepare(s_row, rx_paths, traces, tap_start)
    tx_delay = lax.all_to_all(delay, "rx", 0, 0)
    slope, part = focus(tx_delay, rx_delay, window)
    part = lax.all_to_all(part, "rx", 0, 0)
    red, pair = pl.pallas_call(
        gather_sum_kernel,
        out_shape=[shaped(2 * tx_count, PB), shaped(tx_size, 2, PB)],
        compiler_params=params(4),
        name="sum_receivers",
    )(part)
    pair = lax.all_to_all(pair, "tx", 0, 0)
    spread = pl.pallas_call(
        spread_kernel,
        out_shape=shaped(rx_size, tx_count + 2, PB),
        compiler_params=params(4),
        name="sum_transmits",
    )(pair, red)
    every = lax.all_to_all(spread, "rx", 0, 0)
    me = lax.axis_index("rx").astype(jnp.int32).reshape(1)
    share = gradient(
        tx_count * tx_size,
        tx_size * rx_size,
        me,
        patch_cotangent,
        every,
        pixel_order,
        red,
        tx_paths,
        slope,
        rx_paths,
    )
    share = lax.all_to_all(share, ("tx", "rx"), 0, 0, tiled=True)
    return share.sum(0)[:cells]


def solution(mesh):
    in_specs = (
        P(),
        P("tx", None, "rx"),
        P("rx", None, None),
        P("tx", "rx", None),
        P("tx", "rx", None),
        P(),
        P(),
    )
    out_specs = P()
    return jax.shard_map(
        on_device, mesh=mesh, in_specs=in_specs, out_specs=out_specs, check_vma=False
    )
```

time: 119 us -> 111 us (0.933)
  Pallas kernels: 29.4 us -> 15.2 us
  local copies, waits for them, and re-layouts: 8.14 us -> 15 us
    pallas_call x6, Pallas kernels: 29.4 us -> 15.2 us  [the longest x1 7.39 us: focus(): pl.pallas_call(focus_kernel, out_shape=[shaped(rx_count, PB, lanes), shap...]
    unnamed x20 -> x24, local copies, waits for them, and re-layouts: 8.14 us -> 14.9 us
  transfers between devices with their start and end apart: 2 -> 2, of which waited for: 1 -> 1; matrix products, arithmetic and copies ran while one was open for 0% -> 0% of each run, Pallas kernels for 6% -> 3%
where the time goes in v2:
time: 111 us
  blocking collectives  53.3 us (48%)
  Pallas kernels  15.2 us (14%)
  local copies, waits for them, and re-layouts  15 us (14%)
  starting transfers between devices  15 us (14%)
  waiting for transfers between devices  11.3 us (10%)
    all_to_all x1, blocking collectives, on_device(): part = lax.all_to_all(part, 'rx', 0, 0)  18.7 us
    all_to_all x1, blocking collectives, on_device(): share = lax.all_to_all(share, ('tx', 'rx'), 0, 0, tiled=True)  17.7 us
    all_to_all x1, blocking collectives, on_device(): pair = lax.all_to_all(pair, 'tx', 0, 0)  16.9 us
    unnamed x24, local copies, waits for them, and re-layouts  14.9 us
    all_to_all x1, waiting for transfers between devices, on_device(): every = lax.all_to_all(spread, 'rx', 0, 0)  11.3 us
    all_to_all x1, starting transfers between devices, on_device(): tx_delay = lax.all_to_all(delay, 'rx', 0, 0)  10 us
    pallas_call x1, Pallas kernels, focus(): pl.pallas_call(focus_kernel, out_shape=[shaped(rx_count, PB, lanes), shap...  7.39 us
    all_to_all x1, starting transfers between devices, on_device(): every = lax.all_to_all(spread, 'rx', 0, 0)  5.01 us
  transfers between devices with their start and end apart: 2, of which 1 were waited for; matrix products, arithmetic and copies ran while one was open for 0% of the time, Pallas kernels for 3%

profile of v2, /device:TPU:1, one launch (start us, length us, event | category | flops | bytes accessed | tf_op | source)
XLA Modules:
  0.0 110.7 jit_solution(4135570627364377713)
XLA Ops:
  0.0 0.8 copy-done.4
  0.8 0.7 copy-done.9
  1.5 0.9 tx_delay.1
  2.4 10.0 %all-to-all-start = ((f32[32,8,128]{2,1,0:T(8,128)}), f32[32,8,128]{2,1,0:T(8,128)S(1)}, u32[]{:S(2)}, u32[]{:S(2)}) async-start(f32[32,8,128]{2,1,0:T(8,128)} %tx_delay.1), calls=%async_computation | async-start | bytes 262144 | tf_op jit(solution)/shard_map/all_to_all | solution.py:379
  12.4 0.0 copy-start
  12.4 3.4 %copy-done = bf16[32,32,4096]{2,1,0:T(8,128)(2,1)S(1)} copy-done((bf16[32,32,4096]{2,1,0:T(8,128)(2,1)S(1)}, bf16[32,32,4096]{2,1,0:T(8,128)(2,1)}, u32[]{:S(2)}) %copy-start) | copy-done | bytes 8388632
  15.8 0.9 copy-done.6
  16.7 0.9 copy-done.7
  17.6 0.7 copy-done.10
  18.3 2.8 %prepare.1 = (f32[32,128,128]{2,1,0:T(8,128)S(1)}, f32[32,8,256]{2,1,0:T(8,128)S(1)}) custom-call(bf16[1,32]{1,0:T(2,128)(2,1)S(1)} %bitcast.11, bf16[32,32,4096]{2,1,0:T(8,128)(2,1)S(1)} %copy-done, bf16[8,32,512]{2,1,0:T(8,128)(2,1)S(1)} %copy-done.6, s32[8,32,32]{2,1,0:T(8,128)S(1)} %copy-done.7), custom_call_target="tpu_custom_call" | custom-call | tf_op jit(solution)/shard_map/prepare/pallas_call | solution.py:294
  21.1 0.0 all-to-all-done.tx_ref
  21.1 7.4 %focus.1 = (f32[32,128,256]{2,1,0:T(8,128)S(1)}, f32[32,16,128]{2,1,0:T(8,128)S(1)}) custom-call(f32[32,8,128]{2,1,0:T(8,128)S(1)} %all-to-all-done.tx_ref, f32[32,128,128]{2,1,0:T(8,128)S(1)} %get-tuple-element.11.rx_ref, f32[32,8,256]{2,1,0:T(8,128)S(1)} %get-tuple-element.12.win_ref), custom_call_target="tpu_custom_call" | custom-call | tf_op jit(solution)/shard_map/focus/pallas_call | solution.py:321
  28.5 2.0 %copy-done.2 = f32[32,128,256]{2,1,0:T(8,128)} copy-done((f32[32,128,256]{2,1,0:T(8,128)}, f32[32,128,256]{2,1,0:T(8,128)S(1)}, u32[]{:S(2)}) %copy-start.2) | copy-done | bytes 4194328
  30.5 18.7 %all_to_all.29.part_ref = f32[32,16,128]{2,1,0:T(8,128)S(1)} all-to-all(f32[32,16,128]{2,1,0:T(8,128)S(1)} %get-tuple-element.13), channel_id=1, replica_groups=mesh['tx'=8,'rx'=32] {'rx'}, dimensions={0} | all-to-all | bytes 524288 | tf_op jit(solution)/shard_map/all_to_all | solution.py:381
  49.2 16.9 %all_to_all.30.pair_ref = f32[8,2,128]{2,1,0:T(2,128)S(1)} all-to-all(f32[8,2,128]{2,1,0:T(2,128)S(1)} %get-tuple-element.14), channel_id=1, replica_groups=mesh['tx'=8,'rx'=32] {'tx'}, dimensions={0} | all-to-all | bytes 16384 | tf_op jit(solution)/shard_map/all_to_all | solution.py:388
  66.1 0.7 sum_transmits.1
  66.8 5.0 %all-to-all-start.3 = ((f32[32,10,128]{2,1,0:T(8,128)}), f32[32,10,128]{2,1,0:T(8,128)S(1)}, u32[]{:S(2)}, u32[]{:S(2)}) async-start(f32[32,10,128]{2,1,0:T(8,128)} %sum_transmits.1), calls=%async_computation.3 | async-start | bytes 524288 | tf_op jit(solution)/shard_map/all_to_all | solution.py:395
  71.9 0.1 copy.9.refs_1_
  71.9 11.3 %all-to-all-done.3.refs_2_ = f32[32,10,128]{2,1,0:T(8,128)S(1)} async-done(((f32[32,10,128]{2,1,0:T(8,128)}), f32[32,10,128]{2,1,0:T(8,128)S(1)}, u32[]{:S(2)}, u32[]{:S(2)}) %all-to-all-start.3) | async-done | bytes 163872 | tf_op jit(solution)/shard_map/all_to_all | solution.py:395
  83.2 3.4 %copy-done.1 = bf16[32,32,4096]{2,1,0:T(8,128)(2,1)S(1)} copy-done((bf16[32,32,4096]{2,1,0:T(8,128)(2,1)S(1)}, bf16[32,32,4096]{2,1,0:T(8,128)(2,1)}, u32[]{:S(2)}) %copy-start.1) | copy-done | bytes 8388632
  86.6 2.2 %copy-done.3 = f32[32,128,256]{2,1,0:T(8,128)S(1)} copy-done((f32[32,128,256]{2,1,0:T(8,128)S(1)}, f32[32,128,256]{2,1,0:T(8,128)}, u32[]{:S(2)}) %copy-start.3) | copy-done | bytes 4194328
  88.8 3.4 %gradient.1 = f32[256,128]{1,0:T(8,128)S(1)} custom-call(s32[1]{0:T(128)} %bitcast.refs_0_, f32[16,1]{1,0:T(8,128)S(1)} %copy.9.refs_1_, f32[32,10,128]{2,1,0:T(8,128)S(1)} %all-to-all-done.3.refs_2_, s32[32,128]{1,0:T(8,128)S(1)} %bitcast.9, f32[16,128]{1,0:T(8,128)S(1)} %get-tuple-element.15.red_ref.refs_4_, bf16[8,32,128]{2,1,0:T(8,128)(2,1)S(1)} %copy-done.5, ...), custom_call_target="tpu_custom_call" | custom-call | tf_op jit(solution)/shard_map/gradient/pallas_call | solution.py:336
  92.2 17.7 %all_to_all.31 = f32[256,1,128]{2,1,0:T(1,128)S(1)} all-to-all(f32[256,1,128]{2,1,0:T(1,128)S(1)} %bitcast.8), channel_id=1, replica_groups=mesh['tx'=8,'rx'=32] {'tx','rx'}, dimensions={0} | all-to-all | bytes 262144 | tf_op jit(solution)/shard_map/all_to_all | solution.py:409
  109.9 0.8 reduce_sum.9
  (15 shorter events, 0.1 us)
Async XLA Ops:
  0.0 0.8 copy-start.4
  0.8 0.7 copy-start.9
  2.4 18.7 %all-to-all-start = ((f32[32,8,128]{2,1,0:T(8,128)}), f32[32,8,128]{2,1,0:T(8,128)S(1)}, u32[]{:S(2)}, u32[]{:S(2)}) async-start(f32[32,8,128]{2,1,0:T(8,128)} %tx_delay.1), calls=%async_computation | async-start | bytes 262144 | tf_op jit(solution)/shard_map/all_to_all | solution.py:379
  12.4 3.4 %copy-start = (bf16[32,32,4096]{2,1,0:T(8,128)(2,1)S(1)}, bf16[32,32,4096]{2,1,0:T(8,128)(2,1)}, u32[]{:S(2)}) copy-start(bf16[32,32,4096]{2,1,0:T(8,128)(2,1)} %refs_7_.1) | copy-start | bytes 25165828
  15.8 0.9 copy-start.6
  16.7 0.9 copy-start.7
  17.6 0.7 copy-start.10
  18.3 53.6 %copy-start.11 = (f32[16]{0:T(128)S(1)}, f32[16]{0:T(128)}, u32[]{:S(2)}) copy-start(f32[16]{0:T(128)} %param.13) | copy-start | bytes 196
  18.3 65.0 %copy-start.5 = (bf16[8,32,128]{2,1,0:T(8,128)(2,1)S(1)}, bf16[8,32,128]{2,1,0:T(8,128)(2,1)}, u32[]{:S(2)}) copy-start(bf16[8,32,128]{2,1,0:T(8,128)(2,1)} %refs_5_.1) | copy-start | bytes 196612
  18.3 65.0 %copy-start.8 = (s32[4096]{0:T(1024)S(1)}, s32[4096]{0:T(1024)}, u32[]{:S(2)}) copy-start(s32[4096]{0:T(1024)} %param.12) | copy-start | bytes 49156
  28.5 2.0 %copy-start.2 = (f32[32,128,256]{2,1,0:T(8,128)}, f32[32,128,256]{2,1,0:T(8,128)S(1)}, u32[]{:S(2)}) copy-start(f32[32,128,256]{2,1,0:T(8,128)S(1)} %get-tuple-element.16.refs_6_) | copy-start | bytes 12582916
  66.8 16.4 %all-to-all-start.3 = ((f32[32,10,128]{2,1,0:T(8,128)}), f32[32,10,128]{2,1,0:T(8,128)S(1)}, u32[]{:S(2)}, u32[]{:S(2)}) async-start(f32[32,10,128]{2,1,0:T(8,128)} %sum_transmits.1), calls=%async_computation.3 | async-start | bytes 524288 | tf_op jit(solution)/shard_map/all_to_all | solution.py:395
  83.2 3.4 %copy-start.1 = (bf16[32,32,4096]{2,1,0:T(8,128)(2,1)S(1)}, bf16[32,32,4096]{2,1,0:T(8,128)(2,1)}, u32[]{:S(2)}) copy-start(bf16[32,32,4096]{2,1,0:T(8,128)(2,1)} %refs_7_.1) | copy-start | bytes 25165828
  86.6 2.2 %copy-start.3 = (f32[32,128,256]{2,1,0:T(8,128)S(1)}, f32[32,128,256]{2,1,0:T(8,128)}, u32[]{:S(2)}) copy-start(f32[32,128,256]{2,1,0:T(8,128)} %copy-done.2) | copy-start | bytes 12582916

commit v3 on v2

--- a/solution.py
+++ b/solution.py
@@ -181,7 +181,10 @@
         sums.append(jnp.sum(jnp.concatenate(rows, axis=0), axis=1, keepdims=True))
     numer, power_sum = sums
     denom = total_tx * power_sum
-    cot = cot_ref[...]
+    cot = jnp.zeros_like(numer)
+    row = lax.broadcasted_iota(jnp.int32, cot.shape, 0)
+    for q in range(patches):
+        cot = jnp.where(row == q, cot_ref[q], cot)
     value_n = -2.0 * (cot / (numer + EPS))
     value_d = 2.0 * (cot * total_tx / (denom + EPS))
     scale_n = jnp.zeros_like(square)
@@ -195,7 +198,6 @@
 
 def gradient_kernel(
     total_tx,
-    me_ref,
     cot_ref,
     all_ref,
     ids_ref,
@@ -227,8 +229,9 @@
             stack = [bg_ref[half * per + i] for i in range(per)]
             bg_lane_ref[:, half * 128 : (half + 1) * 128] = jnp.concatenate(stack, axis=0).T
         acc = jnp.zeros((cells, PB), F32)
+        me = lax.axis_index("rx")
         for t in range(count):
-            own = bg_ref[t, pl.ds(me_ref[0], 1), :] * red_ref[count + t : count + t + 1, :]
+            own = bg_ref[t, pl.ds(me, 1), :] * red_ref[count + t : count + t + 1, :]
             acc = acc + tx_path_ref[t].astype(F32) * own
         acc_ref[...] = acc
 
@@ -276,6 +279,10 @@
     return jax.ShapeDtypeStruct(shape, F32)
 
 
+def in_hbm(array):
+    return pltpu.with_memory_space_constraint(array, pltpu.HBM)
+
+
 def tx_delays(s_row, tx_paths, rx_size):
     tx_count, _, own_pixels = tx_paths.shape
     return pl.pallas_call(
@@ -283,7 +290,7 @@
         out_shape=shaped(rx_size, tx_count, own_pixels),
         compiler_params=params(4),
         name="tx_delay",
-    )(s_row, tx_paths)
+    )(in_hbm(s_row), in_hbm(tx_paths))
 
 
 def prepare(s_row, rx_paths, traces, tap_start):
@@ -311,7 +318,7 @@
         ],
         compiler_params=params(12),
         name="prepare",
-    )(s_row, rx_paths, traces, tap_start)
+    )(in_hbm(s_row), in_hbm(rx_paths), in_hbm(traces), in_hbm(tap_start))
 
 
 def focus(tx_delay, rx_delay, window):
@@ -327,7 +334,7 @@
     )(tx_delay, rx_delay, window)
 
 
-def gradient(total_tx, parts, me, patch_cotangent, every, pixel_order, red, tx_paths, slope, rx_paths):
+def gradient(total_tx, parts, patch_cotangent, every, pixel_order, red, tx_paths, slope, rx_paths):
     rx_count, cells, pixels = rx_paths.shape
     blocks = pixels // PB
     tx_count = tx_paths.shape[0]
@@ -338,7 +345,6 @@
         grid=(rx_count // rows,),
         in_specs=[
             pl.BlockSpec(memory_space=pltpu.SMEM),
-            whole((patch_cotangent.shape[0], 1)),
             whole(every.shape),
             whole((blocks, PB)),
             whole(red.shape),
@@ -357,8 +363,7 @@
         compiler_params=params(12),
         name="gradient",
     )(
-        me,
-        patch_cotangent.reshape(-1, 1),
+        patch_cotangent,
         every,
         pixel_order.reshape(blocks, PB),
         red,
@@ -393,11 +398,9 @@
         name="sum_transmits",
     )(pair, red)
     every = lax.all_to_all(spread, "rx", 0, 0)
-    me = lax.axis_index("rx").astype(jnp.int32).reshape(1)
     share = gradient(
         tx_count * tx_size,
         tx_size * rx_size,
-        me,
         patch_cotangent,
         every,
         pixel_order,

time: 111 us -> 103 us (0.928)
  blocking collectives: 53.3 us -> 66.3 us
  local copies, waits for them, and re-layouts: 15 us -> 3.4 us
  waiting for transfers between devices: 11.3 us -> 3.15 us
  starting transfers between devices: 15 us -> 10 us
  Pallas kernels: 15.2 us -> 18.6 us
    all_to_all x0 -> x1, blocking collectives: none -> 16.1 us  [on_device(): every = lax.all_to_all(spread, 'rx', 0, 0)]
    unnamed x24 -> x8, local copies, waits for them, and re-layouts: 14.9 us -> 3.4 us
    all_to_all x1 -> x0, waiting for transfers between devices: 11.3 us -> none  [on_device(): every = lax.all_to_all(spread, 'rx', 0, 0)]
    all_to_all x1 -> x0, starting transfers between devices: 5.01 us -> none  [on_device(): every = lax.all_to_all(spread, 'rx', 0, 0)]
    all_to_all x1, waiting for transfers between devices: 0.02 us -> 3.15 us  [on_device(): tx_delay = lax.all_to_all(delay, 'rx', 0, 0)]
    all_to_all x1, blocking collectives: 18.7 us -> 15.6 us  [on_device(): part = lax.all_to_all(part, 'rx', 0, 0)]
    pallas_call x1, Pallas kernels: 2.78 us -> 5.51 us  [prepare(): pl.pallas_call(prepare_kernel, grid=(rx_count // rows,), in_specs=[whole(...]
  transfers between devices with their start and end apart: 2 -> 1, of which waited for: 1 -> 1; matrix products, arithmetic and copies ran while one was open for 0% -> 0% of each run, Pallas kernels for 3% -> 5%
where the time goes in v3:
time: 103 us; the launch traced here: 102 us
  blocking collectives  66.3 us (64%)
  Pallas kernels  18.6 us (18%)
  starting transfers between devices  10 us (10%)
  local copies, waits for them, and re-layouts  3.4 us (3%)
  waiting for transfers between devices  3.15 us (3%)
    all_to_all x1, blocking collectives, on_device(): share = lax.all_to_all(share, ('tx', 'rx'), 0, 0, tiled=True)  17.7 us
    all_to_all x1, blocking collectives, on_device(): pair = lax.all_to_all(pair, 'tx', 0, 0)  16.9 us
    all_to_all x1, blocking collectives, on_device(): every = lax.all_to_all(spread, 'rx', 0, 0)  16.1 us
    all_to_all x1, blocking collectives, on_device(): part = lax.all_to_all(part, 'rx', 0, 0)  15.6 us
    all_to_all x1, starting transfers between devices, on_device(): tx_delay = lax.all_to_all(delay, 'rx', 0, 0)  10 us
    pallas_call x1, Pallas kernels, focus(): pl.pallas_call(focus_kernel, out_shape=[shaped(rx_count, PB, lanes), shap...  7.39 us
    pallas_call x1, Pallas kernels, prepare(): pl.pallas_call(prepare_kernel, grid=(rx_count // rows,), in_specs=[whole(...  5.51 us
    pallas_call x1, Pallas kernels, gradient(): pl.pallas_call(lambda *refs: gradient_kernel(total_tx, *refs), grid=(rx_c...  3.98 us
  transfers between devices with their start and end apart: 1, of which 1 were waited for; matrix products, arithmetic and copies ran while one was open for 0% of the time, Pallas kernels for 5%

profile of v3, /device:TPU:1, one launch (start us, length us, event | category | flops | bytes accessed | tf_op | source)
XLA Modules:
  0.0 102.3 jit_solution(11207585191912493119)
XLA Ops:
  0.0 1.7 %tx_delay.1 = f32[32,8,128]{2,1,0:T(8,128)} custom-call(bf16[1,32]{1,0:T(2,128)(2,1)} %bitcast.8, bf16[8,32,128]{2,1,0:T(8,128)(2,1)} %refs_4_.1), custom_call_target="tpu_custom_call" | custom-call | tf_op jit(solution)/shard_map/tx_delay/pallas_call | solution.py:288
  1.7 10.0 %all-to-all-start = ((f32[32,8,128]{2,1,0:T(8,128)}), f32[32,8,128]{2,1,0:T(8,128)S(1)}, u32[]{:S(2)}, u32[]{:S(2)}) async-start(f32[32,8,128]{2,1,0:T(8,128)} %tx_delay.1), calls=%async_computation | async-start | bytes 262144 | tf_op jit(solution)/shard_map/all_to_all | solution.py:384
  11.7 0.0 copy-start.1
  11.7 0.0 copy-start.2
  11.8 0.0 copy-start.3
  11.8 5.5 %prepare.1 = (f32[32,128,128]{2,1,0:T(8,128)S(1)}, f32[32,8,256]{2,1,0:T(8,128)S(1)}) custom-call(bf16[1,32]{1,0:T(2,128)(2,1)} %bitcast.9, bf16[32,32,4096]{2,1,0:T(8,128)(2,1)} %refs_6_.1, bf16[8,32,512]{2,1,0:T(8,128)(2,1)} %trace_ref.1, s32[8,32,32]{2,1,0:T(8,128)} %start_ref.1), custom_call_target="tpu_custom_call" | custom-call | tf_op jit(solution)/shard_map/prepare/pallas_call | solution.py:301
  17.3 3.2 %all-to-all-done.tx_ref = f32[32,8,128]{2,1,0:T(8,128)S(1)} async-done(((f32[32,8,128]{2,1,0:T(8,128)}), f32[32,8,128]{2,1,0:T(8,128)S(1)}, u32[]{:S(2)}, u32[]{:S(2)}) %all-to-all-start) | async-done | bytes 131104 | tf_op jit(solution)/shard_map/all_to_all | solution.py:384
  20.4 7.4 %focus.1 = (f32[32,128,256]{2,1,0:T(8,128)S(1)}, f32[32,16,128]{2,1,0:T(8,128)S(1)}) custom-call(f32[32,8,128]{2,1,0:T(8,128)S(1)} %all-to-all-done.tx_ref, f32[32,128,128]{2,1,0:T(8,128)S(1)} %get-tuple-element.11.rx_ref, f32[32,8,256]{2,1,0:T(8,128)S(1)} %get-tuple-element.12.win_ref), custom_call_target="tpu_custom_call" | custom-call | tf_op jit(solution)/shard_map/focus/pallas_call | solution.py:328
  27.8 15.6 %all_to_all.29.part_ref = f32[32,16,128]{2,1,0:T(8,128)S(1)} all-to-all(f32[32,16,128]{2,1,0:T(8,128)S(1)} %get-tuple-element.13), channel_id=1, replica_groups=mesh['tx'=8,'rx'=32] {'rx'}, dimensions={0} | all-to-all | bytes 524288 | tf_op jit(solution)/shard_map/all_to_all | solution.py:386
  43.5 16.9 %all_to_all.30.pair_ref = f32[8,2,128]{2,1,0:T(2,128)S(1)} all-to-all(f32[8,2,128]{2,1,0:T(2,128)S(1)} %get-tuple-element.14), channel_id=1, replica_groups=mesh['tx'=8,'rx'=32] {'tx'}, dimensions={0} | all-to-all | bytes 16384 | tf_op jit(solution)/shard_map/all_to_all | solution.py:393
  60.4 16.1 %all_to_all.31.refs_1_ = f32[32,10,128]{2,1,0:T(8,128)S(1)} all-to-all(f32[32,10,128]{2,1,0:T(8,128)S(1)} %sum_transmits.1), channel_id=1, replica_groups=mesh['tx'=8,'rx'=32] {'rx'}, dimensions={0} | all-to-all | bytes 327680 | tf_op jit(solution)/shard_map/all_to_all | solution.py:400
  76.5 0.0 copy-done.1
  76.5 0.0 copy-done.2
  76.5 0.0 copy-done.3
  76.5 0.0 copy-start
  76.5 3.4 %copy-done = bf16[32,32,4096]{2,1,0:T(8,128)(2,1)S(1)} copy-done((bf16[32,32,4096]{2,1,0:T(8,128)(2,1)S(1)}, bf16[32,32,4096]{2,1,0:T(8,128)(2,1)}, u32[]{:S(2)}) %copy-start) | copy-done | bytes 8388632
  79.9 4.0 %gradient.1 = f32[256,128]{1,0:T(8,128)S(1)} custom-call(f32[16]{0:T(128)S(1)} %copy-done.3, f32[32,10,128]{2,1,0:T(8,128)S(1)} %all_to_all.31.refs_1_, s32[32,128]{1,0:T(8,128)S(1)} %bitcast.7, f32[16,128]{1,0:T(8,128)S(1)} %get-tuple-element.15.red_ref.refs_3_, bf16[8,32,128]{2,1,0:T(8,128)(2,1)S(1)} %copy-done.1, ...), custom_call_target="tpu_custom_call" | custom-call | tf_op jit(solution)/shard_map/gradient/pallas_call | solution.py:343
  83.9 17.7 %all_to_all.32 = f32[256,1,128]{2,1,0:T(1,128)S(1)} all-to-all(f32[256,1,128]{2,1,0:T(1,128)S(1)} %bitcast.6), channel_id=1, replica_groups=mesh['tx'=8,'rx'=32] {'tx','rx'}, dimensions={0} | all-to-all | bytes 262144 | tf_op jit(solution)/shard_map/all_to_all | solution.py:412
  101.5 0.8 reduce_sum.9
  (2 shorter events, 0.1 us)
Async XLA Ops:
  1.7 18.7 %all-to-all-start = ((f32[32,8,128]{2,1,0:T(8,128)}), f32[32,8,128]{2,1,0:T(8,128)S(1)}, u32[]{:S(2)}, u32[]{:S(2)}) async-start(f32[32,8,128]{2,1,0:T(8,128)} %tx_delay.1), calls=%async_computation | async-start | bytes 262144 | tf_op jit(solution)/shard_map/all_to_all | solution.py:384
  11.7 64.7 %copy-start.1 = (bf16[8,32,128]{2,1,0:T(8,128)(2,1)S(1)}, bf16[8,32,128]{2,1,0:T(8,128)(2,1)}, u32[]{:S(2)}) copy-start(bf16[8,32,128]{2,1,0:T(8,128)(2,1)} %refs_4_.1) | copy-start | bytes 196612
  11.7 64.7 %copy-start.2 = (s32[4096]{0:T(1024)S(1)}, s32[4096]{0:T(1024)}, u32[]{:S(2)}) copy-start(s32[4096]{0:T(1024)} %param.12) | copy-start | bytes 49156
  11.8 64.7 %copy-start.3 = (f32[16]{0:T(128)S(1)}, f32[16]{0:T(128)}, u32[]{:S(2)}) copy-start(f32[16]{0:T(128)} %refs_0_.1) | copy-start | bytes 196
  76.5 3.4 %copy-start = (bf16[32,32,4096]{2,1,0:T(8,128)(2,1)S(1)}, bf16[32,32,4096]{2,1,0:T(8,128)(2,1)}, u32[]{:S(2)}) copy-start(bf16[32,32,4096]{2,1,0:T(8,128)(2,1)} %refs_6_.1) | copy-start | bytes 25165828

commit v4 on v3

--- a/solution.py
+++ b/solution.py
@@ -84,7 +84,23 @@
             win_ref[:, j, lanes] = total * math.exp(-0.5 * off * off)
 
 
-def focus_kernel(tx_ref, rx_ref, win_ref, slope_ref, sum_ref, tx_lane_ref, total_f_ref, total_s_ref):
+def focus_kernel(
+    tx_ref,
+    rx_ref,
+    win_ref,
+    path_ref,
+    slope_ref,
+    keep_ref,
+    give_ref,
+    path_copy_ref,
+    tx_lane_ref,
+    total_f_ref,
+    total_s_ref,
+    turned_ref,
+    copied,
+):
+    fetch = pltpu.make_async_copy(path_ref, path_copy_ref, copied)
+    fetch.start()
     blocks, count, _ = tx_ref.shape
     rows = rx_ref.shape[0]
     per = 128 // blocks
@@ -137,11 +153,21 @@
         return carry
 
     lax.fori_loop(0, rows, receiver, 0)
+    mine = lax.axis_index("rx") % 2
     for source, base in ((total_f_ref, 0), (total_s_ref, count)):
         for half in range(halves):
-            turned = source[:, half * 128 : (half + 1) * 128].T
+            turned_ref[...] = source[:, half * 128 : (half + 1) * 128].T
             for i in range(per):
-                sum_ref[:, base + half * per + i, :] = turned[i * blocks : (i + 1) * blocks]
+                row = base + half * per + i
+                even = turned_ref[pl.ds(i * blocks, blocks // 2, stride=2), :]
+                odd = turned_ref[pl.ds(i * blocks + 1, blocks // 2, stride=2), :]
+                keep_ref[:, row, :] = jnp.where(mine == 0, even, odd)
+                give_ref[:, row, :] = jnp.where(mine == 0, odd, even)
+    fetch.wait()
+
+
+def pair_sum_kernel(keep_ref, got_ref, out_ref):
+    out_ref[...] = keep_ref[...] + got_ref[...]
 
 
 def gather_sum_kernel(part_ref, red_ref, rep_ref):
@@ -199,72 +225,75 @@
 def gradient_kernel(
     total_tx,
     cot_ref,
-    all_ref,
+    here_ref,
+    there_ref,
     ids_ref,
     red_ref,
     tx_path_ref,
     slope_ref,
     path_ref,
     out_ref,
+    all_ref,
     bg_ref,
     bg_lane_ref,
     grad_ref,
-    acc_ref,
 ):
-    step = pl.program_id(0)
     rows, cells, _ = path_ref.shape
-    blocks = all_ref.shape[0]
+    pairs = here_ref.shape[0]
+    blocks = 2 * pairs
     count = red_ref.shape[0] // 2
     per = 128 // blocks
-
-    @pl.when(step == 0)
-    def _():
-        coherent = all_ref[:, count, :]
-        power = all_ref[:, count + 1, :]
-        scale_n, scale_d = patch_scales(total_tx, cot_ref, ids_ref[...] // PP, coherent, power)
-        common = coherent * scale_n
-        for t in range(count):
-            bg_ref[t] = common + all_ref[:, t, :] * scale_d
-        for half in range(count // per):
-            stack = [bg_ref[half * per + i] for i in range(per)]
-            bg_lane_ref[:, half * 128 : (half + 1) * 128] = jnp.concatenate(stack, axis=0).T
-        acc = jnp.zeros((cells, PB), F32)
-        me = lax.axis_index("rx")
-        for t in range(count):
-            own = bg_ref[t, pl.ds(me, 1), :] * red_ref[count + t : count + t + 1, :]
-            acc = acc + tx_path_ref[t].astype(F32) * own
-        acc_ref[...] = acc
-
-    acc = [acc_ref[...], jnp.zeros((cells, PB), F32)]
-    for r in range(rows):
-        grad = None
-        for half in range(count // per):
-            lanes = slice(half * 128, (half + 1) * 128)
-            term = slope_ref[r, :, lanes] * bg_lane_ref[:, lanes]
-            grad = term if grad is None else grad + term
-        grad = grad.T
-        total = grad[0:blocks]
-        for i in range(1, per):
-            total = total + grad[i * blocks : (i + 1) * blocks]
-        grad_ref[r] = total
-        for k in range(blocks):
-            paths = path_ref[r, :, k * PB : (k + 1) * PB].astype(F32)
-            acc[k % 2] = acc[k % 2] + paths * grad_ref[r, k : k + 1, :]
-    acc = acc[0] + acc[1]
-    acc_ref[...] = acc
-
-    @pl.when(step == pl.num_programs(0) - 1)
-    def _():
-        ones = jnp.ones((8, PB), F32)
-        row = lax.dot_general(
-            ones,
-            acc,
-            (((1,), (1,)), ((), ())),
-            precision=lax.Precision.HIGHEST,
-            preferred_element_type=F32,
-        )
-        row = jnp.concatenate([row] * (PB // cells), axis=1)
-        out_ref[...] = jnp.broadcast_to(row[0:1, :], out_ref.shape)
+    together = grad_ref.shape[0]
+    me = lax.axis_index("rx")
+
+    for row in range(count + 2):
+        here = here_ref[:, row, :]
+        there = there_ref[:, row, :]
+        all_ref[row, pl.ds(0, pairs, stride=2), :] = jnp.where(me % 2 == 0, here, there)
+        all_ref[row, pl.ds(1, pairs, stride=2), :] = jnp.where(me % 2 == 0, there, here)
+    coherent = all_ref[count]
+    power = all_ref[count + 1]
+    scale_n, scale_d = patch_scales(total_tx, cot_ref, ids_ref[...] // PP, coherent, power)
+    common = coherent * scale_n
+    for t in range(count):
+        bg_ref[t] = common + all_ref[t] * scale_d
+    for half in range(count // per):
+        stack = [bg_ref[half * per + i] for i in range(per)]
+        bg_lane_ref[:, half * 128 : (half + 1) * 128] = jnp.concatenate(stack, axis=0).T
+    start = jnp.zeros((cells, PB), F32)
+    for t in range(count):
+        own = bg_ref[t, pl.ds(me, 1), :] * red_ref[count + t : count + t + 1, :]
+        start = start + tx_path_ref[t].astype(F32) * own
+
+    def receivers(step, acc):
+        acc = list(acc)
+        for i in range(together):
+            r = step * together + i
+            grad = None
+            for half in range(count // per):
+                lanes = slice(half * 128, (half + 1) * 128)
+                term = slope_ref[r, :, lanes] * bg_lane_ref[:, lanes]
+                grad = term if grad is None else grad + term
+            grad = grad.T
+            total = grad[0:blocks]
+            for group in range(1, per):
+                total = total + grad[group * blocks : (group + 1) * blocks]
+            grad_ref[i] = total
+            for k in range(blocks):
+                paths = path_ref[r, :, k * PB : (k + 1) * PB].astype(F32)
+                acc[k % 2] = acc[k % 2] + paths * grad_ref[i, k : k + 1, :]
+        return tuple(acc)
+
+    acc = lax.fori_loop(0, rows // together, receivers, (start, jnp.zeros_like(start)))
+    row = lax.dot_general(
+        jnp.ones((8, PB), F32),
+        acc[0] + acc[1],
+        (((1,), (1,)), ((), ())),
+        precision=lax.Precision.HIGHEST,
+        preferred_element_type=F32,
+    )
+    row = jnp.concatenate([row] * (PB // cells), axis=1)
+    out_ref[...] = jnp.broadcast_to(row[0:1, :], out_ref.shape)
 
 
 def params(megabytes):
@@ -321,50 +350,52 @@
     )(in_hbm(s_row), in_hbm(rx_paths), in_hbm(traces), in_hbm(tap_start))
 
 
-def focus(tx_delay, rx_delay, window):
+def focus(tx_delay, rx_delay, window, rx_paths):
     blocks, tx_count, _ = tx_delay.shape
     rx_count = rx_delay.shape[0]
     lanes = tx_count * blocks
+    vmem = pl.BlockSpec(memory_space=pltpu.VMEM)
     return pl.pallas_call(
         focus_kernel,
-        out_shape=[shaped(rx_count, PB, lanes), shaped(blocks, 2 * tx_count, PB)],
-        scratch_shapes=[pltpu.VMEM((PB, lanes), F32)] * 3,
-        compiler_params=params(12),
+        in_specs=[vmem, vmem, vmem, pl.BlockSpec(memory_space=pl.ANY)],
+        out_specs=[vmem] * 4,
+        out_shape=[
+            shaped(rx_count, PB, lanes),
+            shaped(blocks // 2, 2 * tx_count, PB),
+            shaped(blocks // 2, 2 * tx_count, PB),
+            jax.ShapeDtypeStruct(rx_paths.shape, rx_paths.dtype),
+        ],
+        scratch_shapes=[pltpu.VMEM((PB, lanes), F32)] * 3
+        + [pltpu.VMEM((128, PB), F32), pltpu.SemaphoreType.DMA],
+        compiler_params=params(20),
         name="focus",
-    )(tx_delay, rx_delay, window)
-
-
-def gradient(total_tx, parts, patch_cotangent, every, pixel_order, red, tx_paths, slope, rx_paths):
-    rx_count, cells, pixels = rx_paths.shape
-    blocks = pixels // PB
+    )(tx_delay, rx_delay, window, in_hbm(rx_paths))
+
+
+def gradient(total_tx, parts, patch_cotangent, here, there, pixel_order, red, tx_paths, slope, rx_paths):
+    rx_count = rx_paths.shape[0]
+    blocks = 2 * here.shape[0]
     tx_count = tx_paths.shape[0]
     lanes = tx_count * blocks
-    rows = 4
+    together = 4
+    vmem = pl.BlockSpec(memory_space=pltpu.VMEM)
     return pl.pallas_call(
         lambda *refs: gradient_kernel(total_tx, *refs),
-        grid=(rx_count // rows,),
-        in_specs=[
-            pl.BlockSpec(memory_space=pltpu.SMEM),
-            whole(every.shape),
-            whole((blocks, PB)),
-            whole(red.shape),
-            whole(tx_paths.shape),
-            pl.BlockSpec((rows, PB, lanes), lambda i: (i, 0, 0)),
-            pl.BlockSpec((rows, cells, pixels), lambda i: (i, 0, 0)),
-        ],
-        out_specs=whole((parts, PB)),
+        in_specs=[pl.BlockSpec(memory_space=pltpu.SMEM)] + [vmem] * 7,
+        out_specs=vmem,
         out_shape=shaped(parts, PB),
         scratch_shapes=[
+            pltpu.VMEM((tx_count + 2, blocks, PB), F32),
             pltpu.VMEM((tx_count, blocks, PB), F32),
             pltpu.VMEM((PB, lanes), F32),
-            pltpu.VMEM((rows, blocks, PB), F32),
-            pltpu.VMEM((cells, PB), F32),
+            pltpu.VMEM((together, blocks, PB), F32),
         ],
-        compiler_params=params(12),
+        compiler_params=params(20),
         name="gradient",
     )(
         patch_cotangent,
-        every,
+        here,
+        there,
         pixel_order.reshape(blocks, PB),
         red,
         tx_paths,
@@ -377,13 +408,26 @@
     tx_count, cells, _ = tx_paths.shape
     tx_size = lax.axis_size("tx")
     rx_size = lax.axis_size("rx")
+    pairs = rx_size // 2
     s_row = slowness.reshape(1, cells)
+    partner = [(i, i ^ 1) for i in range(rx_size)]
+    same_core = [list(range(core, rx_size, 2)) for core in range(2)]
+
+    def between_chips(array):
+        return lax.all_to_all(array, "rx", 0, 0, axis_index_groups=same_core)
 
     delay = tx_delays(s_row, tx_paths, rx_size)
     rx_delay, window = prepare(s_row, rx_paths, traces, tap_start)
     tx_delay = lax.all_to_all(delay, "rx", 0, 0)
-    slope, part = focus(tx_delay, rx_delay, window)
-    part = lax.all_to_all(part, "rx", 0, 0)
+    slope, keep, give, path_copy = focus(tx_delay, rx_delay, window, rx_paths)
+    got = lax.ppermute(give, "rx", partner)
+    part = pl.pallas_call(
+        pair_sum_kernel,
+        out_shape=shaped(*keep.shape),
+        compiler_params=params(4),
+        name="sum_cores",
+    )(keep, got)
+    part = between_chips(part)
     red, pair = pl.pallas_call(
         gather_sum_kernel,
         out_shape=[shaped(2 * tx_count, PB), shaped(tx_size, 2, PB)],
@@ -393,21 +437,23 @@
     pair = lax.all_to_all(pair, "tx", 0, 0)
     spread = pl.pallas_call(
         spread_kernel,
-        out_shape=shaped(rx_size, tx_count + 2, PB),
+        out_shape=shaped(pairs, tx_count + 2, PB),
         compiler_params=params(4),
         name="sum_transmits",
     )(pair, red)
-    every = lax.all_to_all(spread, "rx", 0, 0)
+    here = between_chips(spread)
+    there = lax.ppermute(here, "rx", partner)
     share = gradient(
         tx_count * tx_size,
         tx_size * rx_size,
         patch_cotangent,
-        every,
+        here,
+        there,
         pixel_order,
         red,
         tx_paths,
         slope,
-        rx_paths,
+        path_copy,
     )
     share = lax.all_to_all(share, ("tx", "rx"), 0, 0, tiled=True)
     return share.sum(0)[:cells]

time: 103 us -> 95.9 us (0.931)
  blocking collectives: 66.3 us -> 56.7 us
  starting transfers between devices: 10 us -> 14.2 us
  local copies, waits for them, and re-layouts: 3.4 us -> 0.02 us
  waiting for transfers between devices: 3.15 us -> 5.13 us
    all_to_all x2, blocking collectives: 31.7 us -> 21.9 us  [between_chips(): return lax.all_to_all(array, 'rx', 0, 0, axis_index_groups=same_core)]
    ppermute x0 -> x2, starting transfers between devices: none -> 4.18 us  [the longest x1 3.7 us: on_device(): there = lax.ppermute(here, 'rx', partner)]
    unnamed x8 -> x6, local copies, waits for them, and re-layouts: 3.4 us -> 0.02 us
    ppermute x0 -> x2, waiting for transfers between devices: none -> 1.97 us  [the longest x1 0.99 us: on_device(): got = lax.ppermute(give, 'rx', partner)]
    pallas_call x3 -> x4, Pallas kernels: 11.4 us -> 11.4 us  [the longest x1 7.45 us: focus(): pl.pallas_call(focus_kernel, in_specs=[vmem, vmem, vmem, pl.BlockSpec(mem...]
  transfers between devices with their start and end apart: 1 -> 3, of which waited for: 1 -> 3; matrix products, arithmetic and copies ran while one was open for 0% -> 0% of each run, Pallas kernels for 5% -> 6%
where the time goes in v4:
time: 95.9 us; the launch traced here: 95.6 us
  blocking collectives  56.7 us (59%)
  Pallas kernels  18.7 us (19%)
  starting transfers between devices  14.2 us (15%)
  waiting for transfers between devices  5.13 us (5%)
    all_to_all x2, blocking collectives, between_chips(): return lax.all_to_all(array, 'rx', 0, 0, axis_index_groups=same_core)  21.9 us
    all_to_all x1, blocking collectives, on_device(): share = lax.all_to_all(share, ('tx', 'rx'), 0, 0, tiled=True)  18 us
    all_to_all x1, blocking collectives, on_device(): pair = lax.all_to_all(pair, 'tx', 0, 0)  16.9 us
    all_to_all x1, starting transfers between devices, on_device(): tx_delay = lax.all_to_all(delay, 'rx', 0, 0)  10 us
    pallas_call x1, Pallas kernels, focus(): pl.pallas_call(focus_kernel, in_specs=[vmem, vmem, vmem, pl.BlockSpec(mem...  7.45 us
    pallas_call x1, Pallas kernels, prepare(): pl.pallas_call(prepare_kernel, grid=(rx_count // rows,), in_specs=[whole(...  5.51 us
    pallas_call x1, Pallas kernels, gradient(): pl.pallas_call(lambda *refs: gradient_kernel(total_tx, *refs), in_specs=[...  3.94 us
    ppermute x1, starting transfers between devices, on_device(): there = lax.ppermute(here, 'rx', partner)  3.7 us
  transfers between devices with their start and end apart: 3, of which 3 were waited for; matrix products, arithmetic and copies ran while one was open for 0% of the time, Pallas kernels for 6%

profile of v4, /device:TPU:1, one launch (start us, length us, event | category | flops | bytes accessed | tf_op | source)
XLA Modules:
  0.0 95.6 jit_solution(13086038745215132046)
XLA Ops:
  0.0 1.7 %tx_delay.1 = f32[32,8,128]{2,1,0:T(8,128)} custom-call(bf16[1,32]{1,0:T(2,128)(2,1)} %bitcast.8, bf16[8,32,128]{2,1,0:T(8,128)(2,1)} %refs_5_.1), custom_call_target="tpu_custom_call" | custom-call | tf_op jit(solution)/shard_map/tx_delay/pallas_call | solution.py:317
  1.7 10.0 %all-to-all-start = ((f32[32,8,128]{2,1,0:T(8,128)}), f32[32,8,128]{2,1,0:T(8,128)S(1)}, u32[]{:S(2)}, u32[]{:S(2)}) async-start(f32[32,8,128]{2,1,0:T(8,128)} %tx_delay.1), calls=%async_computation | async-start | bytes 262144 | tf_op jit(solution)/shard_map/all_to_all | solution.py:421
  11.7 0.0 copy-start
  11.7 0.0 copy-start.1
  11.8 0.0 copy-start.2
  11.8 5.5 %prepare.1 = (f32[32,128,128]{2,1,0:T(8,128)S(1)}, f32[32,8,256]{2,1,0:T(8,128)S(1)}) custom-call(bf16[1,32]{1,0:T(2,128)(2,1)} %bitcast.9, bf16[32,32,4096]{2,1,0:T(8,128)(2,1)} %path_ref.5, bf16[8,32,512]{2,1,0:T(8,128)(2,1)} %trace_ref.1, s32[8,32,32]{2,1,0:T(8,128)} %start_ref.1), custom_call_target="tpu_custom_call" | custom-call | tf_op jit(solution)/shard_map/prepare/pallas_call | solution.py:330
  17.3 3.2 %all-to-all-done.tx_ref = f32[32,8,128]{2,1,0:T(8,128)S(1)} async-done(((f32[32,8,128]{2,1,0:T(8,128)}), f32[32,8,128]{2,1,0:T(8,128)S(1)}, u32[]{:S(2)}, u32[]{:S(2)}) %all-to-all-start) | async-done | bytes 131104 | tf_op jit(solution)/shard_map/all_to_all | solution.py:421
  20.4 7.4 %focus.1 = (f32[32,128,256]{2,1,0:T(8,128)S(1)}, f32[16,16,128]{2,1,0:T(8,128)S(1)}, f32[16,16,128]{2,1,0:T(8,128)S(1)}, bf16[32,32,4096]{2,1,0:T(8,128)(2,1)S(1)}) custom-call(f32[32,8,128]{2,1,0:T(8,128)S(1)} %all-to-all-done.tx_ref, f32[32,128,128]{2,1,0:T(8,128)S(1)} %get-tuple-element.13.rx_ref, f32[32,8,256]{2,1,0:T(8,128)S(1)} %get-tuple-element.14.win_ref, ...), custom_call_target="tpu_custom_call" | custom-call | tf_op jit(solution)/shard_map/focus/pallas_call | solution.py:358
  27.9 0.5 collective-permute-start
  28.4 1.0 %collective-permute-done.got_ref = f32[16,16,128]{2,1,0:T(8,128)S(1)} collective-permute-done((f32[16,16,128]{2,1,0:T(8,128)S(1)}, f32[16,16,128]{2,1,0:T(8,128)S(1)}, u32[]{:S(2)}, u32[]{:S(2)}) %collective-permute-start) | collective-permute-done | bytes 131104 | tf_op jit(solution)/shard_map/ppermute | solution.py:423
  29.4 10.9 %all_to_all.29.part_ref = f32[16,16,128]{2,1,0:T(8,128)S(1)} all-to-all(f32[16,16,128]{2,1,0:T(8,128)S(1)} %sum_cores.1), channel_id=1, replica_groups={{0,2,4,6,8,10,12,14,16,18,20,22,24,26,28,30},{1,3,5,7,9,11,13,15,17,19,..., dimensions={0} | all-to-all | bytes 262144 | tf_op jit(solution)/shard_map/all_to_all | solution.py:417
  40.3 16.9 %all_to_all.30.pair_ref = f32[8,2,128]{2,1,0:T(2,128)S(1)} all-to-all(f32[8,2,128]{2,1,0:T(2,128)S(1)} %get-tuple-element.17), channel_id=1, replica_groups=mesh['tx'=8,'rx'=32] {'tx'}, dimensions={0} | all-to-all | bytes 16384 | tf_op jit(solution)/shard_map/all_to_all | solution.py:437
  57.2 11.0 %all_to_all.31.refs_1_ = f32[16,10,128]{2,1,0:T(8,128)S(1)} all-to-all(f32[16,10,128]{2,1,0:T(8,128)S(1)} %sum_transmits.1), channel_id=1, replica_groups={{0,2,4,6,8,10,12,14,16,18,20,22,24,26,28,30},{1,3,5,7,9,11,13,15,17,19,..., dimensions={0} | all-to-all | bytes 163840 | tf_op jit(solution)/shard_map/all_to_all | solution.py:417
  68.1 3.7 %collective-permute-start.1 = (f32[16,10,128]{2,1,0:T(8,128)S(1)}, f32[16,10,128]{2,1,0:T(8,128)S(1)}, u32[]{:S(2)}, u32[]{:S(2)}) collective-permute-start(f32[16,10,128]{2,1,0:T(8,128)S(1)} %all_to_all.31.refs_1_), channel_id=1, source_target_pairs={{0,1},{1,0},{2,3},{3,2},{4,5},{5,4},{6,7},{7,6},{8,9},{9,8},{10,11... | collective-permute-start | bytes 245768 | tf_op jit(solution)/shard_map/ppermute | solution.py:445
  71.9 1.0 %collective-permute-done.1.refs_2_ = f32[16,10,128]{2,1,0:T(8,128)S(1)} collective-permute-done((f32[16,10,128]{2,1,0:T(8,128)S(1)}, f32[16,10,128]{2,1,0:T(8,128)S(1)}, u32[]{:S(2)}, u32[]{:S(2)}) %collective-permute-start.1) | collective-permute-done | bytes 81952 | tf_op jit(solution)/shard_map/ppermute | solution.py:445
  72.8 0.0 copy-done
  72.8 0.0 copy-done.1
  72.8 0.0 copy-done.2
  72.8 3.9 %gradient.1 = f32[256,128]{1,0:T(8,128)S(1)} custom-call(f32[16]{0:T(128)S(1)} %copy-done.2, f32[16,10,128]{2,1,0:T(8,128)S(1)} %all_to_all.31.refs_1_, f32[16,10,128]{2,1,0:T(8,128)S(1)} %collective-permute-done.1.refs_2_, s32[32,128]{1,0:T(8,128)S(1)} %bitcast.7, f32[16,128]{1,0:T(8,128)S(1)} %get-tuple-element.18.red_ref.refs_4_, ...), custom_call_target="tpu_custom_call" | custom-call | tf_op jit(solution)/shard_map/gradient/pallas_call | solution.py:382
  76.8 18.0 %all_to_all.32 = f32[256,1,128]{2,1,0:T(1,128)S(1)} all-to-all(f32[256,1,128]{2,1,0:T(1,128)S(1)} %bitcast.6), channel_id=1, replica_groups=mesh['tx'=8,'rx'=32] {'tx','rx'}, dimensions={0} | all-to-all | bytes 262144 | tf_op jit(solution)/shard_map/all_to_all | solution.py:458
  94.8 0.8 reduce_sum.9
  (3 shorter events, 0.1 us)
Async XLA Ops:
  1.7 18.7 %all-to-all-start = ((f32[32,8,128]{2,1,0:T(8,128)}), f32[32,8,128]{2,1,0:T(8,128)S(1)}, u32[]{:S(2)}, u32[]{:S(2)}) async-start(f32[32,8,128]{2,1,0:T(8,128)} %tx_delay.1), calls=%async_computation | async-start | bytes 262144 | tf_op jit(solution)/shard_map/all_to_all | solution.py:421
  11.7 61.1 %copy-start = (bf16[8,32,128]{2,1,0:T(8,128)(2,1)S(1)}, bf16[8,32,128]{2,1,0:T(8,128)(2,1)}, u32[]{:S(2)}) copy-start(bf16[8,32,128]{2,1,0:T(8,128)(2,1)} %refs_5_.1) | copy-start | bytes 196612
  11.7 61.1 %copy-start.1 = (s32[4096]{0:T(1024)S(1)}, s32[4096]{0:T(1024)}, u32[]{:S(2)}) copy-start(s32[4096]{0:T(1024)} %param.12) | copy-start | bytes 49156
  11.8 61.1 %copy-start.2 = (f32[16]{0:T(128)S(1)}, f32[16]{0:T(128)}, u32[]{:S(2)}) copy-start(f32[16]{0:T(128)} %refs_0_.1) | copy-start | bytes 196
  27.9 1.5 %collective-permute-start = (f32[16,16,128]{2,1,0:T(8,128)S(1)}, f32[16,16,128]{2,1,0:T(8,128)S(1)}, u32[]{:S(2)}, u32[]{:S(2)}) collective-permute-start(f32[16,16,128]{2,1,0:T(8,128)S(1)} %get-tuple-element.16), channel_id=1, source_target_pairs={{0,1},{1,0},{2,3},{3,2},{4,5},{5,4},{6,7},{7,6},{8,9},{9,8},{10,11... | collective-permute-start | bytes 393224 | tf_op jit(solution)/shard_map/ppermute | solution.py:423
  68.1 4.7 %collective-permute-start.1 = (f32[16,10,128]{2,1,0:T(8,128)S(1)}, f32[16,10,128]{2,1,0:T(8,128)S(1)}, u32[]{:S(2)}, u32[]{:S(2)}) collective-permute-start(f32[16,10,128]{2,1,0:T(8,128)S(1)} %all_to_all.31.refs_1_), channel_id=1, source_target_pairs={{0,1},{1,0},{2,3},{3,2},{4,5},{5,4},{6,7},{7,6},{8,9},{9,8},{10,11... | collective-permute-start | bytes 245768 | tf_op jit(solution)/shard_map/ppermute | solution.py:445

commit v5 on v4

--- a/solution.py
+++ b/solution.py
@@ -24,7 +24,15 @@
     return jnp.where(mine, jnp.broadcast_to(wide, shape), 0.0).astype(jnp.bfloat16)
 
 
-def tx_delay_kernel(s_ref, path_ref, out_ref):
+def tx_delay_kernel(s_hbm, path_hbm, out_ref, s_ref, path_ref, copied):
+    fetches = [
+        pltpu.make_async_copy(s_hbm, s_ref, copied.at[0]),
+        pltpu.make_async_copy(path_hbm, path_ref, copied.at[1]),
+    ]
+    for fetch in fetches:
+        fetch.start()
+    for fetch in fetches:
+        fetch.wait()
     rows, cells, width = path_ref.shape
     left = block_diagonal(s_ref[...].astype(F32), rows, cells)
     delay = jnp.dot(
@@ -137,22 +145,31 @@
         slope = gauss * (gauss * (change + (m + m) * both))
         return focused, slope
 
-    def receiver(r, carry):
+    def receivers(step, carry):
         for half in range(halves):
             lanes = slice(half * 128, (half + 1) * 128)
-            tap = [
-                jnp.broadcast_to(win_ref[r, j : j + 1, lanes], (8, 128)) for j in range(W)
+            taps = [
+                [
+                    jnp.broadcast_to(win_ref[2 * step + i, j : j + 1, lanes], (8, 128))
+                    for j in range(W)
+                ]
+                for i in range(2)
             ]
             for first in range(0, PB, 8):
                 here = slice(first, first + 8)
-                h = tx_lane_ref[here, lanes] + rx_ref[r, here, :]
-                focused, slope = point(tap, h)
-                slope_ref[r, here, lanes] = slope
-                total_f_ref[here, lanes] += focused
-                total_s_ref[here, lanes] += slope
+                total_f = total_f_ref[here, lanes]
+                total_s = total_s_ref[here, lanes]
+                for i in range(2):
+                    h = tx_lane_ref[here, lanes] + rx_ref[2 * step + i, here, :]
+                    focused, slope = point(taps[i], h)
+                    slope_ref[2 * step + i, here, lanes] = slope
+                    total_f = total_f + focused
+                    total_s = total_s + slope
+                total_f_ref[here, lanes] = total_f
+                total_s_ref[here, lanes] = total_s
         return carry
 
-    lax.fori_loop(0, rows, receiver, 0)
+    lax.fori_loop(0, rows // 2, receivers, 0)
     mine = lax.axis_index("rx") % 2
     for source, base in ((total_f_ref, 0), (total_s_ref, count)):
         for half in range(halves):
@@ -170,29 +187,48 @@
     out_ref[...] = keep_ref[...] + got_ref[...]
 
 
-def gather_sum_kernel(part_ref, red_ref, rep_ref):
+def gather_sum_kernel(part_ref, beam_ref, slope_ref):
     total = part_ref[0]
     for i in range(1, part_ref.shape[0]):
         total = total + part_ref[i]
-    red_ref[...] = total
-    beam = total[0 : total.shape[0] // 2]
-    coherent = jnp.sum(beam, axis=0, keepdims=True)
-    power = jnp.sum(beam * beam, axis=0, keepdims=True)
-    pair = jnp.concatenate([coherent, power], axis=0)
-    rep_ref[...] = jnp.broadcast_to(pair[None], rep_ref.shape)
-
-
-def spread_kernel(pair_ref, red_ref, out_ref):
-    pair = pair_ref[0]
+    count = beam_ref.shape[0]
+    beam_ref[...] = total[0:count]
+    slope_ref[...] = total[count : 2 * count]
+
+
+def square_kernel(here_ref, there_ref, out_ref):
+    rows = []
+    for ref in (here_ref, there_ref):
+        beam = ref[...]
+        rows.append(jnp.sum(beam, axis=0, keepdims=True))
+        rows.append(jnp.sum(beam * beam, axis=0, keepdims=True))
+    out_ref[...] = jnp.broadcast_to(jnp.concatenate(rows, axis=0)[None], out_ref.shape)
+
+
+def spread_kernel(pair_ref, here_ref, there_ref, out_ref):
+    even_core = lax.axis_index("rx") % 2 == 0
+    total = pair_ref[0]
     for i in range(1, pair_ref.shape[0]):
-        pair = pair + pair_ref[i]
-    count = red_ref.shape[0] // 2
-    out_ref[:, 0:count, :] = jnp.broadcast_to(
-        red_ref[0:count, :][None], (out_ref.shape[0], count, PB)
-    )
-    out_ref[:, count : count + 2, :] = jnp.broadcast_to(
-        pair[None], (out_ref.shape[0], 2, PB)
-    )
+        total = total + pair_ref[i]
+    even = jnp.where(even_core, total[0:2], total[2:4])
+    odd = jnp.where(even_core, total[2:4], total[0:2])
+    here = here_ref[...]
+    there = there_ref[...]
+    fields = [
+        jnp.where(even_core, here, there),
+        jnp.where(even_core, there, here),
+        jnp.concatenate([even, odd], axis=0),
+    ]
+    group = 0
+    for field in fields:
+        for first in range(0, field.shape[0], 4):
+            block = field[first : first + 4]
+            out_ref[:, group] = jnp.broadcast_to(block[None], (out_ref.shape[0], 4, PB))
+            group += 1
+
+
+def total_kernel(share_ref, out_ref):
+    out_ref[...] = jnp.sum(share_ref[...], axis=0)[0 : out_ref.shape[0]]
 
 
 def patch_scales(total_tx, cot_ref, ids, coherent, power):
@@ -225,10 +261,9 @@
 def gradient_kernel(
     total_tx,
     cot_ref,
-    here_ref,
-    there_ref,
+    every_ref,
     ids_ref,
-    red_ref,
+    slope_sum_ref,
     tx_path_ref,
     slope_ref,
     path_ref,
@@ -239,18 +274,18 @@
     grad_ref,
 ):
     rows, cells, _ = path_ref.shape
-    pairs = here_ref.shape[0]
+    pairs = every_ref.shape[0]
     blocks = 2 * pairs
-    count = red_ref.shape[0] // 2
+    count = slope_sum_ref.shape[0]
     per = 128 // blocks
     together = grad_ref.shape[0]
     me = lax.axis_index("rx")
 
     for row in range(count + 2):
-        here = here_ref[:, row, :]
-        there = there_ref[:, row, :]
-        all_ref[row, pl.ds(0, pairs, stride=2), :] = jnp.where(me % 2 == 0, here, there)
-        all_ref[row, pl.ds(1, pairs, stride=2), :] = jnp.where(me % 2 == 0, there, here)
+        for parity in range(2):
+            place = parity * count + row if row < count else count + parity * 2 + row
+            source = every_ref[:, place // 4, place % 4, :]
+            all_ref[row, pl.ds(parity, pairs, stride=2), :] = source
     coherent = all_ref[count]
     power = all_ref[count + 1]
     scale_n, scale_d = patch_scales(total_tx, cot_ref, ids_ref[...] // PP, coherent, power)
@@ -262,7 +297,7 @@
         bg_lane_ref[:, half * 128 : (half + 1) * 128] = jnp.concatenate(stack, axis=0).T
     start = jnp.zeros((cells, PB), F32)
     for t in range(count):
-        own = bg_ref[t, pl.ds(me, 1), :] * red_ref[count + t : count + t + 1, :]
+        own = bg_ref[t, pl.ds(me, 1), :] * slope_sum_ref[t : t + 1, :]
         start = start + tx_path_ref[t].astype(F32) * own
 
     def receivers(step, acc):
@@ -285,15 +320,9 @@
         return tuple(acc)
 
     acc = lax.fori_loop(0, rows // together, receivers, (start, jnp.zeros_like(start)))
-    row = lax.dot_general(
-        jnp.ones((8, PB), F32),
-        acc[0] + acc[1],
-        (((1,), (1,)), ((), ())),
-        precision=lax.Precision.HIGHEST,
-        preferred_element_type=F32,
-    )
+    row = jnp.sum((acc[0] + acc[1]).T, axis=0, keepdims=True)
     row = jnp.concatenate([row] * (PB // cells), axis=1)
-    out_ref[...] = jnp.broadcast_to(row[0:1, :], out_ref.shape)
+    out_ref[...] = jnp.broadcast_to(row, out_ref.shape)
 
 
 def params(megabytes):
@@ -316,7 +345,13 @@
     tx_count, _, own_pixels = tx_paths.shape
     return pl.pallas_call(
         tx_delay_kernel,
+        in_specs=[pl.BlockSpec(memory_space=pl.ANY)] * 2,
         out_shape=shaped(rx_size, tx_count, own_pixels),
+        scratch_shapes=[
+            pltpu.VMEM(s_row.shape, s_row.dtype),
+            pltpu.VMEM(tx_paths.shape, tx_paths.dtype),
+            pltpu.SemaphoreType.DMA((2,)),
+        ],
         compiler_params=params(4),
         name="tx_delay",
     )(in_hbm(s_row), in_hbm(tx_paths))
@@ -372,16 +407,16 @@
     )(tx_delay, rx_delay, window, in_hbm(rx_paths))
 
 
-def gradient(total_tx, parts, patch_cotangent, here, there, pixel_order, red, tx_paths, slope, rx_paths):
+def gradient(total_tx, parts, patch_cotangent, every, pixel_order, slope_sum, tx_paths, slope, rx_paths):
     rx_count = rx_paths.shape[0]
-    blocks = 2 * here.shape[0]
+    blocks = 2 * every.shape[0]
     tx_count = tx_paths.shape[0]
     lanes = tx_count * blocks
-    together = 4
+    together = 8
     vmem = pl.BlockSpec(memory_space=pltpu.VMEM)
     return pl.pallas_call(
         lambda *refs: gradient_kernel(total_tx, *refs),
-        in_specs=[pl.BlockSpec(memory_space=pltpu.SMEM)] + [vmem] * 7,
+        in_specs=[pl.BlockSpec(memory_space=pltpu.SMEM)] + [vmem] * 6,
         out_specs=vmem,
         out_shape=shaped(parts, PB),
         scratch_shapes=[
@@ -394,10 +429,9 @@
         name="gradient",
     )(
         patch_cotangent,
-        here,
-        there,
+        every,
         pixel_order.reshape(blocks, PB),
-        red,
+        slope_sum,
         tx_paths,
         slope,
         rx_paths,
@@ -428,35 +462,45 @@
         name="sum_cores",
     )(keep, got)
     part = between_chips(part)
-    red, pair = pl.pallas_call(
+    beam, slope_sum = pl.pallas_call(
         gather_sum_kernel,
-        out_shape=[shaped(2 * tx_count, PB), shaped(tx_size, 2, PB)],
+        out_shape=[shaped(tx_count, PB), shaped(tx_count, PB)],
         compiler_params=params(4),
         name="sum_receivers",
     )(part)
+    other = lax.ppermute(beam, "rx", partner)
+    pair = pl.pallas_call(
+        square_kernel,
+        out_shape=shaped(tx_size, 4, PB),
+        compiler_params=params(4),
+        name="squares",
+    )(beam, other)
     pair = lax.all_to_all(pair, "tx", 0, 0)
     spread = pl.pallas_call(
         spread_kernel,
-        out_shape=shaped(pairs, tx_count + 2, PB),
+        out_shape=shaped(pairs, (2 * tx_count + 4) // 4, 4, PB),
         compiler_params=params(4),
         name="sum_transmits",
-    )(pair, red)
-    here = between_chips(spread)
-    there = lax.ppermute(here, "rx", partner)
+    )(pair, beam, other)
+    every = between_chips(spread)
     share = gradient(
         tx_count * tx_size,
         tx_size * rx_size,
         patch_cotangent,
-        here,
-        there,
+        every,
         pixel_order,
-        red,
+        slope_sum,
         tx_paths,
         slope,
         path_copy,
     )
     share = lax.all_to_all(share, ("tx", "rx"), 0, 0, tiled=True)
-    return share.sum(0)[:cells]
+    return pl.pallas_call(
+        total_kernel,
+        out_shape=shaped(cells),
+        compiler_params=params(4),
+        name="total",
+    )(share)
 
 
 def solution(mesh):

time: 95.9 us -> 95.2 us (level)
  blocking collectives: 56.7 us -> 58.7 us
  starting transfers between devices: 14.2 us -> 12.5 us
    all_to_all x1, blocking collectives: 18 us -> 20.8 us  [on_device(): share = lax.all_to_all(share, ('tx', 'rx'), 0, 0, tiled=True)]
    ppermute x1, starting transfers between devices: 3.7 us -> 1.97 us  [on_device(): other = lax.ppermute(beam, 'rx', partner)]
    pallas_call x3 -> x5, Pallas kernels: 1.75 us -> 2.32 us  [the longest x1 1.72 us: tx_delays(): pl.pallas_call(tx_delay_kernel, in_specs=[pl.BlockSpec(memory_space=pl.AN...]
where the time goes in v5:
time: 95.2 us; the launch traced here: 94.8 us
  blocking collectives  58.7 us (62%)
  Pallas kernels  18.6 us (20%)
  starting transfers between devices  12.5 us (13%)
  waiting for transfers between devices  4.96 us (5%)
    all_to_all x2, blocking collectives, between_chips(): return lax.all_to_all(array, 'rx', 0, 0, axis_index_groups=same_core)  20.9 us
    all_to_all x1, blocking collectives, on_device(): share = lax.all_to_all(share, ('tx', 'rx'), 0, 0, tiled=True)  20.8 us
    all_to_all x1, blocking collectives, on_device(): pair = lax.all_to_all(pair, 'tx', 0, 0)  16.9 us
    all_to_all x1, starting transfers between devices, on_device(): tx_delay = lax.all_to_all(delay, 'rx', 0, 0)  10 us
    pallas_call x1, Pallas kernels, focus(): pl.pallas_call(focus_kernel, in_specs=[vmem, vmem, vmem, pl.BlockSpec(mem...  7.14 us
    pallas_call x1, Pallas kernels, prepare(): pl.pallas_call(prepare_kernel, grid=(rx_count // rows,), in_specs=[whole(...  5.51 us
    pallas_call x1, Pallas kernels, gradient(): pl.pallas_call(lambda *refs: gradient_kernel(total_tx, *refs), in_specs=[...  3.59 us
    all_to_all x1, waiting for transfers between devices, on_device(): tx_delay = lax.all_to_all(delay, 'rx', 0, 0)  3.15 us
  transfers between devices with their start and end apart: 3, of which 3 were waited for; matrix products, arithmetic and copies ran while one was open for 0% of the time, Pallas kernels for 6%

profile of v5, /device:TPU:1, one launch (start us, length us, event | category | flops | bytes accessed | tf_op | source)
XLA Modules:
  0.0 94.8 jit_solution(12950090646202827458)
XLA Ops:
  0.0 1.7 %tx_delay.1 = f32[32,8,128]{2,1,0:T(8,128)} custom-call(bf16[1,32]{1,0:T(2,128)(2,1)} %bitcast.9, bf16[8,32,128]{2,1,0:T(8,128)(2,1)} %refs_4_.1), custom_call_target="tpu_custom_call" | custom-call | tf_op jit(solution)/shard_map/tx_delay/pallas_call | solution.py:346
  1.7 10.0 %all-to-all-start = ((f32[32,8,128]{2,1,0:T(8,128)}), f32[32,8,128]{2,1,0:T(8,128)S(1)}, u32[]{:S(2)}, u32[]{:S(2)}) async-start(f32[32,8,128]{2,1,0:T(8,128)} %tx_delay.1), calls=%async_computation | async-start | bytes 262144 | tf_op jit(solution)/shard_map/all_to_all | solution.py:455
  11.8 0.0 copy-start
  11.8 0.0 copy-start.1
  11.8 0.0 copy-start.2
  11.8 5.5 %prepare.1 = (f32[32,128,128]{2,1,0:T(8,128)S(1)}, f32[32,8,256]{2,1,0:T(8,128)S(1)}) custom-call(bf16[1,32]{1,0:T(2,128)(2,1)} %bitcast.10, bf16[32,32,4096]{2,1,0:T(8,128)(2,1)} %path_ref.3, bf16[8,32,512]{2,1,0:T(8,128)(2,1)} %trace_ref.1, s32[8,32,32]{2,1,0:T(8,128)} %start_ref.1), custom_call_target="tpu_custom_call" | custom-call | tf_op jit(solution)/shard_map/prepare/pallas_call | solution.py:365
  17.3 3.2 %all-to-all-done.tx_ref = f32[32,8,128]{2,1,0:T(8,128)S(1)} async-done(((f32[32,8,128]{2,1,0:T(8,128)}), f32[32,8,128]{2,1,0:T(8,128)S(1)}, u32[]{:S(2)}, u32[]{:S(2)}) %all-to-all-start) | async-done | bytes 131104 | tf_op jit(solution)/shard_map/all_to_all | solution.py:455
  20.5 7.1 %focus.1 = (f32[32,128,256]{2,1,0:T(8,128)S(1)}, f32[16,16,128]{2,1,0:T(8,128)S(1)}, f32[16,16,128]{2,1,0:T(8,128)S(1)}, bf16[32,32,4096]{2,1,0:T(8,128)(2,1)S(1)}) custom-call(f32[32,8,128]{2,1,0:T(8,128)S(1)} %all-to-all-done.tx_ref, f32[32,128,128]{2,1,0:T(8,128)S(1)} %get-tuple-element.13.rx_ref, f32[32,8,256]{2,1,0:T(8,128)S(1)} %get-tuple-element.14.win_ref, ...), custom_call_target="tpu_custom_call" | custom-call | tf_op jit(solution)/shard_map/focus/pallas_call | solution.py:393
  27.6 0.5 collective-permute-start
  28.1 1.0 %collective-permute-done.got_ref = f32[16,16,128]{2,1,0:T(8,128)S(1)} collective-permute-done((f32[16,16,128]{2,1,0:T(8,128)S(1)}, f32[16,16,128]{2,1,0:T(8,128)S(1)}, u32[]{:S(2)}, u32[]{:S(2)}) %collective-permute-start) | collective-permute-done | bytes 131104 | tf_op jit(solution)/shard_map/ppermute | solution.py:457
  29.1 10.9 %all_to_all.31.part_ref = f32[16,16,128]{2,1,0:T(8,128)S(1)} all-to-all(f32[16,16,128]{2,1,0:T(8,128)S(1)} %sum_cores.1), channel_id=1, replica_groups={{0,2,4,6,8,10,12,14,16,18,20,22,24,26,28,30},{1,3,5,7,9,11,13,15,17,19,..., dimensions={0} | all-to-all | bytes 262144 | tf_op jit(solution)/shard_map/all_to_all | solution.py:451
  40.0 2.0 %collective-permute-start.1 = (f32[8,128]{1,0:T(8,128)S(1)}, f32[8,128]{1,0:T(8,128)S(1)}, u32[]{:S(2)}, u32[]{:S(2)}) collective-permute-start(f32[8,128]{1,0:T(8,128)S(1)} %get-tuple-element.17.here_ref), channel_id=1, source_target_pairs={{0,1},{1,0},{2,3},{3,2},{4,5},{5,4},{6,7},{7,6},{8,9},{9,8},{10,11... | collective-permute-start | bytes 12296 | tf_op jit(solution)/shard_map/ppermute | solution.py:471
  42.0 0.8 collective-permute-done.1.there_ref
  42.8 16.9 %all_to_all.32.pair_ref = f32[8,4,128]{2,1,0:T(4,128)S(1)} all-to-all(f32[8,4,128]{2,1,0:T(4,128)S(1)} %squares.1), channel_id=1, replica_groups=mesh['tx'=8,'rx'=32] {'tx'}, dimensions={0} | all-to-all | bytes 32768 | tf_op jit(solution)/shard_map/all_to_all | solution.py:478
  59.7 10.1 %all_to_all.33.refs_1_ = f32[16,5,4,128]{3,2,1,0:T(4,128)S(1)} all-to-all(f32[16,5,4,128]{3,2,1,0:T(4,128)S(1)} %sum_transmits.1), channel_id=1, replica_groups={{0,2,4,6,8,10,12,14,16,18,20,22,24,26,28,30},{1,3,5,7,9,11,13,15,17,19,..., dimensions={0} | all-to-all | bytes 327680 | tf_op jit(solution)/shard_map/all_to_all | solution.py:451
  69.8 0.0 copy-done
  69.8 0.0 copy-done.1
  69.8 0.0 copy-done.2
  69.8 3.6 %gradient.1 = f32[256,128]{1,0:T(8,128)S(1)} custom-call(f32[16]{0:T(128)S(1)} %copy-done.2, f32[16,5,4,128]{3,2,1,0:T(4,128)S(1)} %all_to_all.33.refs_1_, s32[32,128]{1,0:T(8,128)S(1)} %bitcast.8, f32[8,128]{1,0:T(8,128)S(1)} %get-tuple-element.18.refs_3_, bf16[8,32,128]{2,1,0:T(8,128)(2,1)S(1)} %copy-done, f32[32,128,256]{2,1,0:T(8,128)S(1)} %get-tuple-element.19.refs_5_, ...), custom_call_target="tpu_custom_call" | custom-call | tf_op jit(solution)/shard_map/gradient/pallas_call | solution.py:417
  73.4 20.8 %all_to_all.34 = f32[256,1,128]{2,1,0:T(1,128)S(1)} all-to-all(f32[256,1,128]{2,1,0:T(1,128)S(1)} %bitcast.6), channel_id=1, replica_groups=mesh['tx'=8,'rx'=32] {'tx','rx'}, dimensions={0} | all-to-all | bytes 262144 | tf_op jit(solution)/shard_map/all_to_all | solution.py:497
  94.2 0.6 total.1
  (4 shorter events, 0.1 us)
Async XLA Ops:
  1.7 18.8 %all-to-all-start = ((f32[32,8,128]{2,1,0:T(8,128)}), f32[32,8,128]{2,1,0:T(8,128)S(1)}, u32[]{:S(2)}, u32[]{:S(2)}) async-start(f32[32,8,128]{2,1,0:T(8,128)} %tx_delay.1), calls=%async_computation | async-start | bytes 262144 | tf_op jit(solution)/shard_map/all_to_all | solution.py:455
  11.8 58.0 %copy-start = (bf16[8,32,128]{2,1,0:T(8,128)(2,1)S(1)}, bf16[8,32,128]{2,1,0:T(8,128)(2,1)}, u32[]{:S(2)}) copy-start(bf16[8,32,128]{2,1,0:T(8,128)(2,1)} %refs_4_.1) | copy-start | bytes 196612
  11.8 58.0 %copy-start.1 = (s32[4096]{0:T(1024)S(1)}, s32[4096]{0:T(1024)}, u32[]{:S(2)}) copy-start(s32[4096]{0:T(1024)} %param.12) | copy-start | bytes 49156
  11.8 58.0 %copy-start.2 = (f32[16]{0:T(128)S(1)}, f32[16]{0:T(128)}, u32[]{:S(2)}) copy-start(f32[16]{0:T(128)} %refs_0_.1) | copy-start | bytes 196
  27.6 1.5 %collective-permute-start = (f32[16,16,128]{2,1,0:T(8,128)S(1)}, f32[16,16,128]{2,1,0:T(8,128)S(1)}, u32[]{:S(2)}, u32[]{:S(2)}) collective-permute-start(f32[16,16,128]{2,1,0:T(8,128)S(1)} %get-tuple-element.16), channel_id=1, source_target_pairs={{0,1},{1,0},{2,3},{3,2},{4,5},{5,4},{6,7},{7,6},{8,9},{9,8},{10,11... | collective-permute-start | bytes 393224 | tf_op jit(solution)/shard_map/ppermute | solution.py:457
  40.0 2.8 %collective-permute-start.1 = (f32[8,128]{1,0:T(8,128)S(1)}, f32[8,128]{1,0:T(8,128)S(1)}, u32[]{:S(2)}, u32[]{:S(2)}) collective-permute-start(f32[8,128]{1,0:T(8,128)S(1)} %get-tuple-element.17.here_ref), channel_id=1, source_target_pairs={{0,1},{1,0},{2,3},{3,2},{4,5},{5,4},{6,7},{7,6},{8,9},{9,8},{10,11... | collective-permute-start | bytes 12296 | tf_op jit(solution)/shard_map/ppermute | solution.py:471

commit v6 on v5

--- a/solution.py
+++ b/solution.py
@@ -5,6 +5,7 @@
 from jax import lax
 from jax.experimental import pallas as pl
 from jax.experimental.pallas import tpu as pltpu
+from jax.sharding import Mesh
 from jax.sharding import PartitionSpec as P
 
 W = 8
@@ -14,6 +15,9 @@
 LN2 = math.log(2.0)
 HALF_LOG2E = 0.5 / LN2
 F32 = jnp.float32
+FINE = (("zh", 2), ("y", 4), ("x", 4), ("zl", 4), ("c", 2))
+TX = ("zh", "y")
+RX = ("x", "zl", "c")
 
 
 def block_diagonal(s_row, rows, cells):
@@ -170,7 +174,7 @@
         return carry
 
     lax.fori_loop(0, rows // 2, receivers, 0)
-    mine = lax.axis_index("rx") % 2
+    mine = lax.axis_index("c")
     for source, base in ((total_f_ref, 0), (total_s_ref, count)):
         for half in range(halves):
             turned_ref[...] = source[:, half * 128 : (half + 1) * 128].T
@@ -187,44 +191,66 @@
     out_ref[...] = keep_ref[...] + got_ref[...]
 
 
-def gather_sum_kernel(part_ref, beam_ref, slope_ref):
-    total = part_ref[0]
-    for i in range(1, part_ref.shape[0]):
-        total = total + part_ref[i]
-    count = beam_ref.shape[0]
-    beam_ref[...] = total[0:count]
-    slope_ref[...] = total[count : 2 * count]
-
-
-def square_kernel(here_ref, there_ref, out_ref):
-    rows = []
-    for ref in (here_ref, there_ref):
-        beam = ref[...]
-        rows.append(jnp.sum(beam, axis=0, keepdims=True))
-        rows.append(jnp.sum(beam * beam, axis=0, keepdims=True))
-    out_ref[...] = jnp.broadcast_to(jnp.concatenate(rows, axis=0)[None], out_ref.shape)
-
-
-def spread_kernel(pair_ref, here_ref, there_ref, out_ref):
-    even_core = lax.axis_index("rx") % 2 == 0
-    total = pair_ref[0]
-    for i in range(1, pair_ref.shape[0]):
-        total = total + pair_ref[i]
-    even = jnp.where(even_core, total[0:2], total[2:4])
-    odd = jnp.where(even_core, total[2:4], total[0:2])
-    here = here_ref[...]
-    there = there_ref[...]
-    fields = [
-        jnp.where(even_core, here, there),
-        jnp.where(even_core, there, here),
-        jnp.concatenate([even, odd], axis=0),
-    ]
-    group = 0
-    for field in fields:
-        for first in range(0, field.shape[0], 4):
-            block = field[first : first + 4]
-            out_ref[:, group] = jnp.broadcast_to(block[None], (out_ref.shape[0], 4, PB))
-            group += 1
+def sum_x_kernel(part_ref, out_ref):
+    sources, blocks, rows, _ = part_ref.shape
+    count = rows // 2
+    for block in range(blocks):
+        total = part_ref[0, block]
+        for i in range(1, sources):
+            total = total + part_ref[i, block]
+        here = slice(block * count, (block + 1) * count)
+        beam = total[0:count]
+        out_ref[:, here] = jnp.broadcast_to(beam[None], (out_ref.shape[0], count, PB))
+        for far in range(out_ref.shape[0] // blocks):
+            out_ref[far * blocks + block, blocks * count :] = total[count:rows]
+
+
+def sum_z_kernel(part_ref, out_ref, slope_sum_ref):
+    blocks = 4
+    rows = part_ref.shape[1]
+    count = rows // (blocks + 1)
+    first = lax.axis_index("zh") == 0
+    totals = []
+    for far in range(part_ref.shape[0] // blocks):
+        total = part_ref[far * blocks]
+        for i in range(1, blocks):
+            total = total + part_ref[far * blocks + i]
+        totals.append(total)
+    own = jnp.where(first, totals[0], totals[1])
+    slope_sum_ref[...] = own[blocks * count :]
+    lines = []
+    for power in (False, True):
+        for block in range(blocks):
+            line = None
+            for total in totals:
+                beam = total[block * count : (block + 1) * count]
+                part = jnp.sum(beam * beam if power else beam, axis=0, keepdims=True)
+                line = part if line is None else line + part
+            lines.append(line)
+    wide = out_ref.shape[0]
+    out_ref[:, 0 : blocks * count] = jnp.broadcast_to(
+        own[0 : blocks * count][None], (wide, blocks * count, PB)
+    )
+    out_ref[:, blocks * count :] = jnp.broadcast_to(
+        jnp.concatenate(lines, axis=0)[None], (wide, 2 * blocks, PB)
+    )
+
+
+def sum_y_kernel(part_ref, out_ref):
+    own = lax.axis_index("y")
+    sides = 4
+    blocks = 4
+    count = out_ref.shape[1] - 2
+    for x in range(part_ref.shape[0] // sides):
+        total = part_ref[x * sides, blocks * count :, :]
+        for y in range(1, sides):
+            total = total + part_ref[x * sides + y, blocks * count :, :]
+        beams = part_ref[x * sides + own, 0 : blocks * count, :]
+        for block in range(blocks):
+            place = x * blocks + block
+            out_ref[place, 0:count] = beams[block * count : (block + 1) * count]
+            out_ref[place, count : count + 1] = total[block : block + 1]
+            out_ref[place, count + 1 : count + 2] = total[blocks + block : blocks + block + 1]
 
 
 def total_kernel(share_ref, out_ref):
@@ -261,7 +287,8 @@
 def gradient_kernel(
     total_tx,
     cot_ref,
-    every_ref,
+    here_ref,
+    there_ref,
     ids_ref,
     slope_sum_ref,
     tx_path_ref,
@@ -274,18 +301,19 @@
     grad_ref,
 ):
     rows, cells, _ = path_ref.shape
-    pairs = every_ref.shape[0]
+    pairs = here_ref.shape[0]
     blocks = 2 * pairs
     count = slope_sum_ref.shape[0]
     per = 128 // blocks
     together = grad_ref.shape[0]
-    me = lax.axis_index("rx")
+    core = lax.axis_index("c")
+    me = (lax.axis_index("x") * lax.axis_size("zl") + lax.axis_index("zl")) * 2 + core
 
     for row in range(count + 2):
-        for parity in range(2):
-            place = parity * count + row if row < count else count + parity * 2 + row
-            source = every_ref[:, place // 4, place % 4, :]
-            all_ref[row, pl.ds(parity, pairs, stride=2), :] = source
+        here = here_ref[:, row, :]
+        there = there_ref[:, row, :]
+        all_ref[row, pl.ds(0, pairs, stride=2), :] = jnp.where(core == 0, here, there)
+        all_ref[row, pl.ds(1, pairs, stride=2), :] = jnp.where(core == 0, there, here)
     coherent = all_ref[count]
     power = all_ref[count + 1]
     scale_n, scale_d = patch_scales(total_tx, cot_ref, ids_ref[...] // PP, coherent, power)
@@ -407,16 +435,16 @@
     )(tx_delay, rx_delay, window, in_hbm(rx_paths))
 
 
-def gradient(total_tx, parts, patch_cotangent, every, pixel_order, slope_sum, tx_paths, slope, rx_paths):
+def gradient(total_tx, parts, patch_cotangent, here, there, pixel_order, slope_sum, tx_paths, slope, rx_paths):
     rx_count = rx_paths.shape[0]
-    blocks = 2 * every.shape[0]
+    blocks = 2 * here.shape[0]
     tx_count = tx_paths.shape[0]
     lanes = tx_count * blocks
     together = 8
     vmem = pl.BlockSpec(memory_space=pltpu.VMEM)
     return pl.pallas_call(
         lambda *refs: gradient_kernel(total_tx, *refs),
-        in_specs=[pl.BlockSpec(memory_space=pltpu.SMEM)] + [vmem] * 6,
+        in_specs=[pl.BlockSpec(memory_space=pltpu.SMEM)] + [vmem] * 7,
         out_specs=vmem,
         out_shape=shaped(parts, PB),
         scratch_shapes=[
@@ -429,7 +457,8 @@
         name="gradient",
     )(
         patch_cotangent,
-        every,
+        here,
+        there,
         pixel_order.reshape(blocks, PB),
         slope_sum,
         tx_paths,
@@ -438,82 +467,71 @@
     )
 
 
+def local(kernel, name, out_shape, *arrays):
+    return pl.pallas_call(
+        kernel, out_shape=out_shape, compiler_params=params(4), name=name
+    )(*arrays)
+
+
 def on_device(slowness, tx_paths, rx_paths, traces, tap_start, pixel_order, patch_cotangent):
     tx_count, cells, _ = tx_paths.shape
-    tx_size = lax.axis_size("tx")
-    rx_size = lax.axis_size("rx")
-    pairs = rx_size // 2
+    rx_size = lax.axis_size(RX)
+    tx_size = lax.axis_size(TX)
+    x_size = lax.axis_size("x")
+    near = lax.axis_size("zl")
+    pairs = x_size * near
     s_row = slowness.reshape(1, cells)
-    partner = [(i, i ^ 1) for i in range(rx_size)]
-    same_core = [list(range(core, rx_size, 2)) for core in range(2)]
-
-    def between_chips(array):
-        return lax.all_to_all(array, "rx", 0, 0, axis_index_groups=same_core)
+    swap = [(0, 1), (1, 0)]
 
     delay = tx_delays(s_row, tx_paths, rx_size)
     rx_delay, window = prepare(s_row, rx_paths, traces, tap_start)
-    tx_delay = lax.all_to_all(delay, "rx", 0, 0)
+    tx_delay = lax.all_to_all(delay, RX, 0, 0)
     slope, keep, give, path_copy = focus(tx_delay, rx_delay, window, rx_paths)
-    got = lax.ppermute(give, "rx", partner)
-    part = pl.pallas_call(
-        pair_sum_kernel,
-        out_shape=shaped(*keep.shape),
-        compiler_params=params(4),
-        name="sum_cores",
-    )(keep, got)
-    part = between_chips(part)
-    beam, slope_sum = pl.pallas_call(
-        gather_sum_kernel,
-        out_shape=[shaped(tx_count, PB), shaped(tx_count, PB)],
-        compiler_params=params(4),
-        name="sum_receivers",
-    )(part)
-    other = lax.ppermute(beam, "rx", partner)
-    pair = pl.pallas_call(
-        square_kernel,
-        out_shape=shaped(tx_size, 4, PB),
-        compiler_params=params(4),
-        name="squares",
-    )(beam, other)
-    pair = lax.all_to_all(pair, "tx", 0, 0)
-    spread = pl.pallas_call(
-        spread_kernel,
-        out_shape=shaped(pairs, (2 * tx_count + 4) // 4, 4, PB),
-        compiler_params=params(4),
-        name="sum_transmits",
-    )(pair, beam, other)
-    every = between_chips(spread)
+    got = lax.ppermute(give, "c", swap)
+    part = local(pair_sum_kernel, "sum_cores", shaped(*keep.shape), keep, got)
+    part = lax.all_to_all(part.reshape(x_size, near, 2 * tx_count, PB), "x", 0, 0)
+    rows = (near + 1) * tx_count
+    part = local(sum_x_kernel, "sum_x", shaped(2 * near, rows, PB), part)
+    part = lax.all_to_all(part, ("zh", "zl"), 0, 0)
+    rows = near * (tx_count + 2)
+    part, slope_sum = local(
+        sum_z_kernel,
+        "sum_z",
+        [shaped(x_size * lax.axis_size("y"), rows, PB), shaped(tx_count, PB)],
+        part,
+    )
+    part = lax.all_to_all(part, ("x", "y"), 0, 0)
+    here = local(sum_y_kernel, "sum_y", shaped(pairs, tx_count + 2, PB), part)
+    there = lax.ppermute(here, "c", swap)
     share = gradient(
         tx_count * tx_size,
         tx_size * rx_size,
         patch_cotangent,
-        every,
+        here,
+        there,
         pixel_order,
         slope_sum,
         tx_paths,
         slope,
         path_copy,
     )
-    share = lax.all_to_all(share, ("tx", "rx"), 0, 0, tiled=True)
-    return pl.pallas_call(
-        total_kernel,
-        out_shape=shaped(cells),
-        compiler_params=params(4),
-        name="total",
-    )(share)
+    share = lax.all_to_all(share, TX + RX, 0, 0, tiled=True)
+    return local(total_kernel, "total", shaped(cells), share)
 
 
 def solution(mesh):
+    names = tuple(name for name, _ in FINE)
+    fine = Mesh(mesh.devices.reshape([size for _, size in FINE]), names)
     in_specs = (
         P(),
-        P("tx", None, "rx"),
-        P("rx", None, None),
-        P("tx", "rx", None),
-        P("tx", "rx", None),
+        P(TX, None, RX),
+        P(RX, None, None),
+        P(TX, RX, None),
+        P(TX, RX, None),
         P(),
         P(),
     )
     out_specs = P()
     return jax.shard_map(
-        on_device, mesh=mesh, in_specs=in_specs, out_specs=out_specs, check_vma=False
-    )
+        on_device, mesh=fine, in_specs=in_specs, out_specs=out_specs, check_vma=False
+    )

time: 95.2 us -> 90.5 us (0.951)
  blocking collectives: 58.7 us -> 51.2 us
  starting transfers between devices: 12.5 us -> 14.9 us
    all_to_all x4, blocking collectives: 58.7 us -> 51.2 us  [the longest x1 18 us: on_device(): share = lax.all_to_all(share, TX + RX, 0, 0, tiled=True)]
    ppermute x2, starting transfers between devices: 2.45 us -> 4.91 us  [the longest x1 4.42 us: on_device(): there = lax.ppermute(here, 'c', swap)]
where the time goes in v6:
time: 90.5 us; the launch traced here: 90.1 us
  blocking collectives  51.2 us (57%)
  Pallas kernels  18.7 us (21%)
  starting transfers between devices  14.9 us (16%)
  waiting for transfers between devices  5.14 us (6%)
    all_to_all x1, blocking collectives, on_device(): share = lax.all_to_all(share, TX + RX, 0, 0, tiled=True)  18 us
    all_to_all x1, blocking collectives, on_device(): part = lax.all_to_all(part, ('zh', 'zl'), 0, 0)  13.6 us
    all_to_all x1, blocking collectives, on_device(): part = lax.all_to_all(part, ('x', 'y'), 0, 0)  12.4 us
    all_to_all x1, starting transfers between devices, on_device(): tx_delay = lax.all_to_all(delay, RX, 0, 0)  10 us
    all_to_all x1, blocking collectives, on_device(): lax.all_to_all(part.reshape(x_size, near, 2 * tx_count, PB), 'x', 0, 0)  7.22 us
    pallas_call x1, Pallas kernels, focus(): pl.pallas_call(focus_kernel, in_specs=[vmem, vmem, vmem, pl.BlockSpec(mem...  7.14 us
    pallas_call x1, Pallas kernels, prepare(): pl.pallas_call(prepare_kernel, grid=(rx_count // rows,), in_specs=[whole(...  5.5 us
    ppermute x1, starting transfers between devices, on_device(): there = lax.ppermute(here, 'c', swap)  4.42 us
  transfers between devices with their start and end apart: 3, of which 3 were waited for; matrix products, arithmetic and copies ran while one was open for 0% of the time, Pallas kernels for 6%

profile of v6, /device:TPU:1, one launch (start us, length us, event | category | flops | bytes accessed | tf_op | source)
XLA Modules:
  0.0 90.1 jit_solution(8714455442389205694)
XLA Ops:
  0.0 1.7 %tx_delay.1 = f32[32,8,128]{2,1,0:T(8,128)} custom-call(bf16[1,32]{1,0:T(2,128)(2,1)} %bitcast.11, bf16[8,32,128]{2,1,0:T(8,128)(2,1)} %refs_5_.1), custom_call_target="tpu_custom_call" | custom-call | tf_op jit(solution)/shard_map/tx_delay/pallas_call | solution.py:374
  1.7 10.0 %all-to-all-start = ((f32[32,8,128]{2,1,0:T(8,128)}), f32[32,8,128]{2,1,0:T(8,128)S(1)}, u32[]{:S(2)}, u32[]{:S(2)}) async-start(f32[32,8,128]{2,1,0:T(8,128)} %tx_delay.1), calls=%async_computation | async-start | bytes 262144 | tf_op jit(solution)/shard_map/all_to_all | solution.py:488
  11.8 5.5 %prepare.1 = (f32[32,128,128]{2,1,0:T(8,128)S(1)}, f32[32,8,256]{2,1,0:T(8,128)S(1)}) custom-call(bf16[1,32]{1,0:T(2,128)(2,1)} %bitcast.12, bf16[32,32,4096]{2,1,0:T(8,128)(2,1)} %path_ref.3, bf16[8,32,512]{2,1,0:T(8,128)(2,1)} %trace_ref.1, s32[8,32,32]{2,1,0:T(8,128)} %start_ref.1), custom_call_target="tpu_custom_call" | custom-call | tf_op jit(solution)/shard_map/prepare/pallas_call | solution.py:393
  17.3 0.0 copy-start
  17.3 0.0 copy-start.1
  17.3 0.0 copy-start.2
  17.3 3.2 %all-to-all-done.tx_ref = f32[32,8,128]{2,1,0:T(8,128)S(1)} async-done(((f32[32,8,128]{2,1,0:T(8,128)}), f32[32,8,128]{2,1,0:T(8,128)S(1)}, u32[]{:S(2)}, u32[]{:S(2)}) %all-to-all-start) | async-done | bytes 131104 | tf_op jit(solution)/shard_map/all_to_all | solution.py:488
  20.5 7.1 %focus.1 = (f32[32,128,256]{2,1,0:T(8,128)S(1)}, f32[16,16,128]{2,1,0:T(8,128)S(1)}, f32[16,16,128]{2,1,0:T(8,128)S(1)}, bf16[32,32,4096]{2,1,0:T(8,128)(2,1)S(1)}) custom-call(f32[32,8,128]{2,1,0:T(8,128)S(1)} %all-to-all-done.tx_ref, f32[32,128,128]{2,1,0:T(8,128)S(1)} %get-tuple-element.13.rx_ref, f32[32,8,256]{2,1,0:T(8,128)S(1)} %get-tuple-element.14.win_ref, ...), custom_call_target="tpu_custom_call" | custom-call | tf_op jit(solution)/shard_map/focus/pallas_call | solution.py:421
  27.6 0.5 collective-permute-start
  28.1 1.0 %collective-permute-done.got_ref = f32[16,16,128]{2,1,0:T(8,128)S(1)} collective-permute-done((f32[16,16,128]{2,1,0:T(8,128)S(1)}, f32[16,16,128]{2,1,0:T(8,128)S(1)}, u32[]{:S(2)}, u32[]{:S(2)}) %collective-permute-start) | collective-permute-done | bytes 131104 | tf_op jit(solution)/shard_map/ppermute | solution.py:490
  29.1 7.2 %all_to_all.31.part_ref = f32[4,4,16,128]{3,2,1,0:T(8,128)S(1)} all-to-all(f32[4,4,16,128]{3,2,1,0:T(8,128)S(1)} %bitcast.8), channel_id=1, replica_groups=mesh['zh'=2,'y'=4,'x'=4,'zl'=4,'c'=2] {'x'}, dimensions={0} | all-to-all | bytes 262144 | tf_op jit(solution)/shard_map/all_to_all | solution.py:492
  36.4 13.6 %all_to_all.32.part_ref = f32[8,40,128]{2,1,0:T(8,128)S(1)} all-to-all(f32[8,40,128]{2,1,0:T(8,128)S(1)} %sum_x.1), channel_id=1, replica_groups=mesh['zh'=2,'y'=4,'x'=4,'zl'=4,'c'=2] {'zh','zl'}, dimensions={0} | all-to-all | bytes 327680 | tf_op jit(solution)/shard_map/all_to_all | solution.py:495
  50.0 12.4 %all_to_all.33.part_ref = f32[16,40,128]{2,1,0:T(8,128)S(1)} all-to-all(f32[16,40,128]{2,1,0:T(8,128)S(1)} %get-tuple-element.17), channel_id=1, replica_groups=mesh['zh'=2,'y'=4,'x'=4,'zl'=4,'c'=2] {'x','y'}, dimensions={0} | all-to-all | bytes 655360 | tf_op jit(solution)/shard_map/all_to_all | solution.py:503
  62.4 4.4 %collective-permute-start.1 = (f32[16,10,128]{2,1,0:T(8,128)S(1)}, f32[16,10,128]{2,1,0:T(8,128)S(1)}, u32[]{:S(2)}, u32[]{:S(2)}) collective-permute-start(f32[16,10,128]{2,1,0:T(8,128)S(1)} %sum_y.1.refs_1_), channel_id=1, source_target_pairs={{0,1},{1,0},{2,3},{3,2},{4,5},{5,4},{6,7},{7,6},{8,9},{9,8},{10,11... | collective-permute-start | bytes 245768 | tf_op jit(solution)/shard_map/ppermute | solution.py:505
  66.8 1.0 %collective-permute-done.1.refs_2_ = f32[16,10,128]{2,1,0:T(8,128)S(1)} collective-permute-done((f32[16,10,128]{2,1,0:T(8,128)S(1)}, f32[16,10,128]{2,1,0:T(8,128)S(1)}, u32[]{:S(2)}, u32[]{:S(2)}) %collective-permute-start.1) | collective-permute-done | bytes 81952 | tf_op jit(solution)/shard_map/ppermute | solution.py:505
  67.8 0.0 copy-done
  67.8 0.0 copy-done.1
  67.8 0.0 copy-done.2
  67.8 3.7 %gradient.1 = f32[256,128]{1,0:T(8,128)S(1)} custom-call(f32[16]{0:T(128)S(1)} %copy-done.2, f32[16,10,128]{2,1,0:T(8,128)S(1)} %sum_y.1.refs_1_, f32[16,10,128]{2,1,0:T(8,128)S(1)} %collective-permute-done.1.refs_2_, s32[32,128]{1,0:T(8,128)S(1)} %bitcast.10, f32[8,128]{1,0:T(8,128)S(1)} %get-tuple-element.18.refs_4_, bf16[8,32,128]{2,1,0:T(8,128)(2,1)S(1)} %copy-done, ...), custom_call_target="tpu_custom_call" | custom-call | tf_op jit(solution)/shard_map/gradient/pallas_call | solution.py:445
  71.6 18.0 %all_to_all.34 = f32[256,1,128]{2,1,0:T(1,128)S(1)} all-to-all(f32[256,1,128]{2,1,0:T(1,128)S(1)} %bitcast.7), channel_id=1, replica_groups=mesh['zh'=2,'y'=4,'x'=4,'zl'=4,'c'=2] {'zh','y','x','zl','c'}, dimensions={0} | all-to-all | bytes 262144 | tf_op jit(solution)/shard_map/all_to_all | solution.py:518
  89.6 0.6 total.1
  (4 shorter events, 0.1 us)
Async XLA Ops:
  1.7 18.8 %all-to-all-start = ((f32[32,8,128]{2,1,0:T(8,128)}), f32[32,8,128]{2,1,0:T(8,128)S(1)}, u32[]{:S(2)}, u32[]{:S(2)}) async-start(f32[32,8,128]{2,1,0:T(8,128)} %tx_delay.1), calls=%async_computation | async-start | bytes 262144 | tf_op jit(solution)/shard_map/all_to_all | solution.py:488
  17.3 50.6 %copy-start = (bf16[8,32,128]{2,1,0:T(8,128)(2,1)S(1)}, bf16[8,32,128]{2,1,0:T(8,128)(2,1)}, u32[]{:S(2)}) copy-start(bf16[8,32,128]{2,1,0:T(8,128)(2,1)} %refs_5_.1) | copy-start | bytes 196612
  17.3 50.5 %copy-start.1 = (s32[4096]{0:T(1024)S(1)}, s32[4096]{0:T(1024)}, u32[]{:S(2)}) copy-start(s32[4096]{0:T(1024)} %param.12) | copy-start | bytes 49156
  17.3 50.5 %copy-start.2 = (f32[16]{0:T(128)S(1)}, f32[16]{0:T(128)}, u32[]{:S(2)}) copy-start(f32[16]{0:T(128)} %refs_0_.1) | copy-start | bytes 196
  27.6 1.5 %collective-permute-start = (f32[16,16,128]{2,1,0:T(8,128)S(1)}, f32[16,16,128]{2,1,0:T(8,128)S(1)}, u32[]{:S(2)}, u32[]{:S(2)}) collective-permute-start(f32[16,16,128]{2,1,0:T(8,128)S(1)} %get-tuple-element.16), channel_id=1, source_target_pairs={{0,1},{1,0},{2,3},{3,2},{4,5},{5,4},{6,7},{7,6},{8,9},{9,8},{10,11... | collective-permute-start | bytes 393224 | tf_op jit(solution)/shard_map/ppermute | solution.py:490
  62.4 5.4 %collective-permute-start.1 = (f32[16,10,128]{2,1,0:T(8,128)S(1)}, f32[16,10,128]{2,1,0:T(8,128)S(1)}, u32[]{:S(2)}, u32[]{:S(2)}) collective-permute-start(f32[16,10,128]{2,1,0:T(8,128)S(1)} %sum_y.1.refs_1_), channel_id=1, source_target_pairs={{0,1},{1,0},{2,3},{3,2},{4,5},{5,4},{6,7},{7,6},{8,9},{9,8},{10,11... | collective-permute-start | bytes 245768 | tf_op jit(solution)/shard_map/ppermute | solution.py:505

commit v7 on v6

--- a/solution.py
+++ b/solution.py
@@ -13,7 +13,7 @@
 PP = 256
 EPS = 1e-06
 LN2 = math.log(2.0)
-HALF_LOG2E = 0.5 / LN2
+LOG2E = 1.0 / LN2
 F32 = jnp.float32
 FINE = (("zh", 2), ("y", 4), ("x", 4), ("zl", 4), ("c", 2))
 TX = ("zh", "y")
@@ -42,58 +42,90 @@
     delay = jnp.dot(
         left, path_ref[...].reshape(rows * cells, width), preferred_element_type=F32
     )
-    out_ref[...] = jnp.broadcast_to((delay * HALF_LOG2E)[None], out_ref.shape)
-
-
-def prepare_kernel(s_ref, path_ref, trace_ref, start_ref, delay_ref, win_ref, sample_ref, plain_ref):
-    step = pl.program_id(0)
-    rows, cells, pixels = path_ref.shape
+    out_ref[...] = jnp.broadcast_to((delay * -LOG2E)[None], out_ref.shape)
+
+
+def prepare_kernel(
+    s_hbm,
+    path_hbm,
+    trace_hbm,
+    start_hbm,
+    delay_ref,
+    win_ref,
+    s_ref,
+    path_ref,
+    trace_ref,
+    start_ref,
+    sample_ref,
+    plain_ref,
+    copied,
+):
+    rx_count, cells, pixels = path_ref.shape
     count = trace_ref.shape[0]
     blocks = start_ref.shape[2]
     per = 128 // blocks
-
-    @pl.when(step == 0)
-    def _():
-        sample_ref[...] = trace_ref[...].astype(F32)
-
+    rows = plain_ref.shape[0]
+    groups = rx_count // rows
+
+    fetches = [
+        pltpu.make_async_copy(trace_hbm, trace_ref, copied.at[0]),
+        pltpu.make_async_copy(start_hbm, start_ref, copied.at[1]),
+        pltpu.make_async_copy(s_hbm, s_ref, copied.at[2]),
+    ]
+    for i in range(groups):
+        some = pl.ds(i * rows, rows)
+        fetches.append(
+            pltpu.make_async_copy(path_hbm.at[some], path_ref.at[some], copied.at[3 + i])
+        )
+    for fetch in fetches:
+        fetch.start()
+    for fetch in fetches[:3]:
+        fetch.wait()
+
+    sample_ref[...] = trace_ref[...].astype(F32)
+    lane_group = lax.broadcasted_iota(jnp.int32, (rows, 128), 1) // blocks
+
+    def windows(step, carry):
+        mine = pl.ds(pl.multiple_of(step * rows, rows), rows)
+        for early in range(0, count, per):
+            picks = []
+            for t in range(early, early + per):
+                starts = jnp.concatenate([start_ref[t, mine, :]] * per, axis=1)
+                for first in range(0, W, per):
+                    index = starts + (lane_group + first)
+                    low = index & 127
+                    high = index >> 7
+                    picked = None
+                    for part in range(sample_ref.shape[2] // 128):
+                        source = sample_ref[t, mine, part * 128 : (part + 1) * 128]
+                        got = jnp.take_along_axis(
+                            source, low, axis=1, mode="promise_in_bounds"
+                        )
+                        picked = got if picked is None else jnp.where(high == part, got, picked)
+                    picks.append(picked)
+            lanes = slice(early * blocks, early * blocks + 128)
+            for j in range(W):
+                total = None
+                for i in range(per):
+                    rolled = picks[i * (W // per) + j // per]
+                    shift = ((i - j % per) * blocks) % 128
+                    if shift:
+                        rolled = pltpu.roll(rolled, shift, 1)
+                    total = rolled if total is None else jnp.where(lane_group == i, rolled, total)
+                win_ref[mine, j, lanes] = total * math.exp(-0.5 * j * j)
+        return carry
+
+    lax.fori_loop(0, groups, windows, 0)
     left = block_diagonal(s_ref[...].astype(F32), rows, cells)
-    delay = jnp.dot(
-        left, path_ref[...].reshape(rows * cells, pixels), preferred_element_type=F32
-    )
-    delay = delay * HALF_LOG2E
-    for k in range(blocks):
-        plain_ref[:, k, :] = delay[:, k * PB : (k + 1) * PB]
-    for r in range(rows):
-        delay_ref[r] = jnp.concatenate([plain_ref[r]] * per, axis=0).T
-
-    mine = pl.ds(pl.multiple_of(step * rows, rows), rows)
-    shape = (rows, 128)
-    group = lax.broadcasted_iota(jnp.int32, shape, 1) // blocks
-    for early in range(0, count, per):
-        picks = []
-        for t in range(early, early + per):
-            starts = jnp.concatenate([start_ref[t, mine, :]] * per, axis=1)
-            for first in range(0, W, per):
-                index = starts + (group + first)
-                low = index & 127
-                high = index >> 7
-                picked = None
-                for part in range(sample_ref.shape[2] // 128):
-                    source = sample_ref[t, mine, part * 128 : (part + 1) * 128]
-                    got = jnp.take_along_axis(source, low, axis=1, mode="promise_in_bounds")
-                    picked = got if picked is None else jnp.where(high == part, got, picked)
-                picks.append(picked)
-        for j in range(W):
-            total = None
-            for i in range(per):
-                rolled = picks[i * (W // per) + j // per]
-                shift = ((i - j % per) * blocks) % 128
-                if shift:
-                    rolled = pltpu.roll(rolled, shift, 1)
-                total = rolled if total is None else jnp.where(group == i, rolled, total)
-            off = j - (W - 1) / 2.0
-            lanes = slice(early * blocks, early * blocks + 128)
-            win_ref[:, j, lanes] = total * math.exp(-0.5 * off * off)
+    for i in range(groups):
+        fetches[3 + i].wait()
+        paths = path_ref[i * rows : (i + 1) * rows].reshape(rows * cells, pixels)
+        delay = jnp.dot(left, paths, preferred_element_type=F32)
+        delay = delay * -LOG2E - (W - 1) / 2.0 * LOG2E
+        for k in range(blocks):
+            plain_ref[:, k, :] = delay[:, k * PB : (k + 1) * PB]
+        for r in range(rows):
+            delay_ref[i * rows + r] = jnp.concatenate([plain_ref[r]] * per, axis=0).T
 
 
 def focus_kernel(
@@ -116,7 +148,6 @@
     blocks, count, _ = tx_ref.shape
     rows = rx_ref.shape[0]
     per = 128 // blocks
-    limit = 9.25 / LN2
     halves = count // per
 
     for half in range(halves):
@@ -125,29 +156,25 @@
     total_f_ref[...] = jnp.zeros_like(total_f_ref)
     total_s_ref[...] = jnp.zeros_like(total_s_ref)
 
-    def horner(z, c3, c2, c1, c0):
-        p1 = c3 * z + c2
-        p2 = p1 * z + c1
-        d2 = c3 * z + p1
-        return p2 * z + c0, d2 * z + p2
-
-    def point(tap, h):
-        h = jnp.minimum(jnp.maximum(h, -limit), limit)
-        m = h * (-LN2)
-        s = jnp.exp2(h)
-        si = jnp.exp2(-h)
-        gauss = jnp.exp2(m * h)
-        u = s * s
-        v = si * si
-        up, dup = horner(u, tap[7], tap[6], tap[5], tap[4])
-        down, ddown = horner(v, tap[0], tap[1], tap[2], tap[3])
-        x = s * up
-        y = si * down
-        both = x + y
-        change = (x - y) * 0.5 + ((s * u) * dup - (si * v) * ddown)
-        focused = gauss * (gauss * both)
-        slope = gauss * (gauss * (change + (m + m) * both))
-        return focused, slope
+    def point(tap, tau):
+        ratio = jnp.exp2(tau)
+        twice = tau + tau
+        power = tau * (tau * (-0.5 * LN2) - (W - 1.0))
+        focused = None
+        for j in range(W - 1, -1, -2):
+            upper = jnp.exp2(power)
+            lower = upper * ratio
+            if focused is None:
+                focused = tap[j] * upper
+                moment = focused
+            else:
+                focused = focused + tap[j] * upper
+                moment = moment + focused
+            focused = focused + tap[j - 1] * lower
+            if j > 1:
+                moment = moment + focused
+                power = power + twice
+        return focused, moment * LOG2E + tau * focused
 
     def receivers(step, carry):
         for half in range(halves):
@@ -164,8 +191,8 @@
                 total_f = total_f_ref[here, lanes]
                 total_s = total_s_ref[here, lanes]
                 for i in range(2):
-                    h = tx_lane_ref[here, lanes] + rx_ref[2 * step + i, here, :]
-                    focused, slope = point(taps[i], h)
+                    tau = tx_lane_ref[here, lanes] + rx_ref[2 * step + i, here, :]
+                    focused, slope = point(taps[i], tau)
                     slope_ref[2 * step + i, here, lanes] = slope
                     total_f = total_f + focused
                     total_s = total_s + slope
@@ -348,7 +375,7 @@
         return tuple(acc)
 
     acc = lax.fori_loop(0, rows // together, receivers, (start, jnp.zeros_like(start)))
-    row = jnp.sum((acc[0] + acc[1]).T, axis=0, keepdims=True)
+    row = jnp.sum((acc[0] + acc[1]).T, axis=0, keepdims=True) * LN2
     row = jnp.concatenate([row] * (PB // cells), axis=1)
     out_ref[...] = jnp.broadcast_to(row, out_ref.shape)
 
@@ -390,27 +417,22 @@
     tx_count, _, samples = traces.shape
     blocks = pixels // PB
     rows = 8
+    vmem = pl.BlockSpec(memory_space=pltpu.VMEM)
+    arrays = (s_row, rx_paths, traces, tap_start)
     return pl.pallas_call(
         prepare_kernel,
-        grid=(rx_count // rows,),
-        in_specs=[
-            whole((1, cells)),
-            pl.BlockSpec((rows, cells, pixels), lambda i: (i, 0, 0)),
-            whole((tx_count, rx_count, samples)),
-            whole((tx_count, rx_count, blocks)),
-        ],
-        out_specs=[
-            pl.BlockSpec((rows, PB, 128), lambda i: (i, 0, 0)),
-            pl.BlockSpec((rows, W, tx_count * blocks), lambda i: (i, 0, 0)),
-        ],
+        in_specs=[pl.BlockSpec(memory_space=pl.ANY)] * len(arrays),
+        out_specs=[vmem] * 2,
         out_shape=[shaped(rx_count, PB, 128), shaped(rx_count, W, tx_count * blocks)],
-        scratch_shapes=[
+        scratch_shapes=[pltpu.VMEM(array.shape, array.dtype) for array in arrays]
+        + [
             pltpu.VMEM((tx_count, rx_count, samples), F32),
             pltpu.VMEM((rows, blocks, PB), F32),
+            pltpu.SemaphoreType.DMA((len(arrays) - 1 + rx_count // rows,)),
         ],
-        compiler_params=params(12),
+        compiler_params=params(20),
         name="prepare",
-    )(in_hbm(s_row), in_hbm(rx_paths), in_hbm(traces), in_hbm(tap_start))
+    )(*(in_hbm(array) for array in arrays))
 
 
 def focus(tx_delay, rx_delay, window, rx_paths):

time: 90.5 us -> 89.7 us (level)
  Pallas kernels: 18.7 us -> 17.5 us
where the time goes in v7:
time: 89.7 us; the launch traced here: 89.4 us
  blocking collectives  51.2 us (57%)
  Pallas kernels  17.5 us (20%)
  starting transfers between devices  14.9 us (17%)
  waiting for transfers between devices  5.63 us (6%)
    all_to_all x1, blocking collectives, on_device(): share = lax.all_to_all(share, TX + RX, 0, 0, tiled=True)  18 us
    all_to_all x1, blocking collectives, on_device(): part = lax.all_to_all(part, ('zh', 'zl'), 0, 0)  13.6 us
    all_to_all x1, blocking collectives, on_device(): part = lax.all_to_all(part, ('x', 'y'), 0, 0)  12.4 us
    all_to_all x1, starting transfers between devices, on_device(): tx_delay = lax.all_to_all(delay, RX, 0, 0)  10 us
    all_to_all x1, blocking collectives, on_device(): lax.all_to_all(part.reshape(x_size, near, 2 * tx_count, PB), 'x', 0, 0)  7.22 us
    pallas_call x1, Pallas kernels, focus(): pl.pallas_call(focus_kernel, in_specs=[vmem, vmem, vmem, pl.BlockSpec(mem...  6.41 us
    pallas_call x1, Pallas kernels, prepare(): pl.pallas_call(prepare_kernel, in_specs=[pl.BlockSpec(memory_space=pl.ANY...  5.01 us
    ppermute x1, starting transfers between devices, on_device(): there = lax.ppermute(here, 'c', swap)  4.42 us
  transfers between devices with their start and end apart: 3, of which 3 were waited for; matrix products, arithmetic and copies ran while one was open for 0% of the time, Pallas kernels for 6%

profile of v7, /device:TPU:1, one launch (start us, length us, event | category | flops | bytes accessed | tf_op | source)
XLA Modules:
  0.0 89.4 jit_solution(6317589132987966051)
XLA Ops:
  0.0 1.7 %tx_delay.1 = f32[32,8,128]{2,1,0:T(8,128)} custom-call(bf16[1,32]{1,0:T(2,128)(2,1)} %bitcast.11, bf16[8,32,128]{2,1,0:T(8,128)(2,1)} %refs_5_.1), custom_call_target="tpu_custom_call" | custom-call | tf_op jit(solution)/shard_map/tx_delay/pallas_call | solution.py:401
  1.7 10.0 %all-to-all-start = ((f32[32,8,128]{2,1,0:T(8,128)}), f32[32,8,128]{2,1,0:T(8,128)S(1)}, u32[]{:S(2)}, u32[]{:S(2)}) async-start(f32[32,8,128]{2,1,0:T(8,128)} %tx_delay.1), calls=%async_computation | async-start | bytes 262144 | tf_op jit(solution)/shard_map/all_to_all | solution.py:510
  11.8 5.0 %prepare.1 = (f32[32,128,128]{2,1,0:T(8,128)S(1)}, f32[32,8,256]{2,1,0:T(8,128)S(1)}) custom-call(bf16[1,32]{1,0:T(2,128)(2,1)} %bitcast.12, bf16[32,32,4096]{2,1,0:T(8,128)(2,1)} %path_ref.1, bf16[8,32,512]{2,1,0:T(8,128)(2,1)} %trace_hbm.1, s32[8,32,32]{2,1,0:T(8,128)} %start_hbm.1), custom_call_target="tpu_custom_call" | custom-call | tf_op jit(solution)/shard_map/prepare/pallas_call | solution.py:422
  16.8 0.0 copy-start
  16.8 0.0 copy-start.1
  16.8 0.0 copy-start.2
  16.8 3.7 %all-to-all-done.tx_ref = f32[32,8,128]{2,1,0:T(8,128)S(1)} async-done(((f32[32,8,128]{2,1,0:T(8,128)}), f32[32,8,128]{2,1,0:T(8,128)S(1)}, u32[]{:S(2)}, u32[]{:S(2)}) %all-to-all-start) | async-done | bytes 131104 | tf_op jit(solution)/shard_map/all_to_all | solution.py:510
  20.5 6.4 %focus.1 = (f32[32,128,256]{2,1,0:T(8,128)S(1)}, f32[16,16,128]{2,1,0:T(8,128)S(1)}, f32[16,16,128]{2,1,0:T(8,128)S(1)}, bf16[32,32,4096]{2,1,0:T(8,128)(2,1)S(1)}) custom-call(f32[32,8,128]{2,1,0:T(8,128)S(1)} %all-to-all-done.tx_ref, f32[32,128,128]{2,1,0:T(8,128)S(1)} %get-tuple-element.13.rx_ref, f32[32,8,256]{2,1,0:T(8,128)S(1)} %get-tuple-element.14.win_ref, ...), custom_call_target="tpu_custom_call" | custom-call | tf_op jit(solution)/shard_map/focus/pallas_call | solution.py:443
  26.9 0.5 collective-permute-start
  27.4 1.0 %collective-permute-done.got_ref = f32[16,16,128]{2,1,0:T(8,128)S(1)} collective-permute-done((f32[16,16,128]{2,1,0:T(8,128)S(1)}, f32[16,16,128]{2,1,0:T(8,128)S(1)}, u32[]{:S(2)}, u32[]{:S(2)}) %collective-permute-start) | collective-permute-done | bytes 131104 | tf_op jit(solution)/shard_map/ppermute | solution.py:512
  28.4 7.2 %all_to_all.31.part_ref = f32[4,4,16,128]{3,2,1,0:T(8,128)S(1)} all-to-all(f32[4,4,16,128]{3,2,1,0:T(8,128)S(1)} %bitcast.8), channel_id=1, replica_groups=mesh['zh'=2,'y'=4,'x'=4,'zl'=4,'c'=2] {'x'}, dimensions={0} | all-to-all | bytes 262144 | tf_op jit(solution)/shard_map/all_to_all | solution.py:514
  35.6 13.6 %all_to_all.32.part_ref = f32[8,40,128]{2,1,0:T(8,128)S(1)} all-to-all(f32[8,40,128]{2,1,0:T(8,128)S(1)} %sum_x.1), channel_id=1, replica_groups=mesh['zh'=2,'y'=4,'x'=4,'zl'=4,'c'=2] {'zh','zl'}, dimensions={0} | all-to-all | bytes 327680 | tf_op jit(solution)/shard_map/all_to_all | solution.py:517
  49.3 12.4 %all_to_all.33.part_ref = f32[16,40,128]{2,1,0:T(8,128)S(1)} all-to-all(f32[16,40,128]{2,1,0:T(8,128)S(1)} %get-tuple-element.17), channel_id=1, replica_groups=mesh['zh'=2,'y'=4,'x'=4,'zl'=4,'c'=2] {'x','y'}, dimensions={0} | all-to-all | bytes 655360 | tf_op jit(solution)/shard_map/all_to_all | solution.py:525
  61.7 4.4 %collective-permute-start.1 = (f32[16,10,128]{2,1,0:T(8,128)S(1)}, f32[16,10,128]{2,1,0:T(8,128)S(1)}, u32[]{:S(2)}, u32[]{:S(2)}) collective-permute-start(f32[16,10,128]{2,1,0:T(8,128)S(1)} %sum_y.1.refs_1_), channel_id=1, source_target_pairs={{0,1},{1,0},{2,3},{3,2},{4,5},{5,4},{6,7},{7,6},{8,9},{9,8},{10,11... | collective-permute-start | bytes 245768 | tf_op jit(solution)/shard_map/ppermute | solution.py:527
  66.1 1.0 %collective-permute-done.1.refs_2_ = f32[16,10,128]{2,1,0:T(8,128)S(1)} collective-permute-done((f32[16,10,128]{2,1,0:T(8,128)S(1)}, f32[16,10,128]{2,1,0:T(8,128)S(1)}, u32[]{:S(2)}, u32[]{:S(2)}) %collective-permute-start.1) | collective-permute-done | bytes 81952 | tf_op jit(solution)/shard_map/ppermute | solution.py:527
  67.1 0.0 copy-done
  67.1 0.0 copy-done.1
  67.1 0.0 copy-done.2
  67.1 3.7 %gradient.1 = f32[256,128]{1,0:T(8,128)S(1)} custom-call(f32[16]{0:T(128)S(1)} %copy-done.2, f32[16,10,128]{2,1,0:T(8,128)S(1)} %sum_y.1.refs_1_, f32[16,10,128]{2,1,0:T(8,128)S(1)} %collective-permute-done.1.refs_2_, s32[32,128]{1,0:T(8,128)S(1)} %bitcast.10, f32[8,128]{1,0:T(8,128)S(1)} %get-tuple-element.18.refs_4_, bf16[8,32,128]{2,1,0:T(8,128)(2,1)S(1)} %copy-done, ...), custom_call_target="tpu_custom_call" | custom-call | tf_op jit(solution)/shard_map/gradient/pallas_call | solution.py:467
  70.8 18.0 %all_to_all.34 = f32[256,1,128]{2,1,0:T(1,128)S(1)} all-to-all(f32[256,1,128]{2,1,0:T(1,128)S(1)} %bitcast.7), channel_id=1, replica_groups=mesh['zh'=2,'y'=4,'x'=4,'zl'=4,'c'=2] {'zh','y','x','zl','c'}, dimensions={0} | all-to-all | bytes 262144 | tf_op jit(solution)/shard_map/all_to_all | solution.py:540
  88.8 0.6 total.1
  (4 shorter events, 0.1 us)
Async XLA Ops:
  1.7 18.8 %all-to-all-start = ((f32[32,8,128]{2,1,0:T(8,128)}), f32[32,8,128]{2,1,0:T(8,128)S(1)}, u32[]{:S(2)}, u32[]{:S(2)}) async-start(f32[32,8,128]{2,1,0:T(8,128)} %tx_delay.1), calls=%async_computation | async-start | bytes 262144 | tf_op jit(solution)/shard_map/all_to_all | solution.py:510
  16.8 50.3 %copy-start = (bf16[8,32,128]{2,1,0:T(8,128)(2,1)S(1)}, bf16[8,32,128]{2,1,0:T(8,128)(2,1)}, u32[]{:S(2)}) copy-start(bf16[8,32,128]{2,1,0:T(8,128)(2,1)} %refs_5_.1) | copy-start | bytes 196612
  16.8 50.3 %copy-start.1 = (s32[4096]{0:T(1024)S(1)}, s32[4096]{0:T(1024)}, u32[]{:S(2)}) copy-start(s32[4096]{0:T(1024)} %param.12) | copy-start | bytes 49156
  16.8 50.3 %copy-start.2 = (f32[16]{0:T(128)S(1)}, f32[16]{0:T(128)}, u32[]{:S(2)}) copy-start(f32[16]{0:T(128)} %refs_0_.1) | copy-start | bytes 196
  26.9 1.5 %collective-permute-start = (f32[16,16,128]{2,1,0:T(8,128)S(1)}, f32[16,16,128]{2,1,0:T(8,128)S(1)}, u32[]{:S(2)}, u32[]{:S(2)}) collective-permute-start(f32[16,16,128]{2,1,0:T(8,128)S(1)} %get-tuple-element.16), channel_id=1, source_target_pairs={{0,1},{1,0},{2,3},{3,2},{4,5},{5,4},{6,7},{7,6},{8,9},{9,8},{10,11... | collective-permute-start | bytes 393224 | tf_op jit(solution)/shard_map/ppermute | solution.py:512
  61.7 5.4 %collective-permute-start.1 = (f32[16,10,128]{2,1,0:T(8,128)S(1)}, f32[16,10,128]{2,1,0:T(8,128)S(1)}, u32[]{:S(2)}, u32[]{:S(2)}) collective-permute-start(f32[16,10,128]{2,1,0:T(8,128)S(1)} %sum_y.1.refs_1_), channel_id=1, source_target_pairs={{0,1},{1,0},{2,3},{3,2},{4,5},{5,4},{6,7},{7,6},{8,9},{9,8},{10,11... | collective-permute-start | bytes 245768 | tf_op jit(solution)/shard_map/ppermute | solution.py:527

commit v8 on v7

--- a/solution.py
+++ b/solution.py
@@ -267,7 +267,7 @@
     own = lax.axis_index("y")
     sides = 4
     blocks = 4
-    count = out_ref.shape[1] - 2
+    count = out_ref.shape[0] - 2
     for x in range(part_ref.shape[0] // sides):
         total = part_ref[x * sides, blocks * count :, :]
         for y in range(1, sides):
@@ -275,9 +275,10 @@
         beams = part_ref[x * sides + own, 0 : blocks * count, :]
         for block in range(blocks):
             place = x * blocks + block
-            out_ref[place, 0:count] = beams[block * count : (block + 1) * count]
-            out_ref[place, count : count + 1] = total[block : block + 1]
-            out_ref[place, count + 1 : count + 2] = total[blocks + block : blocks + block + 1]
+            out_ref[0:count, place, :] = beams[block * count : (block + 1) * count]
+        here = slice(x * blocks, (x + 1) * blocks)
+        out_ref[count, here, :] = total[0:blocks]
+        out_ref[count + 1, here, :] = total[blocks : 2 * blocks]
 
 
 def total_kernel(share_ref, out_ref):
@@ -328,7 +329,7 @@
     grad_ref,
 ):
     rows, cells, _ = path_ref.shape
-    pairs = here_ref.shape[0]
+    pairs = here_ref.shape[1]
     blocks = 2 * pairs
     count = slope_sum_ref.shape[0]
     per = 128 // blocks
@@ -337,8 +338,8 @@
     me = (lax.axis_index("x") * lax.axis_size("zl") + lax.axis_index("zl")) * 2 + core
 
     for row in range(count + 2):
-        here = here_ref[:, row, :]
-        there = there_ref[:, row, :]
+        here = here_ref[row]
+        there = there_ref[row]
         all_ref[row, pl.ds(0, pairs, stride=2), :] = jnp.where(core == 0, here, there)
         all_ref[row, pl.ds(1, pairs, stride=2), :] = jnp.where(core == 0, there, here)
     coherent = all_ref[count]
@@ -459,7 +460,7 @@
 
 def gradient(total_tx, parts, patch_cotangent, here, there, pixel_order, slope_sum, tx_paths, slope, rx_paths):
     rx_count = rx_paths.shape[0]
-    blocks = 2 * here.shape[0]
+    blocks = 2 * here.shape[1]
     tx_count = tx_paths.shape[0]
     lanes = tx_count * blocks
     together = 8
@@ -523,7 +524,7 @@
         part,
     )
     part = lax.all_to_all(part, ("x", "y"), 0, 0)
-    here = local(sum_y_kernel, "sum_y", shaped(pairs, tx_count + 2, PB), part)
+    here = local(sum_y_kernel, "sum_y", shaped(tx_count + 2, pairs, PB), part)
     there = lax.ppermute(here, "c", swap)
     share = gradient(
         tx_count * tx_size,

time: 89.7 us -> 89.5 us (level)
  no operation moved by 1% of the time
where the time goes in v8:
time: 89.5 us; the launch traced here: 89.2 us
  blocking collectives  51.2 us (57%)
  Pallas kernels  17.3 us (19%)
  starting transfers between devices  14.9 us (17%)
  waiting for transfers between devices  5.56 us (6%)
    all_to_all x1, blocking collectives, on_device(): share = lax.all_to_all(share, TX + RX, 0, 0, tiled=True)  18 us
    all_to_all x1, blocking collectives, on_device(): part = lax.all_to_all(part, ('zh', 'zl'), 0, 0)  13.6 us
    all_to_all x1, blocking collectives, on_device(): part = lax.all_to_all(part, ('x', 'y'), 0, 0)  12.4 us
    all_to_all x1, starting transfers between devices, on_device(): tx_delay = lax.all_to_all(delay, RX, 0, 0)  10 us
    all_to_all x1, blocking collectives, on_device(): lax.all_to_all(part.reshape(x_size, near, 2 * tx_count, PB), 'x', 0, 0)  7.22 us
    pallas_call x1, Pallas kernels, focus(): pl.pallas_call(focus_kernel, in_specs=[vmem, vmem, vmem, pl.BlockSpec(mem...  6.41 us
    pallas_call x1, Pallas kernels, prepare(): pl.pallas_call(prepare_kernel, in_specs=[pl.BlockSpec(memory_space=pl.ANY...  5.01 us
    ppermute x1, starting transfers between devices, on_device(): there = lax.ppermute(here, 'c', swap)  4.42 us
  transfers between devices with their start and end apart: 3, of which 3 were waited for; matrix products, arithmetic and copies ran while one was open for 0% of the time, Pallas kernels for 6%

profile of v8, /device:TPU:1, one launch (start us, length us, event | category | flops | bytes accessed | tf_op | source)
XLA Modules:
  0.0 89.2 jit_solution(6950157820971797111)
XLA Ops:
  0.0 1.7 %tx_delay.1 = f32[32,8,128]{2,1,0:T(8,128)} custom-call(bf16[1,32]{1,0:T(2,128)(2,1)} %bitcast.11, bf16[8,32,128]{2,1,0:T(8,128)(2,1)} %refs_5_.1), custom_call_target="tpu_custom_call" | custom-call | tf_op jit(solution)/shard_map/tx_delay/pallas_call | solution.py:402
  1.7 10.0 %all-to-all-start = ((f32[32,8,128]{2,1,0:T(8,128)}), f32[32,8,128]{2,1,0:T(8,128)S(1)}, u32[]{:S(2)}, u32[]{:S(2)}) async-start(f32[32,8,128]{2,1,0:T(8,128)} %tx_delay.1), calls=%async_computation | async-start | bytes 262144 | tf_op jit(solution)/shard_map/all_to_all | solution.py:511
  11.8 5.0 %prepare.1 = (f32[32,128,128]{2,1,0:T(8,128)S(1)}, f32[32,8,256]{2,1,0:T(8,128)S(1)}) custom-call(bf16[1,32]{1,0:T(2,128)(2,1)} %bitcast.12, bf16[32,32,4096]{2,1,0:T(8,128)(2,1)} %path_ref.1, bf16[8,32,512]{2,1,0:T(8,128)(2,1)} %trace_hbm.1, s32[8,32,32]{2,1,0:T(8,128)} %start_hbm.1), custom_call_target="tpu_custom_call" | custom-call | tf_op jit(solution)/shard_map/prepare/pallas_call | solution.py:423
  16.8 0.0 copy-start
  16.8 0.0 copy-start.1
  16.8 0.0 copy-start.2
  16.8 3.7 %all-to-all-done.tx_ref = f32[32,8,128]{2,1,0:T(8,128)S(1)} async-done(((f32[32,8,128]{2,1,0:T(8,128)}), f32[32,8,128]{2,1,0:T(8,128)S(1)}, u32[]{:S(2)}, u32[]{:S(2)}) %all-to-all-start) | async-done | bytes 131104 | tf_op jit(solution)/shard_map/all_to_all | solution.py:511
  20.5 6.4 %focus.1 = (f32[32,128,256]{2,1,0:T(8,128)S(1)}, f32[16,16,128]{2,1,0:T(8,128)S(1)}, f32[16,16,128]{2,1,0:T(8,128)S(1)}, bf16[32,32,4096]{2,1,0:T(8,128)(2,1)S(1)}) custom-call(f32[32,8,128]{2,1,0:T(8,128)S(1)} %all-to-all-done.tx_ref, f32[32,128,128]{2,1,0:T(8,128)S(1)} %get-tuple-element.13.rx_ref, f32[32,8,256]{2,1,0:T(8,128)S(1)} %get-tuple-element.14.win_ref, ...), custom_call_target="tpu_custom_call" | custom-call | tf_op jit(solution)/shard_map/focus/pallas_call | solution.py:444
  26.9 0.5 collective-permute-start
  27.4 1.0 %collective-permute-done.got_ref = f32[16,16,128]{2,1,0:T(8,128)S(1)} collective-permute-done((f32[16,16,128]{2,1,0:T(8,128)S(1)}, f32[16,16,128]{2,1,0:T(8,128)S(1)}, u32[]{:S(2)}, u32[]{:S(2)}) %collective-permute-start) | collective-permute-done | bytes 131104 | tf_op jit(solution)/shard_map/ppermute | solution.py:513
  28.4 7.2 %all_to_all.31.part_ref = f32[4,4,16,128]{3,2,1,0:T(8,128)S(1)} all-to-all(f32[4,4,16,128]{3,2,1,0:T(8,128)S(1)} %bitcast.8), channel_id=1, replica_groups=mesh['zh'=2,'y'=4,'x'=4,'zl'=4,'c'=2] {'x'}, dimensions={0} | all-to-all | bytes 262144 | tf_op jit(solution)/shard_map/all_to_all | solution.py:515
  35.6 13.6 %all_to_all.32.part_ref = f32[8,40,128]{2,1,0:T(8,128)S(1)} all-to-all(f32[8,40,128]{2,1,0:T(8,128)S(1)} %sum_x.1), channel_id=1, replica_groups=mesh['zh'=2,'y'=4,'x'=4,'zl'=4,'c'=2] {'zh','zl'}, dimensions={0} | all-to-all | bytes 327680 | tf_op jit(solution)/shard_map/all_to_all | solution.py:518
  49.3 12.4 %all_to_all.33.part_ref = f32[16,40,128]{2,1,0:T(8,128)S(1)} all-to-all(f32[16,40,128]{2,1,0:T(8,128)S(1)} %get-tuple-element.17), channel_id=1, replica_groups=mesh['zh'=2,'y'=4,'x'=4,'zl'=4,'c'=2] {'x','y'}, dimensions={0} | all-to-all | bytes 655360 | tf_op jit(solution)/shard_map/all_to_all | solution.py:526
  61.7 4.4 %collective-permute-start.1 = (f32[10,16,128]{2,1,0:T(8,128)S(1)}, f32[10,16,128]{2,1,0:T(8,128)S(1)}, u32[]{:S(2)}, u32[]{:S(2)}) collective-permute-start(f32[10,16,128]{2,1,0:T(8,128)S(1)} %sum_y.1.refs_1_), channel_id=1, source_target_pairs={{0,1},{1,0},{2,3},{3,2},{4,5},{5,4},{6,7},{7,6},{8,9},{9,8},{10,11... | collective-permute-start | bytes 245768 | tf_op jit(solution)/shard_map/ppermute | solution.py:528
  66.1 0.9 %collective-permute-done.1.refs_2_ = f32[10,16,128]{2,1,0:T(8,128)S(1)} collective-permute-done((f32[10,16,128]{2,1,0:T(8,128)S(1)}, f32[10,16,128]{2,1,0:T(8,128)S(1)}, u32[]{:S(2)}, u32[]{:S(2)}) %collective-permute-start.1) | collective-permute-done | bytes 81952 | tf_op jit(solution)/shard_map/ppermute | solution.py:528
  67.1 0.0 copy-done
  67.1 0.0 copy-done.1
  67.1 0.0 copy-done.2
  67.1 3.5 %gradient.1 = f32[256,128]{1,0:T(8,128)S(1)} custom-call(f32[16]{0:T(128)S(1)} %copy-done.2, f32[10,16,128]{2,1,0:T(8,128)S(1)} %sum_y.1.refs_1_, f32[10,16,128]{2,1,0:T(8,128)S(1)} %collective-permute-done.1.refs_2_, s32[32,128]{1,0:T(8,128)S(1)} %bitcast.10, f32[8,128]{1,0:T(8,128)S(1)} %get-tuple-element.18.refs_4_, bf16[8,32,128]{2,1,0:T(8,128)(2,1)S(1)} %copy-done, ...), custom_call_target="tpu_custom_call" | custom-call | tf_op jit(solution)/shard_map/gradient/pallas_call | solution.py:468
  70.6 18.0 %all_to_all.34 = f32[256,1,128]{2,1,0:T(1,128)S(1)} all-to-all(f32[256,1,128]{2,1,0:T(1,128)S(1)} %bitcast.7), channel_id=1, replica_groups=mesh['zh'=2,'y'=4,'x'=4,'zl'=4,'c'=2] {'zh','y','x','zl','c'}, dimensions={0} | all-to-all | bytes 262144 | tf_op jit(solution)/shard_map/all_to_all | solution.py:541
  88.6 0.6 total.1
  (4 shorter events, 0.1 us)
Async XLA Ops:
  1.7 18.8 %all-to-all-start = ((f32[32,8,128]{2,1,0:T(8,128)}), f32[32,8,128]{2,1,0:T(8,128)S(1)}, u32[]{:S(2)}, u32[]{:S(2)}) async-start(f32[32,8,128]{2,1,0:T(8,128)} %tx_delay.1), calls=%async_computation | async-start | bytes 262144 | tf_op jit(solution)/shard_map/all_to_all | solution.py:511
  16.8 50.3 %copy-start = (bf16[8,32,128]{2,1,0:T(8,128)(2,1)S(1)}, bf16[8,32,128]{2,1,0:T(8,128)(2,1)}, u32[]{:S(2)}) copy-start(bf16[8,32,128]{2,1,0:T(8,128)(2,1)} %refs_5_.1) | copy-start | bytes 196612
  16.8 50.3 %copy-start.1 = (s32[4096]{0:T(1024)S(1)}, s32[4096]{0:T(1024)}, u32[]{:S(2)}) copy-start(s32[4096]{0:T(1024)} %param.12) | copy-start | bytes 49156
  16.8 50.3 %copy-start.2 = (f32[16]{0:T(128)S(1)}, f32[16]{0:T(128)}, u32[]{:S(2)}) copy-start(f32[16]{0:T(128)} %refs_0_.1) | copy-start | bytes 196
  26.9 1.5 %collective-permute-start = (f32[16,16,128]{2,1,0:T(8,128)S(1)}, f32[16,16,128]{2,1,0:T(8,128)S(1)}, u32[]{:S(2)}, u32[]{:S(2)}) collective-permute-start(f32[16,16,128]{2,1,0:T(8,128)S(1)} %get-tuple-element.16), channel_id=1, source_target_pairs={{0,1},{1,0},{2,3},{3,2},{4,5},{5,4},{6,7},{7,6},{8,9},{9,8},{10,11... | collective-permute-start | bytes 393224 | tf_op jit(solution)/shard_map/ppermute | solution.py:513
  61.7 5.3 %collective-permute-start.1 = (f32[10,16,128]{2,1,0:T(8,128)S(1)}, f32[10,16,128]{2,1,0:T(8,128)S(1)}, u32[]{:S(2)}, u32[]{:S(2)}) collective-permute-start(f32[10,16,128]{2,1,0:T(8,128)S(1)} %sum_y.1.refs_1_), channel_id=1, source_target_pairs={{0,1},{1,0},{2,3},{3,2},{4,5},{5,4},{6,7},{7,6},{8,9},{9,8},{10,11... | collective-permute-start | bytes 245768 | tf_op jit(solution)/shard_map/ppermute | solution.py:528

commit v9 on v8

--- a/solution.py
+++ b/solution.py
@@ -2,6 +2,7 @@
 
 import jax
 import jax.numpy as jnp
+import numpy as np
 from jax import lax
 from jax.experimental import pallas as pl
 from jax.experimental.pallas import tpu as pltpu
@@ -16,6 +17,9 @@
 LOG2E = 1.0 / LN2
 F32 = jnp.float32
 FINE = (("zh", 2), ("y", 4), ("x", 4), ("zl", 4), ("c", 2))
+EVERY = tuple(name for name, _ in FINE)
+X_ORDER = (0, 2, 1, 3)
+Z_ORDER = (0, 4, 2, 6, 1, 5, 3, 7)
 TX = ("zh", "y")
 RX = ("x", "zl", "c")
 
@@ -215,7 +219,10 @@
 
 
 def pair_sum_kernel(keep_ref, got_ref, out_ref):
-    out_ref[...] = keep_ref[...] + got_ref[...]
+    near = out_ref.shape[0] // len(X_ORDER)
+    for place, x in enumerate(X_ORDER):
+        some = slice(x * near, (x + 1) * near)
+        out_ref[place * near : (place + 1) * near] = keep_ref[some] + got_ref[some]
 
 
 def sum_x_kernel(part_ref, out_ref):
@@ -228,8 +235,9 @@
         here = slice(block * count, (block + 1) * count)
         beam = total[0:count]
         out_ref[:, here] = jnp.broadcast_to(beam[None], (out_ref.shape[0], count, PB))
-        for far in range(out_ref.shape[0] // blocks):
-            out_ref[far * blocks + block, blocks * count :] = total[count:rows]
+        for place, z in enumerate(Z_ORDER):
+            if z % blocks == block:
+                out_ref[place, blocks * count :] = total[count:rows]
 
 
 def sum_z_kernel(part_ref, out_ref, slope_sum_ref):
@@ -239,9 +247,10 @@
     first = lax.axis_index("zh") == 0
     totals = []
     for far in range(part_ref.shape[0] // blocks):
-        total = part_ref[far * blocks]
-        for i in range(1, blocks):
-            total = total + part_ref[far * blocks + i]
+        total = None
+        for place, z in enumerate(Z_ORDER):
+            if z // blocks == far:
+                total = part_ref[place] if total is None else total + part_ref[place]
         totals.append(total)
     own = jnp.where(first, totals[0], totals[1])
     slope_sum_ref[...] = own[blocks * count :]
@@ -379,6 +388,18 @@
     row = jnp.sum((acc[0] + acc[1]).T, axis=0, keepdims=True) * LN2
     row = jnp.concatenate([row] * (PB // cells), axis=1)
     out_ref[...] = jnp.broadcast_to(row, out_ref.shape)
+
+
+def groups_along(axes, order):
+    sizes = [size for _, size in FINE]
+    ids = np.arange(math.prod(sizes)).reshape(sizes)
+    moved = [EVERY.index(axis) for axis in axes]
+    ids = np.moveaxis(ids, moved, range(-len(moved), 0)).reshape(-1, len(order))
+    return ids[:, list(order)].tolist()
+
+
+def exchange(array, axes, order):
+    return lax.all_to_all(array, EVERY, 0, 0, axis_index_groups=groups_along(axes, order))
 
 
 def params(megabytes):
@@ -512,10 +533,10 @@
     slope, keep, give, path_copy = focus(tx_delay, rx_delay, window, rx_paths)
     got = lax.ppermute(give, "c", swap)
     part = local(pair_sum_kernel, "sum_cores", shaped(*keep.shape), keep, got)
-    part = lax.all_to_all(part.reshape(x_size, near, 2 * tx_count, PB), "x", 0, 0)
+    part = exchange(part.reshape(x_size, near, 2 * tx_count, PB), ("x",), X_ORDER)
     rows = (near + 1) * tx_count
     part = local(sum_x_kernel, "sum_x", shaped(2 * near, rows, PB), part)
-    part = lax.all_to_all(part, ("zh", "zl"), 0, 0)
+    part = exchange(part, ("zh", "zl"), Z_ORDER)
     rows = near * (tx_count + 2)
     part, slope_sum = local(
         sum_z_kernel,
@@ -543,8 +564,7 @@
 
 
 def solution(mesh):
-    names = tuple(name for name, _ in FINE)
-    fine = Mesh(mesh.devices.reshape([size for _, size in FINE]), names)
+    fine = Mesh(mesh.devices.reshape([size for _, size in FINE]), EVERY)
     in_specs = (
         P(),
         P(TX, None, RX),

time: 89.5 us -> 88.6 us (0.990)
    all_to_all x2, blocking collectives: 20.8 us -> 19.1 us  [exchange(): lax.all_to_all(array, EVERY, 0, 0, axis_index_groups=groups_along(axes, o...]
where the time goes in v9:
time: 88.6 us; the launch traced here: 88.3 us
  blocking collectives  50.6 us (57%)
  Pallas kernels  17.3 us (20%)
  starting transfers between devices  14.7 us (17%)
  waiting for transfers between devices  5.56 us (6%)
    all_to_all x2, blocking collectives, exchange(): lax.all_to_all(array, EVERY, 0, 0, axis_index_groups=groups_along(axes, o...  19.1 us
    all_to_all x1, blocking collectives, on_device(): share = lax.all_to_all(share, TX + RX, 0, 0, tiled=True)  18.7 us
    all_to_all x1, blocking collectives, on_device(): part = lax.all_to_all(part, ('x', 'y'), 0, 0)  12.9 us
    all_to_all x1, starting transfers between devices, on_device(): tx_delay = lax.all_to_all(delay, RX, 0, 0)  10 us
    pallas_call x1, Pallas kernels, focus(): pl.pallas_call(focus_kernel, in_specs=[vmem, vmem, vmem, pl.BlockSpec(mem...  6.41 us
    pallas_call x1, Pallas kernels, prepare(): pl.pallas_call(prepare_kernel, in_specs=[pl.BlockSpec(memory_space=pl.ANY...  5.01 us
    ppermute x1, starting transfers between devices, on_device(): there = lax.ppermute(here, 'c', swap)  4.14 us
    all_to_all x1, waiting for transfers between devices, on_device(): tx_delay = lax.all_to_all(delay, RX, 0, 0)  3.65 us
  transfers between devices with their start and end apart: 3, of which 3 were waited for; matrix products, arithmetic and copies ran while one was open for 0% of the time, Pallas kernels for 6%

profile of v9, /device:TPU:1, one launch (start us, length us, event | category | flops | bytes accessed | tf_op | source)
XLA Modules:
  0.0 88.3 jit_solution(8252792268885505791)
XLA Ops:
  0.0 1.7 %tx_delay.1 = f32[32,8,128]{2,1,0:T(8,128)} custom-call(bf16[1,32]{1,0:T(2,128)(2,1)} %bitcast.11, bf16[8,32,128]{2,1,0:T(8,128)(2,1)} %refs_5_.1), custom_call_target="tpu_custom_call" | custom-call | tf_op jit(solution)/shard_map/tx_delay/pallas_call | solution.py:423
  1.7 10.0 %all-to-all-start = ((f32[32,8,128]{2,1,0:T(8,128)}), f32[32,8,128]{2,1,0:T(8,128)S(1)}, u32[]{:S(2)}, u32[]{:S(2)}) async-start(f32[32,8,128]{2,1,0:T(8,128)} %tx_delay.1), calls=%async_computation | async-start | bytes 262144 | tf_op jit(solution)/shard_map/all_to_all | solution.py:532
  11.8 5.0 %prepare.1 = (f32[32,128,128]{2,1,0:T(8,128)S(1)}, f32[32,8,256]{2,1,0:T(8,128)S(1)}) custom-call(bf16[1,32]{1,0:T(2,128)(2,1)} %bitcast.12, bf16[32,32,4096]{2,1,0:T(8,128)(2,1)} %path_ref.1, bf16[8,32,512]{2,1,0:T(8,128)(2,1)} %trace_hbm.1, s32[8,32,32]{2,1,0:T(8,128)} %start_hbm.1), custom_call_target="tpu_custom_call" | custom-call | tf_op jit(solution)/shard_map/prepare/pallas_call | solution.py:444
  16.8 0.0 copy-start
  16.8 0.0 copy-start.1
  16.8 0.0 copy-start.2
  16.8 3.7 %all-to-all-done.tx_ref = f32[32,8,128]{2,1,0:T(8,128)S(1)} async-done(((f32[32,8,128]{2,1,0:T(8,128)}), f32[32,8,128]{2,1,0:T(8,128)S(1)}, u32[]{:S(2)}, u32[]{:S(2)}) %all-to-all-start) | async-done | bytes 131104 | tf_op jit(solution)/shard_map/all_to_all | solution.py:532
  20.5 6.4 %focus.1 = (f32[32,128,256]{2,1,0:T(8,128)S(1)}, f32[16,16,128]{2,1,0:T(8,128)S(1)}, f32[16,16,128]{2,1,0:T(8,128)S(1)}, bf16[32,32,4096]{2,1,0:T(8,128)(2,1)S(1)}) custom-call(f32[32,8,128]{2,1,0:T(8,128)S(1)} %all-to-all-done.tx_ref, f32[32,128,128]{2,1,0:T(8,128)S(1)} %get-tuple-element.13.rx_ref, f32[32,8,256]{2,1,0:T(8,128)S(1)} %get-tuple-element.14.win_ref, ...), custom_call_target="tpu_custom_call" | custom-call | tf_op jit(solution)/shard_map/focus/pallas_call | solution.py:465
  26.9 0.5 collective-permute-start
  27.4 1.0 %collective-permute-done.got_ref = f32[16,16,128]{2,1,0:T(8,128)S(1)} collective-permute-done((f32[16,16,128]{2,1,0:T(8,128)S(1)}, f32[16,16,128]{2,1,0:T(8,128)S(1)}, u32[]{:S(2)}, u32[]{:S(2)}) %collective-permute-start) | collective-permute-done | bytes 131104 | tf_op jit(solution)/shard_map/ppermute | solution.py:534
  28.4 6.9 %all_to_all.31.part_ref = f32[4,4,16,128]{3,2,1,0:T(8,128)S(1)} all-to-all(f32[4,4,16,128]{3,2,1,0:T(8,128)S(1)} %bitcast.8), channel_id=1, replica_groups={{0,16,8,24},{1,17,9,25},{2,18,10,26},{3,19,11,27},{4,20,12,28},{5,21,13..., dimensions={0} | all-to-all | bytes 262144 | tf_op jit(solution)/shard_map/all_to_all | solution.py:402
  35.3 12.1 %all_to_all.32.part_ref = f32[8,40,128]{2,1,0:T(8,128)S(1)} all-to-all(f32[8,40,128]{2,1,0:T(8,128)S(1)} %sum_x.1), channel_id=1, replica_groups={{0,128,4,132,2,130,6,134},{1,129,5,133,3,131,7,135},{8,136,12,140,10,13..., dimensions={0} | all-to-all | bytes 327680 | tf_op jit(solution)/shard_map/all_to_all | solution.py:402
  47.5 12.9 %all_to_all.33.part_ref = f32[16,40,128]{2,1,0:T(8,128)S(1)} all-to-all(f32[16,40,128]{2,1,0:T(8,128)S(1)} %get-tuple-element.17), channel_id=1, replica_groups=mesh['zh'=2,'y'=4,'x'=4,'zl'=4,'c'=2] {'x','y'}, dimensions={0} | all-to-all | bytes 655360 | tf_op jit(solution)/shard_map/all_to_all | solution.py:547
  60.5 4.1 %collective-permute-start.1 = (f32[10,16,128]{2,1,0:T(8,128)S(1)}, f32[10,16,128]{2,1,0:T(8,128)S(1)}, u32[]{:S(2)}, u32[]{:S(2)}) collective-permute-start(f32[10,16,128]{2,1,0:T(8,128)S(1)} %sum_y.1.refs_1_), channel_id=1, source_target_pairs={{0,1},{1,0},{2,3},{3,2},{4,5},{5,4},{6,7},{7,6},{8,9},{9,8},{10,11... | collective-permute-start | bytes 245768 | tf_op jit(solution)/shard_map/ppermute | solution.py:549
  64.6 0.9 %collective-permute-done.1.refs_2_ = f32[10,16,128]{2,1,0:T(8,128)S(1)} collective-permute-done((f32[10,16,128]{2,1,0:T(8,128)S(1)}, f32[10,16,128]{2,1,0:T(8,128)S(1)}, u32[]{:S(2)}, u32[]{:S(2)}) %collective-permute-start.1) | collective-permute-done | bytes 81952 | tf_op jit(solution)/shard_map/ppermute | solution.py:549
  65.5 0.0 copy-done
  65.5 0.0 copy-done.1
  65.5 0.0 copy-done.2
  65.5 3.5 %gradient.1 = f32[256,128]{1,0:T(8,128)S(1)} custom-call(f32[16]{0:T(128)S(1)} %copy-done.2, f32[10,16,128]{2,1,0:T(8,128)S(1)} %sum_y.1.refs_1_, f32[10,16,128]{2,1,0:T(8,128)S(1)} %collective-permute-done.1.refs_2_, s32[32,128]{1,0:T(8,128)S(1)} %bitcast.10, f32[8,128]{1,0:T(8,128)S(1)} %get-tuple-element.18.refs_4_, bf16[8,32,128]{2,1,0:T(8,128)(2,1)S(1)} %copy-done, ...), custom_call_target="tpu_custom_call" | custom-call | tf_op jit(solution)/shard_map/gradient/pallas_call | solution.py:489
  69.1 18.7 %all_to_all.34 = f32[256,1,128]{2,1,0:T(1,128)S(1)} all-to-all(f32[256,1,128]{2,1,0:T(1,128)S(1)} %bitcast.7), channel_id=1, replica_groups=mesh['zh'=2,'y'=4,'x'=4,'zl'=4,'c'=2] {'zh','y','x','zl','c'}, dimensions={0} | all-to-all | bytes 262144 | tf_op jit(solution)/shard_map/all_to_all | solution.py:562
  87.7 0.6 total.1
  (4 shorter events, 0.1 us)
Async XLA Ops:
  1.7 18.8 %all-to-all-start = ((f32[32,8,128]{2,1,0:T(8,128)}), f32[32,8,128]{2,1,0:T(8,128)S(1)}, u32[]{:S(2)}, u32[]{:S(2)}) async-start(f32[32,8,128]{2,1,0:T(8,128)} %tx_delay.1), calls=%async_computation | async-start | bytes 262144 | tf_op jit(solution)/shard_map/all_to_all | solution.py:532
  16.8 48.8 %copy-start = (bf16[8,32,128]{2,1,0:T(8,128)(2,1)S(1)}, bf16[8,32,128]{2,1,0:T(8,128)(2,1)}, u32[]{:S(2)}) copy-start(bf16[8,32,128]{2,1,0:T(8,128)(2,1)} %refs_5_.1) | copy-start | bytes 196612
  16.8 48.7 %copy-start.1 = (s32[4096]{0:T(1024)S(1)}, s32[4096]{0:T(1024)}, u32[]{:S(2)}) copy-start(s32[4096]{0:T(1024)} %param.12) | copy-start | bytes 49156
  16.8 48.7 %copy-start.2 = (f32[16]{0:T(128)S(1)}, f32[16]{0:T(128)}, u32[]{:S(2)}) copy-start(f32[16]{0:T(128)} %refs_0_.1) | copy-start | bytes 196
  26.9 1.5 %collective-permute-start = (f32[16,16,128]{2,1,0:T(8,128)S(1)}, f32[16,16,128]{2,1,0:T(8,128)S(1)}, u32[]{:S(2)}, u32[]{:S(2)}) collective-permute-start(f32[16,16,128]{2,1,0:T(8,128)S(1)} %get-tuple-element.16), channel_id=1, source_target_pairs={{0,1},{1,0},{2,3},{3,2},{4,5},{5,4},{6,7},{7,6},{8,9},{9,8},{10,11... | collective-permute-start | bytes 393224 | tf_op jit(solution)/shard_map/ppermute | solution.py:534
  60.5 5.1 %collective-permute-start.1 = (f32[10,16,128]{2,1,0:T(8,128)S(1)}, f32[10,16,128]{2,1,0:T(8,128)S(1)}, u32[]{:S(2)}, u32[]{:S(2)}) collective-permute-start(f32[10,16,128]{2,1,0:T(8,128)S(1)} %sum_y.1.refs_1_), channel_id=1, source_target_pairs={{0,1},{1,0},{2,3},{3,2},{4,5},{5,4},{6,7},{7,6},{8,9},{9,8},{10,11... | collective-permute-start | bytes 245768 | tf_op jit(solution)/shard_map/ppermute | solution.py:549

commit v10 on v9

--- a/solution.py
+++ b/solution.py
@@ -19,7 +19,7 @@
 FINE = (("zh", 2), ("y", 4), ("x", 4), ("zl", 4), ("c", 2))
 EVERY = tuple(name for name, _ in FINE)
 X_ORDER = (0, 2, 1, 3)
-Z_ORDER = (0, 4, 2, 6, 1, 5, 3, 7)
+Z_ORDER = (0, 2, 5, 7, 4, 6, 1, 3)
 TX = ("zh", "y")
 RX = ("x", "zl", "c")
 

time: 88.6 us -> 89.5 us (1.010)
  blocking collectives: 50.6 us -> 51.6 us
    all_to_all x2, blocking collectives: 19.1 us -> 20.5 us  [exchange(): lax.all_to_all(array, EVERY, 0, 0, axis_index_groups=groups_along(axes, o...]
where the time goes in v10:
time: 89.5 us; the launch traced here: 89.2 us
  blocking collectives  51.6 us (58%)
  Pallas kernels  17.3 us (19%)
  starting transfers between devices  14.6 us (16%)
  waiting for transfers between devices  5.56 us (6%)
    all_to_all x2, blocking collectives, exchange(): lax.all_to_all(array, EVERY, 0, 0, axis_index_groups=groups_along(axes, o...  20.5 us
    all_to_all x1, blocking collectives, on_device(): share = lax.all_to_all(share, TX + RX, 0, 0, tiled=True)  18 us
    all_to_all x1, blocking collectives, on_device(): part = lax.all_to_all(part, ('x', 'y'), 0, 0)  13 us
    all_to_all x1, starting transfers between devices, on_device(): tx_delay = lax.all_to_all(delay, RX, 0, 0)  10 us
    pallas_call x1, Pallas kernels, focus(): pl.pallas_call(focus_kernel, in_specs=[vmem, vmem, vmem, pl.BlockSpec(mem...  6.41 us
    pallas_call x1, Pallas kernels, prepare(): pl.pallas_call(prepare_kernel, in_specs=[pl.BlockSpec(memory_space=pl.ANY...  5.01 us
    ppermute x1, starting transfers between devices, on_device(): there = lax.ppermute(here, 'c', swap)  4.09 us
    all_to_all x1, waiting for transfers between devices, on_device(): tx_delay = lax.all_to_all(delay, RX, 0, 0)  3.65 us
  transfers between devices with their start and end apart: 3, of which 3 were waited for; matrix products, arithmetic and copies ran while one was open for 0% of the time, Pallas kernels for 6%

profile of v10, /device:TPU:1, one launch (start us, length us, event | category | flops | bytes accessed | tf_op | source)
XLA Modules:
  0.0 89.2 jit_solution(14636768108463375330)
XLA Ops:
  0.0 1.7 %tx_delay.1 = f32[32,8,128]{2,1,0:T(8,128)} custom-call(bf16[1,32]{1,0:T(2,128)(2,1)} %bitcast.11, bf16[8,32,128]{2,1,0:T(8,128)(2,1)} %refs_5_.1), custom_call_target="tpu_custom_call" | custom-call | tf_op jit(solution)/shard_map/tx_delay/pallas_call | solution.py:423
  1.7 10.0 %all-to-all-start = ((f32[32,8,128]{2,1,0:T(8,128)}), f32[32,8,128]{2,1,0:T(8,128)S(1)}, u32[]{:S(2)}, u32[]{:S(2)}) async-start(f32[32,8,128]{2,1,0:T(8,128)} %tx_delay.1), calls=%async_computation | async-start | bytes 262144 | tf_op jit(solution)/shard_map/all_to_all | solution.py:532
  11.8 5.0 %prepare.1 = (f32[32,128,128]{2,1,0:T(8,128)S(1)}, f32[32,8,256]{2,1,0:T(8,128)S(1)}) custom-call(bf16[1,32]{1,0:T(2,128)(2,1)} %bitcast.12, bf16[32,32,4096]{2,1,0:T(8,128)(2,1)} %path_ref.1, bf16[8,32,512]{2,1,0:T(8,128)(2,1)} %trace_hbm.1, s32[8,32,32]{2,1,0:T(8,128)} %start_hbm.1), custom_call_target="tpu_custom_call" | custom-call | tf_op jit(solution)/shard_map/prepare/pallas_call | solution.py:444
  16.8 0.0 copy-start
  16.8 0.0 copy-start.1
  16.8 0.0 copy-start.2
  16.8 3.7 %all-to-all-done.tx_ref = f32[32,8,128]{2,1,0:T(8,128)S(1)} async-done(((f32[32,8,128]{2,1,0:T(8,128)}), f32[32,8,128]{2,1,0:T(8,128)S(1)}, u32[]{:S(2)}, u32[]{:S(2)}) %all-to-all-start) | async-done | bytes 131104 | tf_op jit(solution)/shard_map/all_to_all | solution.py:532
  20.5 6.4 %focus.1 = (f32[32,128,256]{2,1,0:T(8,128)S(1)}, f32[16,16,128]{2,1,0:T(8,128)S(1)}, f32[16,16,128]{2,1,0:T(8,128)S(1)}, bf16[32,32,4096]{2,1,0:T(8,128)(2,1)S(1)}) custom-call(f32[32,8,128]{2,1,0:T(8,128)S(1)} %all-to-all-done.tx_ref, f32[32,128,128]{2,1,0:T(8,128)S(1)} %get-tuple-element.13.rx_ref, f32[32,8,256]{2,1,0:T(8,128)S(1)} %get-tuple-element.14.win_ref, ...), custom_call_target="tpu_custom_call" | custom-call | tf_op jit(solution)/shard_map/focus/pallas_call | solution.py:465
  26.9 0.5 collective-permute-start
  27.4 1.0 %collective-permute-done.got_ref = f32[16,16,128]{2,1,0:T(8,128)S(1)} collective-permute-done((f32[16,16,128]{2,1,0:T(8,128)S(1)}, f32[16,16,128]{2,1,0:T(8,128)S(1)}, u32[]{:S(2)}, u32[]{:S(2)}) %collective-permute-start) | collective-permute-done | bytes 131104 | tf_op jit(solution)/shard_map/ppermute | solution.py:534
  28.4 6.9 %all_to_all.31.part_ref = f32[4,4,16,128]{3,2,1,0:T(8,128)S(1)} all-to-all(f32[4,4,16,128]{3,2,1,0:T(8,128)S(1)} %bitcast.8), channel_id=1, replica_groups={{0,16,8,24},{1,17,9,25},{2,18,10,26},{3,19,11,27},{4,20,12,28},{5,21,13..., dimensions={0} | all-to-all | bytes 262144 | tf_op jit(solution)/shard_map/all_to_all | solution.py:402
  35.3 13.6 %all_to_all.32.part_ref = f32[8,40,128]{2,1,0:T(8,128)S(1)} all-to-all(f32[8,40,128]{2,1,0:T(8,128)S(1)} %sum_x.1), channel_id=1, replica_groups={{0,4,130,134,128,132,2,6},{1,5,131,135,129,133,3,7},{8,12,138,142,136,1..., dimensions={0} | all-to-all | bytes 327680 | tf_op jit(solution)/shard_map/all_to_all | solution.py:402
  49.0 13.0 %all_to_all.33.part_ref = f32[16,40,128]{2,1,0:T(8,128)S(1)} all-to-all(f32[16,40,128]{2,1,0:T(8,128)S(1)} %get-tuple-element.17), channel_id=1, replica_groups=mesh['zh'=2,'y'=4,'x'=4,'zl'=4,'c'=2] {'x','y'}, dimensions={0} | all-to-all | bytes 655360 | tf_op jit(solution)/shard_map/all_to_all | solution.py:547
  62.0 4.1 %collective-permute-start.1 = (f32[10,16,128]{2,1,0:T(8,128)S(1)}, f32[10,16,128]{2,1,0:T(8,128)S(1)}, u32[]{:S(2)}, u32[]{:S(2)}) collective-permute-start(f32[10,16,128]{2,1,0:T(8,128)S(1)} %sum_y.1.refs_1_), channel_id=1, source_target_pairs={{0,1},{1,0},{2,3},{3,2},{4,5},{5,4},{6,7},{7,6},{8,9},{9,8},{10,11... | collective-permute-start | bytes 245768 | tf_op jit(solution)/shard_map/ppermute | solution.py:549
  66.1 0.9 %collective-permute-done.1.refs_2_ = f32[10,16,128]{2,1,0:T(8,128)S(1)} collective-permute-done((f32[10,16,128]{2,1,0:T(8,128)S(1)}, f32[10,16,128]{2,1,0:T(8,128)S(1)}, u32[]{:S(2)}, u32[]{:S(2)}) %collective-permute-start.1) | collective-permute-done | bytes 81952 | tf_op jit(solution)/shard_map/ppermute | solution.py:549
  67.1 0.0 copy-done
  67.1 0.0 copy-done.1
  67.1 0.0 copy-done.2
  67.1 3.5 %gradient.1 = f32[256,128]{1,0:T(8,128)S(1)} custom-call(f32[16]{0:T(128)S(1)} %copy-done.2, f32[10,16,128]{2,1,0:T(8,128)S(1)} %sum_y.1.refs_1_, f32[10,16,128]{2,1,0:T(8,128)S(1)} %collective-permute-done.1.refs_2_, s32[32,128]{1,0:T(8,128)S(1)} %bitcast.10, f32[8,128]{1,0:T(8,128)S(1)} %get-tuple-element.18.refs_4_, bf16[8,32,128]{2,1,0:T(8,128)(2,1)S(1)} %copy-done, ...), custom_call_target="tpu_custom_call" | custom-call | tf_op jit(solution)/shard_map/gradient/pallas_call | solution.py:489
  70.6 18.0 %all_to_all.34 = f32[256,1,128]{2,1,0:T(1,128)S(1)} all-to-all(f32[256,1,128]{2,1,0:T(1,128)S(1)} %bitcast.7), channel_id=1, replica_groups=mesh['zh'=2,'y'=4,'x'=4,'zl'=4,'c'=2] {'zh','y','x','zl','c'}, dimensions={0} | all-to-all | bytes 262144 | tf_op jit(solution)/shard_map/all_to_all | solution.py:562
  88.6 0.6 total.1
  (4 shorter events, 0.1 us)
Async XLA Ops:
  1.7 18.8 %all-to-all-start = ((f32[32,8,128]{2,1,0:T(8,128)}), f32[32,8,128]{2,1,0:T(8,128)S(1)}, u32[]{:S(2)}, u32[]{:S(2)}) async-start(f32[32,8,128]{2,1,0:T(8,128)} %tx_delay.1), calls=%async_computation | async-start | bytes 262144 | tf_op jit(solution)/shard_map/all_to_all | solution.py:532
  16.8 50.3 %copy-start = (bf16[8,32,128]{2,1,0:T(8,128)(2,1)S(1)}, bf16[8,32,128]{2,1,0:T(8,128)(2,1)}, u32[]{:S(2)}) copy-start(bf16[8,32,128]{2,1,0:T(8,128)(2,1)} %refs_5_.1) | copy-start | bytes 196612
  16.8 50.3 %copy-start.1 = (s32[4096]{0:T(1024)S(1)}, s32[4096]{0:T(1024)}, u32[]{:S(2)}) copy-start(s32[4096]{0:T(1024)} %param.12) | copy-start | bytes 49156
  16.8 50.3 %copy-start.2 = (f32[16]{0:T(128)S(1)}, f32[16]{0:T(128)}, u32[]{:S(2)}) copy-start(f32[16]{0:T(128)} %refs_0_.1) | copy-start | bytes 196
  26.9 1.5 %collective-permute-start = (f32[16,16,128]{2,1,0:T(8,128)S(1)}, f32[16,16,128]{2,1,0:T(8,128)S(1)}, u32[]{:S(2)}, u32[]{:S(2)}) collective-permute-start(f32[16,16,128]{2,1,0:T(8,128)S(1)} %get-tuple-element.16), channel_id=1, source_target_pairs={{0,1},{1,0},{2,3},{3,2},{4,5},{5,4},{6,7},{7,6},{8,9},{9,8},{10,11... | collective-permute-start | bytes 393224 | tf_op jit(solution)/shard_map/ppermute | solution.py:534
  62.0 5.0 %collective-permute-start.1 = (f32[10,16,128]{2,1,0:T(8,128)S(1)}, f32[10,16,128]{2,1,0:T(8,128)S(1)}, u32[]{:S(2)}, u32[]{:S(2)}) collective-permute-start(f32[10,16,128]{2,1,0:T(8,128)S(1)} %sum_y.1.refs_1_), channel_id=1, source_target_pairs={{0,1},{1,0},{2,3},{3,2},{4,5},{5,4},{6,7},{7,6},{8,9},{9,8},{10,11... | collective-permute-start | bytes 245768 | tf_op jit(solution)/shard_map/ppermute | solution.py:549
